TPU v7x, 32 devices: a whole 2x2x4 slice. The times are simulated.
32 devices in a mesh: dp: 16 (over z, y, x), chan: 2 (over core).
Axes of the slice: x: 2, y: 2, z: 4, core: 2. Of those that a mesh axis runs over, the one named last changes fastest.
Arguments:
- hidden_in: bfloat16 [6144, 384], P('dp'), may hold values from -6 to 6
- out_cot: bfloat16 [6144, 384], P('dp', 'chan'), may hold values from -6 to 6
- segment_ids: int32 [6144], P('dp'), may hold values from 0 to 2, as said below
- norm_gain: float32 [384], replicated
- in_weight: float32 [384, 2, 768], P(None, None, 'chan')
- out_weight: float32 [768, 384], P('chan'), may hold values from -0.21875 to 0.21875
- xproj_weight: float32 [2, 768, 56], P(None, 'chan'), may hold values from -0.21875 to 0.21875
- dtproj_weight: float32 [2, 24, 768], P(None, None, 'chan'), may hold values from -1.25 to 1.25
- conv_weight: float32 [2, 4, 768], P(None, None, 'chan'), may hold values from -3 to 3
- chan_params: float32 [2, 19, 768], P(None, None, 'chan')
- first_norm_gain: float32 [384], P('chan'), may hold values from -448 to 448
- first_in_weight: float32 [384, 2, 768], P(None, None, 'chan'), may hold values from -224 to 224
- first_out_weight: float32 [768, 384], P('chan'), may hold values from -320 to 320
- first_xproj_weight: float32 [2, 768, 56], P(None, 'chan'), may hold values from -448 to 448
- first_dtproj_weight: float32 [2, 24, 768], P(None, None, 'chan'), may hold values from -24 to 24
- first_conv_weight: float32 [2, 4, 768], P(None, None, 'chan'), may hold values from -128 to 128
- first_chan_params: float32 [2, 19, 768], P(None, None, 'chan'), may hold values from -128 to 128
- second_norm_gain: float32 [384], P('chan'), may hold values from 6144 to 24576
- second_in_weight: float32 [384, 2, 768], P(None, None, 'chan'), may hold values from 1536 to 6144
- second_out_weight: float32 [768, 384], P('chan'), may hold values from 3010.56 to 12042.24
- second_xproj_weight: float32 [2, 768, 56], P(None, 'chan'), may hold values from 6144 to 24576
- second_dtproj_weight: float32 [2, 24, 768], P(None, None, 'chan'), may hold values from 15.36 to 61.44
- second_conv_weight: float32 [2, 4, 768], P(None, None, 'chan'), may hold values from 552.96 to 2211.84
- second_chan_params: float32 [2, 19, 768], P(None, None, 'chan'), may hold values from 552.96 to 2211.84
Outputs:
- output: bfloat16 [6144, 384], P('dp', 'chan')
- input_grad: float32 [6144, 384], P('dp', 'chan')
- new_first_norm_gain: float32 [384], P('chan')
- new_second_norm_gain: float32 [384], P('chan')
- new_norm_gain: float32 [384], P('chan')
- copy_norm_gain: bfloat16 [384], P('chan')
- new_first_in_weight: float32 [384, 2, 768], P(None, None, 'chan')
- new_second_in_weight: float32 [384, 2, 768], P(None, None, 'chan')
- new_in_weight: float32 [384, 2, 768], P(None, None, 'chan')
- copy_in_weight: bfloat16 [384, 2, 768], P(None, None, 'chan')
- new_first_out_weight: float32 [768, 384], P('chan')
- new_second_out_weight: float32 [768, 384], P('chan')
- new_out_weight: float32 [768, 384], P('chan')
- copy_out_weight: bfloat16 [768, 384], P('chan')
- new_first_xproj_weight: float32 [2, 768, 56], P(None, 'chan')
- new_second_xproj_weight: float32 [2, 768, 56], P(None, 'chan')
- new_xproj_weight: float32 [2, 768, 56], P(None, 'chan')
- copy_xproj_weight: bfloat16 [2, 768, 56], P(None, 'chan')
- new_first_dtproj_weight: float32 [2, 24, 768], P(None, None, 'chan')
- new_second_dtproj_weight: float32 [2, 24, 768], P(None, None, 'chan')
- new_dtproj_weight: float32 [2, 24, 768], P(None, None, 'chan')
- copy_dtproj_weight: bfloat16 [2, 24, 768], P(None, None, 'chan')
- new_first_conv_weight: float32 [2, 4, 768], P(None, None, 'chan')
- new_second_conv_weight: float32 [2, 4, 768], P(None, None, 'chan')
- new_conv_weight: float32 [2, 4, 768], P(None, None, 'chan')
- copy_conv_weight: bfloat16 [2, 4, 768], P(None, None, 'chan')
- new_first_chan_params: float32 [2, 19, 768], P(None, None, 'chan')
- new_second_chan_params: float32 [2, 19, 768], P(None, None, 'chan')
- new_chan_params: float32 [2, 19, 768], P(None, None, 'chan')
- copy_chan_params: bfloat16 [2, 19, 768], P(None, None, 'chan')
- tensor_norms: float32 [7, 2], replicated
- step_stats: float32 [2, 768], P(None, 'chan')
Inputs may be any that keep to these rules, and one draw needn't show every extreme that they name: `segment_ids`: each block of 384 tokens is a window over clips of 1, 2, 4 or 8 frames of 196 tokens laid end to end; its first and last pieces may be parts of longer clips. Within a block the ids start at 0 and rise by one at each new clip, every piece but the first and last holds a whole clip, and some block holds 3 pieces.
All inputs are finite; a program needn't handle non-finite values.
Results may differ from a plain program's by a relative error of at most 0.012.
The roundings to bfloat16 on the way count: a program that leaves them out, or rounds other values in their place, can miss the bound.
Values may be sent and summed in bfloat16 or wider, within the bound.
No kernel may reach another device: no remote copies, remote signals or barrier semaphores. Data moves between devices by JAX's collectives and lax.ppermute only.
A program may use at most 384 MiB of HBM per device.

v0:
```python
import jax
import jax.numpy as jnp
from jax import lax
from jax.sharding import PartitionSpec as P

STEP = 4


precise = lax.Precision.HIGHEST
norm_eps = 1e-06
beta_one = 0.5
beta_two = 0.5
adam_eps = 1e-06
decay_rate = 0.01
learn_rate = 0.3


def shift_rows(values, offset):
    length = values.shape[0]
    extent = abs(offset)
    padding = jnp.zeros((extent,) + values.shape[1:], values.dtype)
    if offset > 0:
        return jnp.concatenate([padding, values[: length - extent]], 0)
    return jnp.concatenate([values[extent:], padding], 0)


def linear_scan(decays, inflow, backward):
    length = decays.shape[0]
    block_len = 16
    block_len = min(block_len, length)
    block_total = length // block_len
    inner = decays.shape[1:]
    decay_blocks = decays.reshape((block_total, block_len) + inner)
    inflow_blocks = inflow.reshape((block_total, block_len) + inner)
    running = jnp.zeros((block_total,) + inner, jnp.float32)
    product = jnp.ones((block_total,) + inner, jnp.float32)
    run_list = []
    prod_list = []
    positions = list(range(block_len))
    if backward:
        positions = positions[::-1]
    for place in positions:
        factor = decay_blocks[:, place]
        running = factor * running + inflow_blocks[:, place]
        product = factor * product
        run_list.append(running)
        prod_list.append(product)
    if backward:
        run_list = run_list[::-1]
        prod_list = prod_list[::-1]
    local_runs = jnp.stack(run_list, 1)
    local_prods = jnp.stack(prod_list, 1)

    def carry_step(carried, item):
        end_run, end_prod = item
        return (end_prod * carried + end_run, carried)

    ignored, incoming = lax.scan(
        carry_step,
        jnp.zeros((block_total,) + inner, jnp.float32)[0],
        (running, product),
        reverse=backward,
    )
    result = local_runs + local_prods * incoming[:, None]
    return result.reshape((length,) + inner)


def contract_rows(left, right):
    return lax.dot_general(
        left, right, (((0,), (0,)), ((), ())), preferred_element_type=jnp.float32
    )


def contract_cols(left, right):
    return lax.dot_general(
        left, right, (((1,), (1,)), ((), ())), preferred_element_type=jnp.float32
    )


def silu_slope(values):
    sigma = jax.nn.sigmoid(values)
    return sigma * (1.0 + values * (1.0 - sigma))


def lamb_moments(weight, grad, first, second):
    first_new = beta_one * first + (1.0 - beta_one) * grad
    second_new = beta_two * second + (1.0 - beta_two) * grad * grad
    update = (
        first_new
        / (1.0 - beta_one**STEP)
        / (jnp.sqrt(second_new / (1.0 - beta_two**STEP)) + adam_eps)
        + decay_rate * weight
    )
    return (first_new, second_new, update)


def shards(
    hidden_in,
    out_cot,
    segment_ids,
    norm_gain,
    in_weight,
    out_weight,
    xproj_weight,
    dtproj_weight,
    conv_weight,
    chan_params,
    first_norm_gain,
    first_in_weight,
    first_out_weight,
    first_xproj_weight,
    first_dtproj_weight,
    first_conv_weight,
    first_chan_params,
    second_norm_gain,
    second_in_weight,
    second_out_weight,
    second_xproj_weight,
    second_dtproj_weight,
    second_conv_weight,
    second_chan_params,
):
    channels = in_weight.shape[2]
    model_width = hidden_in.shape[1]
    half_width = first_norm_gain.shape[0]
    dt_rank = dtproj_weight.shape[1]
    states = chan_params.shape[1] - 3
    kernel_width = conv_weight.shape[1]
    own_start = lax.axis_index("chan") * half_width
    gain_own = lax.dynamic_slice_in_dim(norm_gain, own_start, half_width)
    weights = (
        gain_own,
        in_weight,
        out_weight,
        xproj_weight,
        dtproj_weight,
        conv_weight,
        chan_params,
    )
    weight_sq = jnp.stack([jnp.sum(tensor * tensor) for tensor in weights])
    source = hidden_in.astype(jnp.float32)
    scale_inv = lax.rsqrt(jnp.mean(source * source, axis=1, keepdims=True) + norm_eps)
    normed_low = (source * scale_inv * norm_gain).astype(jnp.bfloat16)
    in_low = in_weight.astype(jnp.bfloat16).reshape(model_width, 2 * channels)
    mixed = jnp.dot(normed_low, in_low, preferred_element_type=jnp.float32)
    mixing = mixed[:, :channels]
    gate_value = mixed[:, channels:]
    headings = (1, -1)
    segment_masks = []
    for branch_number in range(2):
        mask_list = [None]
        for offset in range(1, kernel_width):
            matched = (segment_ids[offset:] == segment_ids[:-offset]).astype(jnp.float32)
            padding = jnp.zeros((offset,), jnp.float32)
            if branch_number == 0:
                mask_list.append(jnp.concatenate([padding, matched]))
            else:
                mask_list.append(jnp.concatenate([matched, padding]))
        segment_masks.append(mask_list)
    conv_outs = []
    activations = []
    act_lows = []
    partials = []
    for branch_number in range(2):
        heading = headings[branch_number]
        kernel_taps = conv_weight[branch_number]
        branch_params = chan_params[branch_number]
        conv_out = branch_params[0] + kernel_taps[0] * mixing
        for offset in range(1, kernel_width):
            conv_out = (
                conv_out
                + kernel_taps[offset]
                * shift_rows(mixing, heading * offset)
                * segment_masks[branch_number][offset][:, None]
            )
        activation = jax.nn.silu(conv_out)
        act_low = activation.astype(jnp.bfloat16)
        conv_outs.append(conv_out)
        activations.append(activation)
        act_lows.append(act_low)
        partials.append(
            jnp.dot(
                act_low,
                xproj_weight[branch_number].astype(jnp.bfloat16),
                preferred_element_type=jnp.float32,
            )
        )
    projections = lax.psum((partials[0], partials[1]), "chan")
    kept = []
    outputs_y = []
    for branch_number in range(2):
        heading = headings[branch_number]
        branch_params = chan_params[branch_number]
        projection = projections[branch_number]
        dt_low = projection[:, :dt_rank]
        input_map = projection[:, dt_rank : dt_rank + states]
        output_map = projection[:, dt_rank + states :]
        dt_pre = (
            jnp.dot(
                dt_low,
                dtproj_weight[branch_number],
                precision=precise,
                preferred_element_type=jnp.float32,
            )
            + branch_params[1]
        )
        step_size = jax.nn.softplus(dt_pre)
        decay_rates = -jnp.exp(branch_params[3:])
        decays = (
            jnp.exp(step_size[:, None, :] * decay_rates[None])
            * segment_masks[branch_number][1][:, None, None]
        )
        inflow = input_map[:, :, None] * (step_size * activations[branch_number])[:, None, :]
        hidden_states = linear_scan(decays, inflow, heading < 0)
        output_y = (
            jnp.einsum("tne,tn->te", hidden_states, output_map, precision=precise)
            + branch_params[2] * activations[branch_number]
        )
        outputs_y.append(output_y)
        kept.append(
            (dt_low, input_map, output_map, dt_pre, step_size, decay_rates, inflow, hidden_states)
        )
    combined = outputs_y[0] + outputs_y[1]
    gate_act = jax.nn.silu(gate_value)
    branch_low = (combined * gate_act).astype(jnp.bfloat16)
    out_low = out_weight.astype(jnp.bfloat16)
    projected = lax.psum_scatter(
        jnp.dot(branch_low, out_low, preferred_element_type=jnp.float32),
        "chan",
        scatter_dimension=1,
        tiled=True,
    )
    source_own = lax.dynamic_slice_in_dim(source, own_start, half_width, 1)
    output = (source_own + projected).astype(jnp.bfloat16)
    cot_full = lax.all_gather(out_cot, "chan", axis=1, tiled=True)
    grad_out_w = contract_rows(branch_low, cot_full)
    grad_branch = contract_cols(cot_full, out_low)
    grad_gate = grad_branch * combined * silu_slope(gate_value)
    grad_y = grad_branch * gate_act
    grad_parts = []
    scan_grads = []
    for branch_number in range(2):
        heading = headings[branch_number]
        branch_params = chan_params[branch_number]
        dt_low, input_map, output_map, dt_pre, step_size, decay_rates, inflow, hidden_states = kept[
            branch_number
        ]
        activation = activations[branch_number]
        grad_source = output_map[:, :, None] * grad_y[:, None, :]
        size_next = shift_rows(step_size, -heading)
        mask_next = shift_rows(segment_masks[branch_number][1], -heading)
        decays_next = jnp.exp(size_next[:, None, :] * decay_rates[None]) * mask_next[:, None, None]
        grad_hidden = linear_scan(decays_next, grad_source, heading > 0)
        grad_alpha = grad_hidden * (hidden_states - inflow)
        through = jnp.einsum("tne,tn->te", grad_hidden, input_map, precision=precise)
        grad_step = jnp.sum(grad_alpha * decay_rates[None], axis=1) + through * activation
        grad_act_scan = through * step_size + grad_y * branch_params[2]
        grad_input_map = jnp.einsum(
            "tne,te->tn", grad_hidden, step_size * activation, precision=precise
        )
        grad_output_map = jnp.einsum("tne,te->tn", hidden_states, grad_y, precision=precise)
        grad_skip = jnp.sum(grad_y * activation, 0)
        grad_alog = decay_rates * jnp.sum(grad_alpha * step_size[:, None, :], 0)
        grad_pre = grad_step * jax.nn.sigmoid(dt_pre)
        grad_stepbias = jnp.sum(grad_pre, 0)
        grad_dtproj = lax.dot_general(
            dt_low,
            grad_pre,
            (((0,), (0,)), ((), ())),
            precision=precise,
            preferred_element_type=jnp.float32,
        )
        grad_dt_low = lax.dot_general(
            grad_pre,
            dtproj_weight[branch_number],
            (((1,), (1,)), ((), ())),
            precision=precise,
            preferred_element_type=jnp.float32,
        )
        grad_parts.append(jnp.concatenate([grad_dt_low, grad_input_map, grad_output_map], 1))
        scan_grads.append((grad_act_scan, grad_skip, grad_alog, grad_stepbias, grad_dtproj))
    summed_parts = lax.psum((grad_parts[0], grad_parts[1]), "chan")
    grad_mixing = jnp.zeros_like(mixing)
    xproj_grads = []
    dtproj_grads = []
    conv_grads = []
    chan_grads = []
    for branch_number in range(2):
        heading = headings[branch_number]
        kernel_taps = conv_weight[branch_number]
        grad_act_scan, grad_skip, grad_alog, grad_stepbias, grad_dtproj = scan_grads[branch_number]
        parts_low = summed_parts[branch_number].astype(jnp.bfloat16)
        grad_activation = grad_act_scan + contract_cols(
            parts_low, xproj_weight[branch_number].astype(jnp.bfloat16)
        )
        xproj_grads.append(contract_rows(act_lows[branch_number], parts_low))
        grad_conv = grad_activation * silu_slope(conv_outs[branch_number])
        grad_convbias = jnp.sum(grad_conv, 0)
        tap_grads = [jnp.sum(grad_conv * mixing, 0)]
        grad_mixing = grad_mixing + grad_conv * kernel_taps[0]
        for offset in range(1, kernel_width):
            masked = grad_conv * segment_masks[branch_number][offset][:, None]
            tap_grads.append(jnp.sum(masked * shift_rows(mixing, heading * offset), 0))
            grad_mixing = grad_mixing + shift_rows(masked, -heading * offset) * kernel_taps[offset]
        conv_grads.append(jnp.stack(tap_grads))
        dtproj_grads.append(grad_dtproj)
        chan_grads.append(
            jnp.concatenate(
                [grad_convbias[None], grad_stepbias[None], grad_skip[None], grad_alog], 0
            )
        )
    grad_xproj_all = jnp.stack(xproj_grads)
    grad_dtproj_all = jnp.stack(dtproj_grads)
    grad_conv_all = jnp.stack(conv_grads)
    grad_chan_all = jnp.stack(chan_grads)
    grad_mixed_low = jnp.concatenate([grad_mixing, grad_gate], 1).astype(jnp.bfloat16)
    grad_in_w = contract_rows(normed_low, grad_mixed_low).reshape(model_width, 2, channels)
    partial_normed = contract_cols(grad_mixed_low, in_low)
    cot_own = out_cot.astype(jnp.float32)
    full_normed = lax.psum(partial_normed, "chan")
    row_dot = jnp.sum(full_normed * norm_gain * source, axis=1, keepdims=True) / model_width
    grad_normed_own = lax.dynamic_slice_in_dim(full_normed, own_start, half_width, 1)
    weighted_own = grad_normed_own * gain_own
    input_grad = (
        cot_own
        + scale_inv * weighted_own
        - source_own * scale_inv * scale_inv * scale_inv * row_dot
    )
    grad_gain = jnp.sum(grad_normed_own * source_own * scale_inv, 0)
    (
        grad_gain,
        grad_in_w,
        grad_out_w,
        grad_xproj_all,
        grad_dtproj_all,
        grad_conv_all,
        grad_chan_all,
    ) = lax.psum(
        (
            grad_gain,
            grad_in_w,
            grad_out_w,
            grad_xproj_all,
            grad_dtproj_all,
            grad_conv_all,
            grad_chan_all,
        ),
        "dp",
    )
    grads = (
        grad_gain,
        grad_in_w,
        grad_out_w,
        grad_xproj_all,
        grad_dtproj_all,
        grad_conv_all,
        grad_chan_all,
    )
    firsts = (
        first_norm_gain,
        first_in_weight,
        first_out_weight,
        first_xproj_weight,
        first_dtproj_weight,
        first_conv_weight,
        first_chan_params,
    )
    seconds = (
        second_norm_gain,
        second_in_weight,
        second_out_weight,
        second_xproj_weight,
        second_dtproj_weight,
        second_conv_weight,
        second_chan_params,
    )
    moments = [
        lamb_moments(weights[place], grads[place], firsts[place], seconds[place])
        for place in range(7)
    ]
    update_sq = jnp.stack([jnp.sum(entry[2] * entry[2]) for entry in moments])
    weight_totals, update_totals = lax.psum((weight_sq, update_sq), "chan")
    weight_norm = jnp.sqrt(weight_totals)
    update_norm = jnp.sqrt(update_totals)
    trust = weight_norm / (update_norm + adam_eps)
    flat = []
    moves = []
    for place in range(7):
        first_new, second_new, update = moments[place]
        moving = learn_rate * trust[place] * update
        new_weight = weights[place] - moving
        moves.append(moving)
        flat.extend([first_new, second_new, new_weight, new_weight.astype(jnp.bfloat16)])
    tensor_norms = jnp.stack([weight_norm, update_norm], 1)
    step_in = moves[1]
    step_out = moves[2]
    count = 3.0 * model_width
    step_mean = (jnp.sum(step_in, axis=(0, 1)) + jnp.sum(step_out, axis=1)) / count
    dev_in = step_in - step_mean
    dev_out = step_out - step_mean[:, None]
    step_var = (jnp.sum(dev_in * dev_in, axis=(0, 1)) + jnp.sum(dev_out * dev_out, axis=1)) / count
    step_stats = jnp.stack([step_mean, step_var])
    return (
        output,
        input_grad,
        flat[0],
        flat[1],
        flat[2],
        flat[3],
        flat[4],
        flat[5],
        flat[6],
        flat[7],
        flat[8],
        flat[9],
        flat[10],
        flat[11],
        flat[12],
        flat[13],
        flat[14],
        flat[15],
        flat[16],
        flat[17],
        flat[18],
        flat[19],
        flat[20],
        flat[21],
        flat[22],
        flat[23],
        flat[24],
        flat[25],
        flat[26],
        flat[27],
        tensor_norms,
        step_stats,
    )


def solution(mesh):
    placed = (
        P("dp", None),
        P("dp", "chan"),
        P("dp"),
        P(),
        P(None, None, "chan"),
        P("chan", None),
        P(None, "chan", None),
        P(None, None, "chan"),
        P(None, None, "chan"),
        P(None, None, "chan"),
        P("chan"),
        P(None, None, "chan"),
        P("chan", None),
        P(None, "chan", None),
        P(None, None, "chan"),
        P(None, None, "chan"),
        P(None, None, "chan"),
        P("chan"),
        P(None, None, "chan"),
        P("chan", None),
        P(None, "chan", None),
        P(None, None, "chan"),
        P(None, None, "chan"),
        P(None, None, "chan"),
    )
    return jax.shard_map(
        shards,
        mesh=mesh,
        in_specs=placed,
        out_specs=(
            P("dp", "chan"),
            P("dp", "chan"),
            P("chan"),
            P("chan"),
            P("chan"),
            P("chan"),
            P(None, None, "chan"),
            P(None, None, "chan"),
            P(None, None, "chan"),
            P(None, None, "chan"),
            P("chan", None),
            P("chan", None),
            P("chan", None),
            P("chan", None),
            P(None, "chan", None),
            P(None, "chan", None),
            P(None, "chan", None),
            P(None, "chan", None),
            P(None, None, "chan"),
            P(None, None, "chan"),
            P(None, None, "chan"),
            P(None, None, "chan"),
            P(None, None, "chan"),
            P(None, None, "chan"),
            P(None, None, "chan"),
            P(None, None, "chan"),
            P(None, None, "chan"),
            P(None, None, "chan"),
            P(None, None, "chan"),
            P(None, None, "chan"),
            P(),
            P(None, "chan"),
        ),
        check_vma=False,
    )
```

profile of v0, /device:TPU:0, one launch (start us, length us, event | category | flops | bytes accessed | tf_op | source)
XLA Modules:
  0.0 881.7 jit_solution(15596670893077118859)
XLA Ops:
  9.0 3.5 multiply_reduce_fusion.5
  29.2 16.1 %all-reduce.35.cloned.1.call-done = (f32[384,56]{0,1:T(8,128)}, f32[384,56]{0,1:T(8,128)}) async-done(((f32[384,56]{0,1:T(8,128)}, f32[384,56]{0,1:T(8,128)}), (f32[384,56]{0,1:T(8,128)}, f32[384,56]{0,1:T(8,128)})) %all-reduce.35.cloned.1.call-update) | async-done | bytes 172048 | tf_op jit(solution)/shard_map/psum | solution.py:188
  46.6 2.9 fusion.219
  62.4 7.8 exponential_multiply_fusion.2
  75.5 5.1 broadcast_multiply_fusion.1
  80.6 3.6 slice-done.14
  84.2 2.9 add_dynamic-update-slice_fusion.1
  87.1 2.4 bitcast_add_fusion.22
  91.7 2.4 slice_dynamic-update-slice_fusion
  94.1 7.9 bitcast_add_fusion.5
  107.4 9.3 %add_dynamic-update-slice_fusion.2 = (f32[24,16,16,384]{3,2,0,1:T(8,128)}, f32[24,1,16,384]{3,2,0,1:T(8,128)}, f32[24,1,16,384]{3,2,0,1:T(8,128)}, f32[24,1,16,3...) fusion(f32[24,16,16,384]{3,2,0,1:T(8,128)S(1)} %broadcast_multi, ...), kind=kLoop, calls=%fused_computation.368 | loop fusion | flops 4718591 | bytes 23592960
  125.2 2.6 constant_dynamic-update-slice_fusion.11
  130.0 2.6 constant_dynamic-update-slice_fusion.9
  134.7 2.6 constant_dynamic-update-slice_fusion.7
  139.5 2.7 constant_dynamic-update-slice_fusion.5
  144.4 2.6 constant_dynamic-update-slice_fusion.3
  149.2 2.7 constant_dynamic-update-slice_fusion.1
  154.1 2.3 fusion.158
  158.0 3.5 copy-done.9
  162.4 33.0 %while.60 = (s32[]{:T(128)}, f32[16,384]{1,0:T(8,128)S(1)}, f32[24,16,384]{2,1,0:T(8,128)}, f32[24,16,384]{2,1,0:T(8,128)}, f32[24,16,384]{2,1,0:T(8,128)}, /*index=5*/s32[]{:T(128)}, s32[]{:T(128)}) while((s32[]{:T(128)}, f32[16,384]{1,0:T(8,128)S(1)}, f32[24,16,384]{2,1,0:T(8,128)}, f32[24,16,384]{2,1,0:T(8,128)}, ...), condition=%wide.region_3.0_spmd.clone, body=%wide.region_2.0_spmd.clone.sunk | while | flops 24579 | bytes 147560 | solution.py:58
  198.4 3.1 constant_dynamic-update-slice_fusion.84
  205.5 2.7 constant_dynamic-update-slice_fusion.82
  228.3 18.8 %while.62 = (s32[]{:T(128)}, f32[16,384]{1,0:T(8,128)S(1)}, f32[24,16,384]{2,1,0:T(8,128)S(1)}, f32[24,16,384]{2,1,0:T(8,128)}, f32[24,16,384]{2,1,0:T(8,128)}, /*index=5*/s32[]{:T(128)}, s32[]{:T(128)}, s32[]{:T(128)}) while((s32[]{:T(128)}, f32[16,384]{1,0:T(8,128)S(1)}, f32[24,16,384]{2,1,0:T(8,128)S(1)}, ...), condition=%wide.region_9.10_spmd.clone, body=%wide.region_8.9_spmd.clone.sunk | while | flops 24580 | bytes 147580 | solution.py:58
  247.9 2.3 slice_dynamic-update-slice_fusion.1
  250.3 24.6 %multiply_reduce_fusion.1 = (f32[16,384]{1,0:T(8,128)}, f32[24,16,16,384]{3,2,1,0:T(8,128)}, f32[24,16,16,384]{3,2,1,0:T(8,128)}, f32[24,16,16,384]{3,2,1,0:T(8,128)}) fusion(f32[24,16,384]{2,1,0:T(8,128)S(1)} %bitcast.1176, f32[24,16,16,384]{3,2,0,1:T(8,128)} %get-tuple-element.659, f32[24,16,16,384]{3,2,0,1:T(8,128)} %copy-done.9, ...), kind=kLoop, calls=%fused_computation.18 | loop fusion | flops 21227520 | bytes 68468736 | tf_op jit(solution)/shard_map/reduce_sum | solution.py:263
  274.9 5.7 fusion
  282.4 33.0 %while.63 = (s32[]{:T(128)}, f32[16,384]{1,0:T(8,128)S(1)}, f32[24,16,384]{2,1,0:T(8,128)}, f32[24,16,384]{2,1,0:T(8,128)}, f32[24,16,384]{2,1,0:T(8,128)}, /*index=5*/s32[]{:T(128)}, s32[]{:T(128)}) while((s32[]{:T(128)}, f32[16,384]{1,0:T(8,128)S(1)}, f32[24,16,384]{2,1,0:T(8,128)}, f32[24,16,384]{2,1,0:T(8,128)}, ...), condition=%wide.region_13.14_spmd.clone, body=%wide.region_12.13_spmd.clone.sunk | while | flops 24579 | bytes 147560 | solution.py:58
  318.4 3.1 constant_dynamic-update-slice_fusion.55
  325.6 2.9 constant_dynamic-update-slice_fusion.53
  331.3 2.6 constant_dynamic-update-slice_fusion.51
  335.7 2.3 constant_dynamic-update-slice_fusion.49
  347.1 2.4 constant_dynamic-update-slice_fusion.44
  350.4 18.7 %while.61 = (s32[]{:T(128)}, f32[16,384]{1,0:T(8,128)S(1)}, f32[24,16,384]{2,1,0:T(8,128)S(1)}, f32[24,16,384]{2,1,0:T(8,128)}, f32[24,16,384]{2,1,0:T(8,128)}, /*index=5*/s32[]{:T(128)}, s32[]{:T(128)}, s32[]{:T(128)}) while((s32[]{:T(128)}, f32[16,384]{1,0:T(8,128)S(1)}, f32[24,16,384]{2,1,0:T(8,128)S(1)}, ...), condition=%wide.region_6.0_spmd.clone, body=%wide.region_5.0_spmd.clone.sunk | while | flops 24580 | bytes 147580 | solution.py:58
  369.1 3.0 constant_dynamic-update-slice_fusion.100
  372.1 2.9 constant_dynamic-update-slice_fusion.114
  375.0 3.5 constant_dynamic-update-slice_fusion.113
  378.6 2.9 constant_dynamic-update-slice_fusion.112
  381.5 2.7 constant_dynamic-update-slice_fusion.111
  398.1 2.4 slice_dynamic-update-slice_fusion.2
  400.5 19.2 %multiply_reduce_fusion = (f32[16,384]{1,0:T(8,128)}, f32[24,16,384]{2,0,1:T(8,128)}, f32[24,16,16,384]{3,2,0,1:T(8,128)}, f32[24,16,16,384]{3,2,0,1:T(8,128)S(1)}) fusion(f32[24,16,384]{2,0,1:T(8,128)} %copy-done.40, f32[24,16,384]{2,0,1:T(8,128)} %copy-done.36, f32[24,16,16]{2,0,1:T(8,128)S(1)} %copy-done.53, f32[16,384]{1,0:T(8,128)S(1)} %copy-done.80, ...), kind=kLoop, calls=%fused_computation.17 | loop fusion | flops 25798656 | bytes 59645952 | tf_op jit(solution)/shard_map/reduce_sum | solution.py:263
  419.8 4.5 copy.153
  424.6 10.9 %fusion.260 = f32[384,1,384]{2,1,0:T(1,128)} fusion(f32[384,16,384]{2,1,0:T(8,128)} %bitcast.1168, f32[384,16,1]{1,2,0:T(1,128)S(1)} %copy.177), kind=kOutput, calls=%fused_computation.712 | convolution fusion | flops 28311552 | bytes 10051584 | tf_op jit(solution)/shard_map/tne,tn->te/dot_general | solution.py:216
  435.5 13.6 %fusion.169 = f32[384,1,16]{2,1,0:T(1,128)S(1)} fusion(f32[384,16,384]{2,1,0:T(8,128)S(1)} %bitcast.1169, f32[384,384,1]{1,0,2:T(8,128)S(1)} %bitcast.1173), kind=kOutput, calls=%fused_computation.441 | convolution fusion | flops 28311552 | bytes 10051584 | tf_op jit(solution)/shard_map/tne,te->tn/dot_general | solution.py:261
  449.2 13.8 %fusion.171 = f32[384,1,16]{2,1,0:T(1,128)S(1)} fusion(f32[384,16,384]{2,1,0:T(8,128)S(1)} %bitcast.1164, f32[384,384,1]{1,0,2:T(8,128)S(1)} %bitcast.1174), kind=kOutput, calls=%fused_computation.443 | convolution fusion | flops 28311552 | bytes 10051584 | tf_op jit(solution)/shard_map/tne,te->tn/dot_general | solution.py:261
  463.0 7.2 fusion.259
  470.3 4.9 copy.164
  476.3 9.9 %fusion.262 = f32[384,1,384]{2,1,0:T(1,128)} fusion(f32[384,16,384]{2,1,0:T(8,128)} %bitcast.1166, f32[384,16,1]{1,2,0:T(1,128)S(1)} %copy.185), kind=kOutput, calls=%fused_computation.714 | convolution fusion | flops 28311552 | bytes 10051584 | tf_op jit(solution)/shard_map/tne,tn->te/dot_general | solution.py:255
  486.3 13.6 %fusion.160 = f32[384,1,16]{2,1,0:T(1,128)S(1)} fusion(f32[384,16,384]{2,1,0:T(8,128)S(1)} %bitcast.1167, f32[384,384,1]{1,0,2:T(8,128)S(1)} %bitcast.1180), kind=kOutput, calls=%fused_computation.309 | convolution fusion | flops 28311552 | bytes 10051584 | tf_op jit(solution)/shard_map/tne,te->tn/dot_general | solution.py:258
  500.0 8.9 %fusion.261 = f32[384,1,384]{2,1,0:T(1,128)S(1)} fusion(f32[384,16,384]{2,1,0:T(8,128)} %bitcast.1160, f32[384,16,1]{1,2,0:T(1,128)S(1)} %copy-done.61), kind=kOutput, calls=%fused_computation.713 | convolution fusion | flops 28311552 | bytes 10051584 | tf_op jit(solution)/shard_map/tne,tn->te/dot_general | solution.py:255
  508.9 5.3 fusion.239
  515.8 16.2 %fusion.162 = f32[384,1,16]{2,1,0:T(1,128)S(1)} fusion(f32[384,16,384]{2,1,0:T(8,128)} %bitcast.1161, f32[384,384,1]{1,0,2:T(8,128)S(1)} %bitcast.1178), kind=kOutput, calls=%fused_computation.311 | convolution fusion | flops 28311552 | bytes 10051584 | tf_op jit(solution)/shard_map/tne,te->tn/dot_general | solution.py:258
  532.8 4.1 all-reduce.36
  539.2 5.7 multiply_reduce_fusion.17
  555.5 2.9 reshape.277
  575.0 4.5 reduce-scatter.2.cloned.1.call-done
  579.6 2.7 multiply_reduce_fusion.23
  583.6 109.2 %all-reduce.31.cloned.1.call-done = (f32[192]{0:T(256)}, f32[2,4,384]{2,1,0:T(4,128)}, f32[2,19,384]{2,1,0:T(8,128)}) async-done(((f32[192]{0:T(256)}, f32[2,4,384]{2,1,0:T(4,128)}, f32[2,19,384]{2,1,0:T(8,128)}), (f32[192]{0:T(256)}, f32[2,4,384]{2,1,0:T(4,128)}, f32[2,19,384]{2,1,0:T(8,128)})) %all-reduce.31.cloned.1.call-update) | async-done | bytes 71440 | tf_op jit(solution)/shard_map/psum | solution.py:338
  699.5 126.9 %all-reduce.33.cloned.1.call-done = (f32[384,2,384]{2,1,0:T(2,128)}, f32[384,384]{1,0:T(8,128)}, f32[2,384,56]{1,2,0:T(8,128)}, f32[2,24,384]{2,1,0:T(8,128)}) async-done(((f32[384,2,384]{2,1,0:T(2,128)}, f32[384,384]{1,0:T(8,128)}, f32[2,384,56]{1,2,0:T(8,128)}, f32[2,24,384]{2,1,0:T(8,128)}), (f32[384,2,384]{2,1,0:T(2,128)}, f32[384,384]{1,0:T(8,128)}, f32[2,384,56]{1,2,0:T(8,128)}, ...) | async-done | bytes 2015248 | tf_op jit(solution)/shard_map/psum | solution.py:338
  826.4 6.6 multiply_reduce_fusion.4
  833.0 3.5 multiply_reduce_fusion.18
  836.5 2.5 multiply_reduce_fusion.25
  841.3 5.2 stack.145
  846.5 5.1 stack.115
  853.1 3.3 all-reduce.20
  (766 shorter events, 296.0 us)
Async XLA Ops:
  7.3 12.5 %copy-start.55 = (f32[2,384,56]{1,2,0:T(8,128)S(1)}, f32[2,384,56]{1,2,0:T(8,128)}, u32[]{:S(2)}) copy-start(f32[2,384,56]{1,2,0:T(8,128)} %param.38) | copy-start | bytes 516100
  7.3 12.6 %copy-start.15 = (f32[384,384]{1,0:T(8,128)S(1)}, f32[384,384]{1,0:T(8,128)}, u32[]{:S(2)}) copy-start(f32[384,384]{1,0:T(8,128)} %param.37) | copy-start | bytes 1769476
  7.3 38.0 %all-reduce.35.cloned.1.call-start = ((), (), s32[]{:S(2)}) async-start(), calls=%async_computation.5 | async-start | bytes 344064 | tf_op jit(solution)/shard_map/psum | solution.py:188
  19.9 26.7 %copy-start.63 = (f32[2,24,384]{2,1,0:T(8,128)S(1)}, f32[2,24,384]{2,1,0:T(8,128)}, u32[]{:S(2)}) copy-start(f32[2,24,384]{2,1,0:T(8,128)} %param.39) | copy-start | bytes 221188
  22.1 29.8 %copy-start.13 = (f32[384,384]{1,0:T(8,128)}, f32[384,384]{1,0:T(8,128)S(1)}, u32[]{:S(2)}) copy-start(f32[384,384]{1,0:T(8,128)S(1)} %get-tuple-element.557) | copy-start | bytes 1769476
  24.4 549.4 %all-reduce.29.cloned.1.call-start = ((), (), s32[]{:S(2)}) async-start(), calls=%async_computation.2 | async-start | bytes 1179648 | tf_op jit(solution)/shard_map/psum | solution.py:320
  24.5 29.3 %copy-start.76 = (f32[2,19,384]{2,1,0:T(8,128)}, f32[2,19,384]{2,1,0:T(8,128)S(1)}, u32[]{:S(2)}) copy-start(f32[2,19,384]{2,1,0:T(8,128)S(1)} %copy.123) | copy-start | bytes 175108
  29.1 33.2 %copy-start.79 = (f32[16,384]{1,0:T(8,128)}, f32[16,384]{1,0:T(8,128)S(1)}, u32[]{:S(2)}) copy-start(f32[16,384]{1,0:T(8,128)S(1)} %get-tuple-element.772) | copy-start | bytes 73732
  61.6 44.0 %copy-start.44 = (f32[384,384]{1,0:T(8,128)}, f32[384,384]{1,0:T(8,128)S(1)}, u32[]{:S(2)}) copy-start(f32[384,384]{1,0:T(8,128)S(1)} %get-tuple-element.759) | copy-start | bytes 1769476
  107.4 12.3 %slice-start = ((s8[9437184]{0:T(1024)(128)(4,1)}), s8[4194304]{0:T(1024)(128)(4,1)S(1)}, s32[]{:S(2)}) async-start(s8[9437184]{0:T(1024)(128)(4,1)} %bitcast.1142), calls=%async_computation.6 | async-start | bytes 8388608
  107.4 12.3 %slice-start.1 = ((s8[9437184]{0:T(1024)(128)(4,1)}), s8[1048576]{0:T(1024)(128)(4,1)S(1)}, s32[]{:S(2)}) async-start(s8[9437184]{0:T(1024)(128)(4,1)} %bitcast.1142), calls=%async_computation.7 | async-start | bytes 2097152
  157.8 52.1 %slice-start.15 = ((s8[9437184]{0:T(1024)(128)(4,1)}), s8[1048576]{0:T(1024)(128)(4,1)S(1)}, s32[]{:S(2)}) async-start(s8[9437184]{0:T(1024)(128)(4,1)} %bitcast.1152), calls=%async_computation.21 | async-start | bytes 2097152
  195.4 14.5 %copy-start.29 = (f32[24,1,16,384]{3,2,0,1:T(8,128)S(1)}, f32[24,1,16,384]{3,2,0,1:T(8,128)}, u32[]{:S(2)}) copy-start(f32[24,1,16,384]{3,2,0,1:T(8,128)} %get-tuple-element.576) | copy-start | bytes 1769476
  195.4 14.5 %copy-start.32 = (f32[24,1,16,384]{3,2,0,1:T(8,128)S(1)}, f32[24,1,16,384]{3,2,0,1:T(8,128)}, u32[]{:S(2)}) copy-start(f32[24,1,16,384]{3,2,0,1:T(8,128)} %get-tuple-element.582) | copy-start | bytes 1769476
  195.4 14.5 %slice-start.16 = ((s8[9437184]{0:T(1024)(128)(4,1)}), s8[4194304]{0:T(1024)(128)(4,1)S(1)}, s32[]{:S(2)}) async-start(s8[9437184]{0:T(1024)(128)(4,1)} %bitcast.1152), calls=%async_computation.22 | async-start | bytes 8388608
  198.4 15.5 %copy-start.27 = (f32[24,1,16,384]{3,2,0,1:T(8,128)S(1)}, f32[24,1,16,384]{3,2,0,1:T(8,128)}, u32[]{:S(2)}) copy-start(f32[24,1,16,384]{3,2,0,1:T(8,128)} %get-tuple-element.577) | copy-start | bytes 1769476
  198.4 15.5 %copy-start.30 = (f32[24,1,16,384]{3,2,0,1:T(8,128)S(1)}, f32[24,1,16,384]{3,2,0,1:T(8,128)}, u32[]{:S(2)}) copy-start(f32[24,1,16,384]{3,2,0,1:T(8,128)} %get-tuple-element.583) | copy-start | bytes 1769476
  205.5 12.5 %copy-start.25 = (f32[24,1,16,384]{3,2,0,1:T(8,128)S(1)}, f32[24,1,16,384]{3,2,0,1:T(8,128)}, u32[]{:S(2)}) copy-start(f32[24,1,16,384]{3,2,0,1:T(8,128)} %get-tuple-element.578) | copy-start | bytes 1769476
  205.5 12.5 %copy-start.28 = (f32[24,1,16,384]{3,2,0,1:T(8,128)S(1)}, f32[24,1,16,384]{3,2,0,1:T(8,128)}, u32[]{:S(2)}) copy-start(f32[24,1,16,384]{3,2,0,1:T(8,128)} %get-tuple-element.584) | copy-start | bytes 1769476
  220.3 30.0 %copy-start.38 = (f32[384,384]{1,0:T(8,128)S(1)}, f32[384,384]{1,0:T(8,128)}, u32[]{:S(2)}) copy-start(f32[384,384]{1,0:T(8,128)} %copy-done.37) | copy-start | bytes 1769476
  274.9 50.7 %copy-start.24 = (f32[24,1,16,384]{3,2,0,1:T(8,128)S(1)}, f32[24,1,16,384]{3,2,0,1:T(8,128)}, u32[]{:S(2)}) copy-start(f32[24,1,16,384]{3,2,0,1:T(8,128)} %get-tuple-element.646) | copy-start | bytes 1769476
  280.6 50.7 %copy-start.22 = (f32[24,1,16,384]{3,2,0,1:T(8,128)S(1)}, f32[24,1,16,384]{3,2,0,1:T(8,128)}, u32[]{:S(2)}) copy-start(f32[24,1,16,384]{3,2,0,1:T(8,128)} %get-tuple-element.647) | copy-start | bytes 1769476
  280.6 50.7 %copy-start.23 = (f32[24,1,16,384]{3,2,0,1:T(8,128)S(1)}, f32[24,1,16,384]{3,2,0,1:T(8,128)}, u32[]{:S(2)}) copy-start(f32[24,1,16,384]{3,2,0,1:T(8,128)} %get-tuple-element.653) | copy-start | bytes 1769476
  315.4 20.3 %slice-start.9 = ((s8[9437184]{0:T(1024)(128)(4,1)}), s8[4194304]{0:T(1024)(128)(4,1)S(1)}, s32[]{:S(2)}) async-start(s8[9437184]{0:T(1024)(128)(4,1)} %bitcast.1148), calls=%async_computation.15 | async-start | bytes 8388608
  318.4 17.3 %copy-start.20 = (f32[24,1,16,384]{3,2,0,1:T(8,128)S(1)}, f32[24,1,16,384]{3,2,0,1:T(8,128)}, u32[]{:S(2)}) copy-start(f32[24,1,16,384]{3,2,0,1:T(8,128)} %get-tuple-element.648) | copy-start | bytes 1769476
  318.4 17.3 %copy-start.21 = (f32[24,1,16,384]{3,2,0,1:T(8,128)S(1)}, f32[24,1,16,384]{3,2,0,1:T(8,128)}, u32[]{:S(2)}) copy-start(f32[24,1,16,384]{3,2,0,1:T(8,128)} %get-tuple-element.654) | copy-start | bytes 1769476
  321.5 14.2 %slice-start.10 = ((s8[9437184]{0:T(1024)(128)(4,1)}), s8[4194304]{0:T(1024)(128)(4,1)S(1)}, s32[]{:S(2)}) async-start(s8[9437184]{0:T(1024)(128)(4,1)} %bitcast.1148), calls=%async_computation.16 | async-start | bytes 8388608
  325.6 14.3 %copy-start.18 = (f32[24,1,16,384]{3,2,0,1:T(8,128)S(1)}, f32[24,1,16,384]{3,2,0,1:T(8,128)}, u32[]{:S(2)}) copy-start(f32[24,1,16,384]{3,2,0,1:T(8,128)} %get-tuple-element.649) | copy-start | bytes 1769476
  325.6 14.3 %copy-start.19 = (f32[24,1,16,384]{3,2,0,1:T(8,128)S(1)}, f32[24,1,16,384]{3,2,0,1:T(8,128)}, u32[]{:S(2)}) copy-start(f32[24,1,16,384]{3,2,0,1:T(8,128)} %get-tuple-element.655) | copy-start | bytes 1769476
  347.1 34.4 %slice-start.21 = ((s8[9437184]{0:T(1024)(128)(4,1)}), s8[1048576]{0:T(1024)(128)(4,1)S(1)}, s32[]{:S(2)}) async-start(s8[9437184]{0:T(1024)(128)(4,1)} %bitcast.1156), calls=%async_computation.27 | async-start | bytes 2097152
  369.1 15.1 %copy-start.51 = (f32[24,16,384]{2,1,0:T(8,128)}, f32[24,16,384]{2,1,0:T(8,128)S(1)}, u32[]{:S(2)}) copy-start(f32[24,16,384]{2,1,0:T(8,128)S(1)} %get-tuple-element.293) | copy-start | bytes 1769476
  369.1 12.4 %slice-start.22 = ((s8[9437184]{0:T(1024)(128)(4,1)}), s8[4194304]{0:T(1024)(128)(4,1)S(1)}, s32[]{:S(2)}) async-start(s8[9437184]{0:T(1024)(128)(4,1)} %bitcast.1156), calls=%async_computation.28 | async-start | bytes 8388608
  372.1 14.3 %slice-start.24 = ((s8[9437184]{0:T(1024)(128)(4,1)}), s8[1048576]{0:T(1024)(128)(4,1)S(1)}, s32[]{:S(2)}) async-start(s8[9437184]{0:T(1024)(128)(4,1)} %bitcast.1158), calls=%async_computation.30 | async-start | bytes 2097152
  424.6 24.5 %slice-start.27 = ((s8[9437184]{0:T(1024)(128)(4,1)}), s8[4194304]{0:T(1024)(128)(4,1)S(1)}, s32[]{:S(2)}) async-start(s8[9437184]{0:T(1024)(128)(4,1)} %bitcast.1162), calls=%async_computation.33 | async-start | bytes 8388608
  424.6 24.5 %slice-start.28 = ((s8[9437184]{0:T(1024)(128)(4,1)}), s8[4194304]{0:T(1024)(128)(4,1)S(1)}, s32[]{:S(2)}) async-start(s8[9437184]{0:T(1024)(128)(4,1)} %bitcast.1162), calls=%async_computation.34 | async-start | bytes 8388608
  435.5 13.6 %slice-start.29 = ((s8[9437184]{0:T(1024)(128)(4,1)}), s8[1048576]{0:T(1024)(128)(4,1)S(1)}, s32[]{:S(2)}) async-start(s8[9437184]{0:T(1024)(128)(4,1)} %bitcast.1162), calls=%async_computation.35 | async-start | bytes 2097152
  449.2 21.1 %slice-start.30 = ((s8[9437184]{0:T(1024)(128)(4,1)}), s8[4194304]{0:T(1024)(128)(4,1)S(1)}, s32[]{:S(2)}) async-start(s8[9437184]{0:T(1024)(128)(4,1)} %bitcast.1170), calls=%async_computation.36 | async-start | bytes 8388608
  449.2 21.0 %slice-start.31 = ((s8[9437184]{0:T(1024)(128)(4,1)}), s8[4194304]{0:T(1024)(128)(4,1)S(1)}, s32[]{:S(2)}) async-start(s8[9437184]{0:T(1024)(128)(4,1)} %bitcast.1170), calls=%async_computation.37 | async-start | bytes 8388608
  476.3 23.7 %copy-start.61 = (f32[384,16,1]{1,2,0:T(1,128)S(1)}, f32[384,16,1]{1,2,0:T(1,128)}, u32[]{:S(2)}) copy-start(f32[384,16,1]{1,2,0:T(1,128)} %copy.179) | copy-start | bytes 73732
  486.2 22.7 %copy-start.8 = (f32[384,768]{1,0:T(8,128)S(1)}, f32[384,768]{1,0:T(8,128)}, u32[]{:S(2)}) copy-start(f32[384,768]{1,0:T(8,128)} %copy-done.7) | copy-start | bytes 3538948
  486.2 22.7 %copy-start.119 = (f32[384]{0:T(512)S(1)}, f32[384]{0:T(512)}, u32[]{:S(2)}) copy-start(f32[384]{0:T(512)} %get-tuple-element.444) | copy-start | bytes 4612
  486.2 22.7 %copy-start.120 = (f32[384]{0:T(512)S(1)}, f32[384]{0:T(512)}, u32[]{:S(2)}) copy-start(f32[384]{0:T(512)} %get-tuple-element.449) | copy-start | bytes 4612
  500.0 15.1 %copy-start.64 = (f32[2,24,384]{2,1,0:T(8,128)S(1)}, f32[2,24,384]{2,1,0:T(8,128)}, u32[]{:S(2)}) copy-start(f32[2,24,384]{2,1,0:T(8,128)} %param.39) | copy-start | bytes 221188
  500.0 15.8 %copy-start.43 = (f32[384,384]{1,0:T(8,128)S(1)}, f32[384,384]{1,0:T(8,128)}, u32[]{:S(2)}) copy-start(f32[384,384]{1,0:T(8,128)} %copy-done.42) | copy-start | bytes 1769476
  539.2 14.8 %copy-start.12 = (bf16[384,384]{0,1:T(8,128)(2,1)S(1)}, bf16[384,384]{0,1:T(8,128)(2,1)}, u32[]{:S(2)}) copy-start(bf16[384,384]{0,1:T(8,128)(2,1)} %copy-done.11) | copy-start | bytes 884740
  539.2 14.7 %copy-start.92 = (f32[384]{0:T(512)S(1)}, f32[384]{0:T(512)}, u32[]{:S(2)}) copy-start(f32[384]{0:T(512)} %copy-done.91) | copy-start | bytes 4612
  539.2 14.7 %copy-start.94 = (f32[384]{0:T(512)S(1)}, f32[384]{0:T(512)}, u32[]{:S(2)}) copy-start(f32[384]{0:T(512)} %param.35) | copy-start | bytes 4612
  545.0 14.8 %copy-start.16 = (f32[384,384]{1,0:T(8,128)S(1)}, f32[384,384]{1,0:T(8,128)}, u32[]{:S(2)}) copy-start(f32[384,384]{1,0:T(8,128)} %param.37) | copy-start | bytes 1769476
  545.3 23.9 %copy-start.35 = (f32[384,384]{1,0:T(8,128)S(1)}, f32[384,384]{1,0:T(8,128)}, u32[]{:S(2)}) copy-start(f32[384,384]{1,0:T(8,128)} %copy-done.34) | copy-start | bytes 1769476
  547.1 32.5 %reduce-scatter.2.cloned.1.call-start = ((), (), s32[]{:S(2)}) async-start(), calls=%async_computation.1 | async-start | bytes 884736 | tf_op jit(solution)/shard_map/reduce_scatter | solution.py:227
  555.5 27.5 %copy-start.60 = (f32[2,19,384]{2,0,1:T(2,128)S(1)}, f32[2,19,384]{2,0,1:T(2,128)}, u32[]{:S(2)}) copy-start(f32[2,19,384]{2,0,1:T(2,128)} %param.41) | copy-start | bytes 175108
  555.5 140.2 %copy-start.95 = (f32[192]{0:T(256)S(1)}, f32[192]{0:T(256)}, u32[]{:S(2)}) copy-start(f32[192]{0:T(256)} %get-tuple-element.526) | copy-start | bytes 2308
  555.5 142.0 %copy-start.83 = (f32[2,4,384]{2,1,0:T(4,128)S(1)}, f32[2,4,384]{2,1,0:T(4,128)}, u32[]{:S(2)}) copy-start(f32[2,4,384]{2,1,0:T(4,128)} %param.40) | copy-start | bytes 36868
  555.5 142.0 %copy-start.97 = (f32[2,4,384]{2,1,0:T(4,128)S(1)}, f32[2,4,384]{2,1,0:T(4,128)}, u32[]{:S(2)}) copy-start(f32[2,4,384]{2,1,0:T(4,128)} %param.47) | copy-start | bytes 36868
  555.5 142.0 %copy-start.98 = (f32[2,4,384]{2,1,0:T(4,128)S(1)}, f32[2,4,384]{2,1,0:T(4,128)}, u32[]{:S(2)}) copy-start(f32[2,4,384]{2,1,0:T(4,128)} %param.54) | copy-start | bytes 36868
  555.5 270.9 %copy-start.10 = (f32[384,2,384]{2,1,0:T(2,128)S(1)}, f32[384,2,384]{2,1,0:T(2,128)}, u32[]{:S(2)}) copy-start(f32[384,2,384]{2,1,0:T(2,128)} %param.36) | copy-start | bytes 3538948
  562.1 130.8 %all-reduce.31.cloned.1.call-start = ((), (), s32[]{:S(2)}) async-start(), calls=%async_computation.3 | async-start | bytes 174080 | tf_op jit(solution)/shard_map/psum | solution.py:338
  582.3 244.1 %all-reduce.33.cloned.1.call-start = ((), (), s32[]{:S(2)}) async-start(), calls=%async_computation.4 | async-start | bytes 4030464 | tf_op jit(solution)/shard_map/psum | solution.py:338
  695.0 138.0 %copy-start.62 = (f32[2,19,384]{2,1,0:T(8,128)}, f32[2,19,384]{2,1,0:T(8,128)S(1)}, u32[]{:S(2)}) copy-start(f32[2,19,384]{2,1,0:T(8,128)S(1)} %get-tuple-element.528) | copy-start | bytes 175108
  826.4 12.7 %copy-start.89 = (f32[2,24,384]{2,1,0:T(8,128)S(1)}, f32[2,24,384]{2,1,0:T(8,128)}, u32[]{:S(2)}) copy-start(f32[2,24,384]{2,1,0:T(8,128)} %get-tuple-element.504) | copy-start | bytes 221188
  826.4 42.2 %copy-start.96 = (f32[192]{0:T(256)S(1)}, f32[192]{0:T(256)}, u32[]{:S(2)}) copy-start(f32[192]{0:T(256)} %get-tuple-element.526) | copy-start | bytes 2308
  856.4 17.8 %copy-start.65 = (f32[2,24,384]{2,1,0:T(8,128)S(1)}, f32[2,24,384]{2,1,0:T(8,128)}, u32[]{:S(2)}) copy-start(f32[2,24,384]{2,1,0:T(8,128)} %param.39) | copy-start | bytes 221188
  856.4 17.8 %copy-start.77 = (f32[2,24,384]{2,1,0:T(8,128)S(1)}, f32[2,24,384]{2,1,0:T(8,128)}, u32[]{:S(2)}) copy-start(f32[2,24,384]{2,1,0:T(8,128)} %get-tuple-element.534) | copy-start | bytes 221188
  856.4 17.8 %copy-start.78 = (f32[2,24,384]{2,1,0:T(8,128)S(1)}, f32[2,24,384]{2,1,0:T(8,128)}, u32[]{:S(2)}) copy-start(f32[2,24,384]{2,1,0:T(8,128)} %get-tuple-element.535) | copy-start | bytes 221188
  (111 other events, 761.8 us)
Sparse Core Ops, SparseCore 0:
  24.5 20.6 all-reduce.34
  547.2 20.1 all-reduce.28
  570.3 9.2 reduce-scatter.1
  587.0 105.7 all-reduce.30
  700.4 125.9 all-reduce.32
where the time goes:
time: 895 us; the launch traced here: 882 us
  other arithmetic  378 us (42%)
  waiting for transfers between devices  257 us (29%)
  matrix products  126 us (14%)
  local copies, waits for them, and re-layouts  90.9 us (10%)
  between operations  20.6 us (2%)
  blocking collectives  9.49 us (1%)
    psum x2, waiting for transfers between devices, shards(): lax.psum((grad_gain, grad_in_w, grad_out_w, grad_xproj_all, grad_dtproj_a...  236 us
    unnamed x79, other arithmetic  121 us
    add x96, other arithmetic, carry_step(): return (end_prod * carried + end_run, carried)  73.6 us
    unnamed x373, local copies, waits for them, and re-layouts  47.8 us
    reduce_sum x2, other arithmetic, shards(): grad_alog = decay_rates * jnp.sum(grad_alpha * step_size[:, None, :], 0)  43.9 us
    dot_general x2, matrix products, shards(): jnp.einsum('tne,te->tn', grad_hidden, step_size * activation, precision=p...  29.9 us
    dynamic_update_slice x96, other arithmetic, linear_scan(): lax.scan(carry_step, jnp.zeros((block_total,) + inner, jnp.float32)[0], (...  29.7 us
    dot_general x2, matrix products, shards(): jnp.einsum('tne,te->tn', hidden_states, grad_y, precision=precise)  27.4 us
  transfers between devices with their start and end apart: 5, of which 4 were waited for; matrix products, arithmetic and copies ran while one was open for 5% of the time, Pallas kernels for 0%

commit v1 on v0

v1 whole, which is shorter than its diff:
```python
import functools

import jax
import jax.numpy as jnp
from jax import lax
from jax.experimental import pallas as pl
from jax.experimental.pallas import tpu as pltpu
from jax.sharding import PartitionSpec as P

STEP = 4
norm_eps = 1e-06
beta_one = 0.5
beta_two = 0.5
adam_eps = 1e-06
decay_rate = 0.01
learn_rate = 0.3
LOG2E = 1.4426950408889634
FAR = 1e30
FLOOR = -1e-26

f32 = jnp.float32
bf16 = jnp.bfloat16
HIGH = lax.Precision.HIGHEST
LANES = 128
ROWS = 16
MB = 1 << 20


def dot(left, right, dims, precision=None):
    return lax.dot_general(
        left, right, (dims, ((), ())), precision=precision, preferred_element_type=f32
    )


NN = ((1,), (0,))
TN = ((0,), (0,))
NT = ((1,), (1,))


def sigmoid(values):
    return 1.0 / (1.0 + jnp.exp(-values))


def silu_slope(values, sigma):
    return sigma * (1.0 + values * (1.0 - sigma))


def softplus(values):
    return jnp.maximum(values, 0.0) + jnp.log1p(jnp.exp(-jnp.abs(values)))


def wide(tile, times):
    return jnp.concatenate([tile] * times, axis=1)


def fold(values):
    total = values[0:8]
    for start in range(8, values.shape[0], 8):
        total = total + values[start : start + 8]
    return total


def shape(dims, dtype):
    return jax.ShapeDtypeStruct(dims, dtype)


def each_rows(length, body, carry=None, rows=ROWS):
    def step(index, held):
        return body(pl.multiple_of(index * rows, rows), held)

    return lax.fori_loop(0, length // rows, step, carry)


def front_kernel(
    hid, seg, gain, w_in, taps, params, w_xp,
    mix_out, gate_out, conv_out, part_out, norm_out, low_out, same_out,
    padded, sgpad,
):
    tokens, width = hid.shape
    chans = mix_out.shape[1]
    tiles = chans // LANES

    def normalise(start, held):
        source = hid[pl.ds(start, ROWS), :].astype(f32)
        scale = lax.rsqrt(jnp.sum(source * source, axis=1, keepdims=True) / width + norm_eps)
        norm_out[pl.ds(start, ROWS), :] = (source * scale * gain[...]).astype(bf16)
        return held

    each_rows(tokens, normalise, 0)
    for half in range(2):
        low_out[half] = w_in[:, half, :].astype(bf16)
    normed = norm_out[...]
    mixing = dot(normed, low_out[0], NN)
    mix_out[...] = mixing
    padded[0:8, :] = jnp.zeros((8, chans), f32)
    padded[pl.ds(8, tokens), :] = mixing
    padded[pl.ds(8 + tokens, 8), :] = jnp.zeros((8, chans), f32)
    gate_out[...] = dot(normed, low_out[1], NN)
    across = lax.broadcasted_iota(jnp.int32, (tokens, tokens), 0)
    along = lax.broadcasted_iota(jnp.int32, (tokens, tokens), 1)
    picked = jnp.where(across == along, seg[...].astype(f32), 0.0).astype(bf16)
    numbers = dot(picked, jnp.ones((tokens, LANES), bf16), NN)
    sgpad[0:8, :] = jnp.full((8, LANES), -1.0, f32)
    sgpad[pl.ds(8, tokens), :] = numbers
    sgpad[pl.ds(8 + tokens, 8), :] = jnp.full((8, LANES), -1.0, f32)
    width_taps = taps.shape[1]

    def convolve(start, held):
        window = padded[pl.ds(start, ROWS + 16), :]
        marks = sgpad[pl.ds(start, ROWS + 16), :]
        own = marks[8 : 8 + ROWS]
        base = window[8 : 8 + ROWS]
        for heading in range(2):
            total = params[0, heading : heading + 1, :] + taps[heading, 0:1, :] * base
            for offset in range(1, width_taps):
                begin = 8 - offset if heading == 0 else 8 + offset
                same = jnp.where(marks[begin : begin + ROWS] == own, 1.0, 0.0)
                if offset == 1:
                    same_out[heading, pl.ds(start, ROWS), :] = same
                moved = window[begin : begin + ROWS]
                total = total + taps[heading, offset : offset + 1, :] * moved * wide(same, tiles)
            conv_out[heading, pl.ds(start, ROWS), :] = total
        return held

    each_rows(tokens, convolve, 0)
    for heading in range(2):
        pre = conv_out[heading]
        act_low = (pre * sigmoid(pre)).astype(bf16)
        rows = w_xp.shape[1]
        part_out[heading * rows : (heading + 1) * rows, :] = dot(
            w_xp[heading].astype(bf16), act_low, NT
        )


SPAN = 64


def scan_kernel(
    own_part, far_part, conv_pre, gate, same, cot_own, cot_far, w_out, w_dt, params, core,
    grad_part, grad_act_out, gate_low_out, out_own, out_far, grad_out_w, grad_dt, grad_chan,
    proj, pre_step, grad_pre_all, grad_branch, step, far_step, inflow, result, through, decayed,
    grad_y, branch_low, maps_in, maps_out, states, picker, rates, rates2,
):
    tokens, chans = gate.shape
    tiles = chans // LANES
    rank = w_dt.shape[1]
    count = params.shape[0] - 3
    rows = rank + 2 * count
    blocks = tokens // LANES
    block_rows = LANES * count
    half_width = cot_own.shape[0]
    me = core[0]

    def cols(tile):
        return slice(tile * LANES, (tile + 1) * LANES)

    def base_of(heading, tile):
        return (heading * tiles + tile) * tokens

    def whole(ref, heading):
        return jnp.concatenate(
            [
                ref[base_of(heading, tile) : base_of(heading, tile) + tokens, :]
                for tile in range(tiles)
            ],
            axis=1,
        )

    proj[...] = own_part[...] + far_part[...]
    low_out = w_out[...].astype(bf16)
    low_cot = jnp.where(
        me == 0,
        jnp.concatenate([cot_own[...].astype(f32), cot_far[...].astype(f32)], 0),
        jnp.concatenate([cot_far[...].astype(f32), cot_own[...].astype(f32)], 0),
    ).astype(bf16)
    grad_branch[...] = dot(low_cot, low_out, ((0,), (1,)))
    for heading in range(2):
        for n in range(count):
            value = -jnp.exp(params[3 + n, heading : heading + 1, :])
            rates[heading, n : n + 1, :] = value
            rates2[heading, n : n + 1, :] = jnp.minimum(value * LOG2E, FLOOR)
        pre_step[heading] = (
            dot(proj[heading * rows : heading * rows + rank, :], w_dt[heading], TN, HIGH)
            + params[1, heading : heading + 1, :]
        )

    for tile in range(tiles):

        def prepare(start, held, tile=tile):
            here = pl.ds(start, SPAN)
            for heading in range(2):
                pre = conv_pre[heading, here, cols(tile)]
                act = pre * sigmoid(pre)
                size = softplus(pre_step[heading, here, cols(tile)])
                there = pl.ds(base_of(heading, tile) + start, SPAN)
                step[there, :] = size
                inflow[there, :] = size * act
                far_step[there, :] = jnp.where(same[heading, here, :] > 0.5, size, FAR)
            gated = gate[here, cols(tile)]
            grad_y[pl.ds(base_of(0, tile) + start, SPAN), :] = grad_branch[here, cols(tile)] * (
                gated * sigmoid(gated)
            )
            return held

        each_rows(tokens, prepare, 0, SPAN)

    picked = lax.broadcasted_iota(jnp.int32, (block_rows, LANES), 0) // count
    along = lax.broadcasted_iota(jnp.int32, (block_rows, LANES), 1)
    picker[...] = jnp.where(picked == along, 1.0, 0.0).astype(bf16)
    ones = jnp.ones((2 * LANES, LANES), bf16)
    for heading in range(2):
        for which, target in ((0, maps_in), (1, maps_out)):
            first = heading * rows + rank + which * count
            for block in range(blocks):
                tile = proj[first : first + count, cols(block)]
                high = tile.astype(bf16)
                rest = (tile - high.astype(f32)).astype(bf16)
                one = picker[...].reshape(LANES, count, LANES)
                spread = jnp.concatenate(
                    [
                        (one * high[None]).reshape(block_rows, LANES),
                        (one * rest[None]).reshape(block_rows, LANES),
                    ],
                    axis=1,
                )
                target[heading, block * block_rows : (block + 1) * block_rows, :] = dot(
                    spread, ones, NN
                )

    zero = jnp.zeros((count, chans), f32)
    blank = jnp.zeros((count, LANES), f32)
    states[0, 0:count, :] = zero
    states[1, tokens * count : (tokens + 1) * count, :] = zero
    group = 8
    pairs = [(heading, tile) for heading in range(2) for tile in range(tiles)]

    def row(ref, heading, tile, at):
        return ref[pl.ds(base_of(heading, tile) + at, 1), :]

    def forward(index, held):
        carried = list(held)
        for place in range(group):
            ahead = index * group + place
            for heading in range(2):
                at = ahead if heading == 0 else tokens - 1 - ahead
                slot = pl.multiple_of(at * count, count)
                kept = pl.multiple_of(slot + (count if heading == 0 else 0), count)
                enter = maps_in[heading, pl.ds(slot, count), :]
                leave = maps_out[heading, pl.ds(slot, count), :]
                for tile in range(tiles):
                    number = heading * tiles + tile
                    decay = jnp.exp2(
                        row(far_step, heading, tile, at) * rates2[heading, :, cols(tile)]
                    )
                    state = decay * carried[number] + enter * row(inflow, heading, tile, at)
                    carried[number] = state
                    result[pl.ds(base_of(heading, tile) + at, 1), :] = jnp.sum(
                        leave * state, axis=0, keepdims=True
                    )
                    states[heading, pl.ds(kept, count), cols(tile)] = state
        return tuple(carried)

    lax.fori_loop(0, tokens // group, forward, (blank,) * len(pairs))

    for tile in range(tiles):

        def finish_forward(start, held, tile=tile):
            here = pl.ds(start, SPAN)
            total = jnp.zeros((SPAN, LANES), f32)
            sums = []
            back = grad_y[pl.ds(base_of(0, tile) + start, SPAN), :]
            for heading in range(2):
                pre = conv_pre[heading, here, cols(tile)]
                act = pre * sigmoid(pre)
                total = total + result[pl.ds(base_of(heading, tile) + start, SPAN), :]
                total = total + params[2, heading : heading + 1, cols(tile)] * act
                sums.append(held[heading] + fold(back * act))
            gated = gate[here, cols(tile)]
            sigma = sigmoid(gated)
            branch_low[here, cols(tile)] = (total * (gated * sigma)).astype(bf16)
            gate_low_out[here, cols(tile)] = (
                grad_branch[here, cols(tile)] * total * silu_slope(gated, sigma)
            ).astype(bf16)
            return tuple(sums)

        skips = each_rows(tokens, finish_forward, (jnp.zeros((8, LANES), f32),) * 2, SPAN)
        for heading in range(2):
            grad_chan[2, heading : heading + 1, cols(tile)] = jnp.sum(
                skips[heading], axis=0, keepdims=True
            )
    branch = branch_low[...]
    sent = dot(low_out, branch, ((0,), (1,)))
    out_own[...] = jnp.where(me == 0, sent[:half_width], sent[half_width:])
    out_far[...] = jnp.where(me == 0, sent[half_width:], sent[:half_width])
    grad_w = dot(branch, low_cot, ((0,), (1,))).astype(bf16)
    for tile in range(grad_out_w.shape[0]):
        grad_out_w[tile] = grad_w[:, cols(tile)]

    def gather_map(heading, other, target_row):
        shift = count if heading == 0 else 0
        for block in range(blocks):
            begin = block * block_rows + shift
            left = states[heading, begin : begin + block_rows, :].astype(bf16)
            right = other[cols(block), :].astype(bf16)
            products = dot(left, right, NT) * picker[...].astype(f32)
            grad_part[target_row : target_row + count, cols(block)] = jnp.sum(
                products.reshape(LANES, count, LANES), axis=0
            )

    back_rows = whole(grad_y, 0)
    for heading in range(2):
        gather_map(heading, back_rows, heading * rows + rank + count)

    def backward(index, held):
        waiting = list(held[: len(pairs)])
        totals = list(held[len(pairs) :])
        for place in range(group):
            ahead = index * group + place
            for heading in range(2):
                at = tokens - 1 - ahead if heading == 0 else ahead
                slot = pl.multiple_of(at * count, count)
                after = pl.multiple_of((at + 1) * count, count)
                enter = maps_in[heading, pl.ds(slot, count), :]
                leave = maps_out[heading, pl.ds(slot, count), :]
                for tile in range(tiles):
                    number = heading * tiles + tile
                    decay = jnp.exp2(
                        row(far_step, heading, tile, at) * rates2[heading, :, cols(tile)]
                    )
                    grad = leave * row(grad_y, 0, tile, at) + waiting[number]
                    lead = decay * grad
                    waiting[number] = lead
                    before = states[
                        heading, pl.ds(slot if heading == 0 else after, count), cols(tile)
                    ]
                    slope = lead * before
                    here = pl.ds(base_of(heading, tile) + at, 1)
                    decayed[here, :] = jnp.sum(
                        slope * rates[heading, :, cols(tile)], axis=0, keepdims=True
                    )
                    through[here, :] = jnp.sum(grad * enter, axis=0, keepdims=True)
                    totals[number] = totals[number] + slope * row(step, heading, tile, at)
                    states[
                        heading, pl.ds(after if heading == 0 else slot, count), cols(tile)
                    ] = grad
        return tuple(waiting + totals)

    ends = lax.fori_loop(0, tokens // group, backward, (blank,) * (2 * len(pairs)))
    for number, (heading, tile) in enumerate(pairs):
        slopes = ends[len(pairs) + number] * rates[heading, :, cols(tile)]
        for n in range(count):
            grad_chan[3 + n, heading : heading + 1, cols(tile)] = slopes[n : n + 1]
    for heading in range(2):
        gather_map(heading, whole(inflow, heading), heading * rows + rank)

    for tile in range(tiles):

        def finish_backward(start, held, tile=tile):
            here = pl.ds(start, SPAN)
            sums = []
            back = grad_y[pl.ds(base_of(0, tile) + start, SPAN), :]
            for heading in range(2):
                there = pl.ds(base_of(heading, tile) + start, SPAN)
                pre = conv_pre[heading, here, cols(tile)]
                act = pre * sigmoid(pre)
                passed = through[there, :]
                grad_act_out[heading, here, cols(tile)] = (
                    passed * step[there, :] + back * params[2, heading : heading + 1, cols(tile)]
                )
                grad_pre = (decayed[there, :] + passed * act) * sigmoid(
                    pre_step[heading, here, cols(tile)]
                )
                grad_pre_all[heading, here, cols(tile)] = grad_pre
                sums.append(held[heading] + fold(grad_pre))
            return tuple(sums)

        biases = each_rows(tokens, finish_backward, (jnp.zeros((8, LANES), f32),) * 2, SPAN)
        for heading in range(2):
            grad_chan[1, heading : heading + 1, cols(tile)] = jnp.sum(
                biases[heading], axis=0, keepdims=True
            )
    for heading in range(2):
        grad_chan[0, heading : heading + 1, :] = jnp.zeros((1, chans), f32)
        grad_pre = grad_pre_all[heading]
        grad_dt[heading] = dot(
            proj[heading * rows : heading * rows + rank, :], grad_pre, NN, HIGH
        )
        grad_part[heading * rows : heading * rows + rank, :] = dot(
            w_dt[heading], grad_pre, NT, HIGH
        )


def back_kernel(
    own_part, far_part, grad_act, conv_pre, mixing, gate_low, normed, low_in, same_seg, w_xp, taps, hid, gain,
    grad_out_w, grad_dt, grad_chan, core,
    sums_out, in_own, in_far,
    padded, gpad, sgpad, mixed_low, small, act_low,
):
    tokens, width = hid.shape
    chans = mixing.shape[1]
    tiles = chans // LANES
    rows = w_xp.shape[1]
    width_taps = taps.shape[1]
    me = core[0]
    half_width = in_own.shape[0] - 8
    edge = jnp.zeros((8, chans), f32)
    padded[0:8, :] = edge
    padded[pl.ds(8 + tokens, 8), :] = edge
    padded[pl.ds(8, tokens), :] = mixing[...]
    gpad[0, 0:8, :] = edge
    gpad[1, 0:8, :] = edge
    gpad[0, pl.ds(8 + tokens, 8), :] = edge
    gpad[1, pl.ds(8 + tokens, 8), :] = edge
    sgpad[0:8, :] = jnp.full((8, LANES), -1.0, f32)
    sgpad[pl.ds(8 + tokens, 8), :] = jnp.full((8, LANES), -1.0, f32)
    across = lax.broadcasted_iota(jnp.int32, (tokens, tokens), 0)
    along = lax.broadcasted_iota(jnp.int32, (tokens, tokens), 1)
    picked = jnp.where(across == along, same_seg[...].astype(f32), 0.0).astype(bf16)
    sgpad[pl.ds(8, tokens), :] = dot(picked, jnp.ones((tokens, LANES), bf16), NN)

    parts = (own_part[...] + far_part[...]).astype(bf16)
    for heading in range(2):
        part = parts[heading * rows : (heading + 1) * rows, :]
        gpad[heading, pl.ds(8, tokens), :] = dot(part, w_xp[heading].astype(bf16), TN)

    blank = jnp.zeros((8, chans), f32)

    def through_conv(start, held):
        here = pl.ds(start, ROWS)
        window = padded[pl.ds(start, ROWS + 16), :]
        marks = sgpad[pl.ds(start, ROWS + 16), :]
        own = marks[8 : 8 + ROWS]
        base = window[8 : 8 + ROWS]
        sums = []
        for heading in range(2):
            pre = conv_pre[heading, here, :]
            sigma = sigmoid(pre)
            act_low[heading, here, :] = (pre * sigma).astype(bf16)
            inside = pl.ds(pl.multiple_of(start + 8, 8), ROWS)
            grad = (gpad[heading, inside, :] + grad_act[heading, here, :]) * silu_slope(pre, sigma)
            gpad[heading, inside, :] = grad
            sums.append(held[5 * heading] + fold(grad))
            sums.append(held[5 * heading + 1] + fold(grad * base))
            for offset in range(1, width_taps):
                begin = 8 - offset if heading == 0 else 8 + offset
                kept = jnp.where(marks[begin : begin + ROWS] == own, 1.0, 0.0)
                moved = window[begin : begin + ROWS]
                sums.append(held[5 * heading + 1 + offset] + fold(grad * moved * wide(kept, tiles)))
        return tuple(sums)

    sums = each_rows(tokens, through_conv, (blank,) * 10)
    small[...] = jnp.zeros(small.shape, f32)
    for heading in range(2):
        bias = jnp.sum(sums[5 * heading], axis=0, keepdims=True)
        for offset in range(width_taps):
            row = heading * width_taps + offset
            small[row : row + 1, :] = jnp.sum(sums[5 * heading + 1 + offset], axis=0, keepdims=True)
        for entry in range(grad_chan.shape[0]):
            row = 2 * width_taps + 2 * entry + heading
            small[row : row + 1, :] = (
                bias if entry == 0 else grad_chan[entry, heading : heading + 1, :]
            )

    def mixed(start, held):
        here = pl.ds(start, ROWS)
        marks = sgpad[pl.ds(start, ROWS + 16), :]
        own = marks[8 : 8 + ROWS]
        total = jnp.zeros((ROWS, chans), f32)
        for heading in range(2):
            window = gpad[heading, pl.ds(start, ROWS + 16), :]
            total = total + window[8 : 8 + ROWS] * taps[heading, 0:1, :]
            for offset in range(1, width_taps):
                begin = 8 + offset if heading == 0 else 8 - offset
                kept = jnp.where(marks[begin : begin + ROWS] == own, 1.0, 0.0)
                total = total + window[begin : begin + ROWS] * wide(kept, tiles) * taps[
                    heading, offset : offset + 1, :
                ]
        mixed_low[here, :] = total.astype(bf16)
        return held

    each_rows(tokens, mixed, 0)

    base_row = 0

    def put(values):
        nonlocal base_row
        for tile in range(values.shape[1] // LANES):
            sums_out[base_row : base_row + values.shape[0], :] = values[
                :, tile * LANES : (tile + 1) * LANES
            ].astype(bf16)
            base_row += values.shape[0]

    put(dot(normed[...], mixed_low[...], TN))
    put(dot(normed[...], gate_low[...], TN))
    for tile in range(tiles):
        sums_out[base_row : base_row + chans, :] = grad_out_w[tile]
        base_row += chans
    put(
        jnp.concatenate(
            [
                dot(parts[heading * rows : (heading + 1) * rows, :], act_low[heading], NN)
                for heading in range(2)
            ],
            axis=0,
        )
    )
    put(jnp.concatenate([grad_dt[0], grad_dt[1]], axis=0))

    partial = dot(mixed_low[...], low_in[0], NT) + dot(gate_low[...], low_in[1], NT)
    padded[pl.ds(8, tokens), :] = partial

    def gains(start, held):
        here = pl.ds(start, ROWS)
        source = hid[here, :].astype(f32)
        scale = lax.rsqrt(jnp.sum(source * source, axis=1, keepdims=True) / width + norm_eps)
        inside = pl.ds(pl.multiple_of(start + 8, 8), ROWS)
        grad = padded[inside, :]
        padded[inside, :] = grad * gain[...]
        return held + fold(grad * source * scale)

    gain_sum = each_rows(tokens, gains, jnp.zeros((8, width), f32))
    small[46:47, :] = jnp.sum(gain_sum, axis=0, keepdims=True)
    put(small[...])
    sums_out[base_row:, :] = jnp.zeros((sums_out.shape[0] - base_row, LANES), bf16)

    weighted = padded[pl.ds(8, tokens), :]
    products = weighted * hid[...].astype(f32)
    turned = weighted.T
    row_dot = dot(jnp.ones((8, width), f32), products, NT, HIGH)
    in_own[0:half_width, :] = jnp.where(me == 0, turned[:half_width], turned[half_width:])
    in_far[0:half_width, :] = jnp.where(me == 0, turned[half_width:], turned[:half_width])
    in_own[pl.ds(half_width, 8), :] = row_dot
    in_far[pl.ds(half_width, 8), :] = row_dot


def outputs_kernel(hid, cot_own, out_own, out_far, in_own, in_far, core, output, input_grad):
    width = hid.shape[1]
    half_width = cot_own.shape[0]
    me = core[0]
    source = hid[...].astype(f32).T
    scale = lax.rsqrt(jnp.sum(source * source, axis=0, keepdims=True) / width + norm_eps)
    own = jnp.where(me == 0, source[:half_width], source[half_width:])
    output[...] = (own + (out_own[...] + out_far[...])).astype(bf16)
    weighted = in_own[0:half_width, :] + in_far[0:half_width, :]
    row_dot = in_own[half_width : half_width + 1, :] + in_far[half_width : half_width + 1, :]
    input_grad[...] = (
        cot_own[...].astype(f32)
        + scale * weighted
        - own * (scale * scale * scale) * (row_dot / width)
    )


def lamb_moments(weight, grad, first, second):
    first_new = beta_one * first + (1.0 - beta_one) * grad
    second_new = beta_two * second + (1.0 - beta_two) * grad * grad
    update = (
        first_new
        / (1.0 - beta_one**STEP)
        / (jnp.sqrt(second_new / (1.0 - beta_two**STEP)) + adam_eps)
        + decay_rate * weight
    )
    return (first_new, second_new, update)


def moments_kernel(
    sums,
    w_in, w_out, w_xp, w_dt, w_cv, w_cp,
    a_in, a_out, a_xp, a_dt, a_cv, a_cp,
    b_in, b_out, b_xp, b_dt, b_cv, b_cp,
    x_in, x_out, x_xp, x_dt, x_cv, x_cp,
    y_in, y_out, y_xp, y_dt, y_cv, y_cp,
    u_in, u_out, u_xp, u_dt, u_cv, u_cp,
    norms, stats,
):
    width, _, chans = w_in.shape
    tiles = chans // LANES
    zero = jnp.zeros((8, chans), f32)
    norms[...] = jnp.zeros(norms.shape, f32)

    def note(place, weight_sq, update_sq):
        for row, values in ((place, weight_sq), (6 + place, update_sq)):
            total = jnp.sum(values, axis=0, keepdims=True)
            lanes = total[:, 0:LANES]
            for tile in range(1, values.shape[1] // LANES):
                lanes = lanes + total[:, tile * LANES : (tile + 1) * LANES]
            norms[row : row + 1, :] = lanes

    def fetch(base, stride, start, count, number):
        return jnp.concatenate(
            [sums[pl.ds(base + tile * stride + start, count), :].astype(f32) for tile in range(number)],
            axis=1,
        )

    held = (zero, zero)
    mean_rows = zero
    for half in range(2):

        def one_in(start, kept, half=half):
            here = pl.ds(start, ROWS)
            grad = fetch(half * tiles * width, width, start, ROWS, tiles)
            weight = w_in[here, half, :]
            first, second, update = lamb_moments(
                weight, grad, a_in[here, half, :], b_in[here, half, :]
            )
            x_in[here, half, :] = first
            y_in[here, half, :] = second
            u_in[half, here, :] = update
            return (
                kept[0] + fold(weight * weight),
                kept[1] + fold(update * update),
                kept[2] + fold(update),
            )

        got = each_rows(width, one_in, (held[0], held[1], mean_rows))
        held, mean_rows = (got[0], got[1]), got[2]
    note(0, *held)
    base = 2 * tiles * width
    in_sum = jnp.sum(mean_rows, axis=0, keepdims=True)
    in_mean = in_sum / (2 * width)

    def spread_in(start, kept):
        here = pl.ds(start, ROWS)
        for half in range(2):
            away = u_in[half, here, :] - in_mean
            kept = kept + fold(away * away)
        return kept

    in_dev = jnp.sum(each_rows(width, spread_in, zero), axis=0, keepdims=True)

    def one_out(start, kept):
        here = pl.ds(start, ROWS)
        grad = fetch(base, chans, start, ROWS, width // LANES)
        weight = w_out[here, :]
        first, second, update = lamb_moments(weight, grad, a_out[here, :], b_out[here, :])
        x_out[here, :] = first
        y_out[here, :] = second
        u_out[here, :] = update
        return (kept[0] + fold(weight * weight), kept[1] + fold(update * update))

    note(1, *each_rows(chans, one_out, (jnp.zeros((8, width), f32),) * 2))
    base += chans * (width // LANES)
    ones = jnp.ones((8, width), f32)
    out_all = u_out[...]
    out_mean = jnp.sum(out_all, axis=1, keepdims=True) / width
    away = out_all - out_mean
    out_sum = dot(ones, out_all, NT, HIGH)
    out_dev = dot(ones, away * away, NT, HIGH)
    stats[0:1, :] = in_mean
    stats[1:2, :] = in_dev
    stats[2:3, :] = out_sum[0:1] / width
    stats[3:4, :] = out_dev[0:1]
    stats[4:8, :] = jnp.zeros((4, chans), f32)

    def small(place, weight, grad, first, second, pads, x_ref, y_ref, u_ref, index):
        first_new, second_new, update = lamb_moments(weight, grad, first, second)
        x_ref[index] = first_new
        y_ref[index] = second_new
        u_ref[index] = update
        return (weight * weight, update * update)

    def rows_sum(values):
        return jnp.sum(values, axis=0, keepdims=True)

    rows = w_xp.shape[1]
    pair = [jnp.zeros((1, chans), f32)] * 2
    for heading in range(2):
        grad = fetch(base, 2 * rows, heading * rows, rows, tiles)
        got = small(2, w_xp[heading], grad, a_xp[heading], b_xp[heading], None, x_xp, y_xp, u_xp, heading)
        pair = [pair[0] + rows_sum(got[0]), pair[1] + rows_sum(got[1])]
    note(2, *pair)
    base += 2 * rows * tiles
    rank = w_dt.shape[1]
    grads = fetch(base, 2 * rank, 0, 2 * rank, tiles)
    pair = [jnp.zeros((1, chans), f32)] * 2
    for heading in range(2):
        grad = grads[heading * rank : (heading + 1) * rank]
        got = small(3, w_dt[heading], grad, a_dt[heading], b_dt[heading], None, x_dt, y_dt, u_dt, heading)
        pair = [pair[0] + rows_sum(got[0]), pair[1] + rows_sum(got[1])]
    note(3, *pair)
    base += 2 * rank * tiles
    grads = fetch(base, 48, 0, 48, tiles)
    taps = w_cv.shape[1]
    pair = [jnp.zeros((1, chans), f32)] * 2
    for heading in range(2):
        grad = grads[heading * taps : (heading + 1) * taps]
        got = small(4, w_cv[heading], grad, a_cv[heading], b_cv[heading], None, x_cv, y_cv, u_cv, heading)
        pair = [pair[0] + rows_sum(got[0]), pair[1] + rows_sum(got[1])]
    note(4, *pair)
    pair = [jnp.zeros((2, chans), f32)] * 2
    for entry in range(w_cp.shape[0]):
        row = 2 * taps + 2 * entry
        grad = grads[row : row + 2]
        got = small(5, w_cp[entry], grad, a_cp[entry], b_cp[entry], None, x_cp, y_cp, u_cp, entry)
        pair = [pair[0] + got[0], pair[1] + got[1]]
    note(5, *pair)
    for tile in range(tiles):
        norms[12 + tile : 13 + tile, :] = grads[46:47, tile * LANES : (tile + 1) * LANES]


def apply_kernel(
    norms_own, norms_far, stats,
    w_in, w_out, w_xp, w_dt, w_cv, w_cp,
    u_in, u_out, u_xp, u_dt, u_cv, u_cp,
    gain, gain_first, gain_second,
    n_in, c_in, n_out, c_out, n_xp, c_xp, n_dt, c_dt, n_cv, c_cv, n_cp, c_cp,
    g_first, g_second, g_new, g_copy, norms_out, stats_out,
):
    width, _, chans = w_in.shape
    totals = norms_own[...] + norms_far[...]
    gain_grad = jnp.concatenate([totals[12 + tile : 13 + tile, :] for tile in range(width // LANES)], axis=1)
    first, second, update = lamb_moments(
        gain[...], gain_grad, gain_first[...], gain_second[...]
    )
    sums = jnp.sum(totals, axis=1, keepdims=True)
    weight_sq = [jnp.sum(gain[...] * gain[...], axis=1, keepdims=True)] + [
        sums[place : place + 1] for place in range(6)
    ]
    update_sq = [jnp.sum(update * update, axis=1, keepdims=True)] + [
        sums[6 + place : 7 + place] for place in range(6)
    ]
    scales = []
    for place in range(7):
        weight_norm = jnp.sqrt(weight_sq[place])
        update_norm = jnp.sqrt(update_sq[place])
        scales.append(learn_rate * weight_norm / (update_norm + adam_eps))
        norms_out[0:1, place : place + 1] = weight_norm
        norms_out[1:2, place : place + 1] = update_norm
    fresh = gain[...] - scales[0] * update
    g_first[...] = first
    g_second[...] = second
    g_new[...] = fresh
    g_copy[...] = fresh.astype(bf16)

    def one_in(start, held):
        here = pl.ds(start, ROWS)
        for half in range(2):
            fresh = w_in[here, half, :] - scales[1] * u_in[half, here, :]
            n_in[here, half, :] = fresh
            c_in[here, half, :] = fresh.astype(bf16)
        return held

    each_rows(width, one_in, 0)

    def one_out(start, held):
        here = pl.ds(start, ROWS)
        fresh = w_out[here, :] - scales[2] * u_out[here, :]
        n_out[here, :] = fresh
        c_out[here, :] = fresh.astype(bf16)
        return held

    each_rows(chans, one_out, 0)
    for place, weight, change, fresh_ref, copy in (
        (3, w_xp, u_xp, n_xp, c_xp),
        (4, w_dt, u_dt, n_dt, c_dt),
        (5, w_cv, u_cv, n_cv, c_cv),
        (6, w_cp, u_cp, n_cp, c_cp),
    ):
        for index in range(weight.shape[0]):
            fresh = weight[index] - scales[place] * change[index]
            fresh_ref[index] = fresh
            copy[index] = fresh.astype(bf16)
    count_in = 2.0 * width
    count_out = 1.0 * width
    mean_in = scales[1] * stats[0:1, :]
    mean_out = scales[2] * stats[2:3, :]
    mean = (count_in * mean_in + count_out * mean_out) / (count_in + count_out)
    gap_in = mean_in - mean
    gap_out = mean_out - mean
    spread = (
        scales[1] * scales[1] * stats[1:2, :]
        + scales[2] * scales[2] * stats[3:4, :]
        + count_in * gap_in * gap_in
        + count_out * gap_out * gap_out
    ) / (count_in + count_out)
    stats_out[0:1, :] = mean
    stats_out[1:2, :] = spread


def call(kernel, outs, args, scratch=(), limit=32, scalars=0, flops=0):
    specs = [pl.BlockSpec(memory_space=pltpu.VMEM)] * (len(args) - scalars)
    specs += [pl.BlockSpec(memory_space=pltpu.SMEM)] * scalars
    return pl.pallas_call(
        kernel,
        out_shape=outs,
        in_specs=specs,
        out_specs=[pl.BlockSpec(memory_space=pltpu.VMEM)] * len(outs),
        scratch_shapes=list(scratch),
        compiler_params=pltpu.CompilerParams(vmem_limit_bytes=limit * MB),
        cost_estimate=pl.CostEstimate(flops=flops, bytes_accessed=8 * MB, transcendentals=0),
    )(*args)


def program(
    dp,
    hidden_in, out_cot, segment_ids,
    norm_gain, in_weight, out_weight, xproj_weight, dtproj_weight, conv_weight, chan_params,
    first_norm_gain, first_in_weight, first_out_weight, first_xproj_weight,
    first_dtproj_weight, first_conv_weight, first_chan_params,
    second_norm_gain, second_in_weight, second_out_weight, second_xproj_weight,
    second_dtproj_weight, second_conv_weight, second_chan_params,
):
    tokens, width = hidden_in.shape
    chans = in_weight.shape[2]
    half_width = first_norm_gain.shape[0]
    tiles = chans // LANES
    rank = dtproj_weight.shape[1]
    count = chan_params.shape[1] - 3
    rows = rank + 2 * count
    taps = conv_weight.shape[1]

    def swap(values):
        return lax.ppermute(values, "chan", [(0, 1), (1, 0)])

    me = lax.axis_index("chan")
    core = me.astype(jnp.int32).reshape(1)
    cot_own = out_cot.T
    cot_far = swap(cot_own)
    segments = segment_ids.reshape(1, tokens)
    gain = norm_gain.reshape(1, width)
    moments_own = jnp.stack([first_norm_gain, second_norm_gain])
    moments_far = swap(moments_own)
    moments_gain = jnp.where(
        me == 0,
        jnp.concatenate([moments_own, moments_far], 1),
        jnp.concatenate([moments_far, moments_own], 1),
    )

    def flip(values):
        return jnp.swapaxes(values, 1, 2)

    def turn(values):
        return jnp.swapaxes(values, 0, 1)

    w_xp = flip(xproj_weight)
    w_cp = turn(chan_params)
    square = (tokens, chans)

    mixing, gate, conv_pre, part, normed, low_in, same = call(
        front_kernel,
        [
            shape(square, f32), shape(square, f32), shape((2,) + square, f32),
            shape((2 * rows, tokens), f32), shape((tokens, width), bf16),
            shape((2, width, chans), bf16), shape((2, tokens, LANES), f32),
        ],
        [hidden_in, segments, gain, in_weight, conv_weight, w_cp, w_xp],
        [pltpu.VMEM((tokens + 16, chans), f32), pltpu.VMEM((tokens + 16, LANES), f32)],
    )
    part_far = swap(part)
    big = pltpu.VMEM((2,) + square, f32)
    flat = pltpu.VMEM((2 * tiles * tokens, LANES), f32)
    grad_part, grad_act, gate_low, out_own, out_send, grad_out_w, grad_dt, grad_chan = call(
        scan_kernel,
        [
            shape((2 * rows, tokens), f32), shape((2,) + square, f32), shape(square, bf16),
            shape((half_width, tokens), f32), shape((half_width, tokens), f32),
            shape((width // LANES, chans, LANES), bf16), shape((2, rank, chans), f32),
            shape((3 + count, 2, chans), f32),
        ],
        [part, part_far, conv_pre, gate, same, cot_own, cot_far, out_weight, dtproj_weight, w_cp, core],
        [
            pltpu.VMEM((2 * rows, tokens), f32), big, big, pltpu.VMEM(square, f32),
            flat, flat, flat, flat, flat, flat, pltpu.VMEM((tiles * tokens, LANES), f32),
            pltpu.VMEM(square, bf16),
            pltpu.VMEM((2, tokens * count, LANES), f32), pltpu.VMEM((2, tokens * count, LANES), f32),
            pltpu.VMEM((2, (tokens + 1) * count, chans), f32),
            pltpu.VMEM((LANES * count, LANES), bf16),
            pltpu.VMEM((2, count, chans), f32), pltpu.VMEM((2, count, chans), f32),
        ],
        limit=60, scalars=1,
    )
    grad_far = swap(grad_part)
    out_far = swap(out_send)
    total_rows = (
        2 * tiles * width + (width // LANES) * chans + tiles * (2 * rows + 2 * rank + 48)
    )
    chunk = -(-total_rows // (dp * 16)) * 16
    sums, in_own, in_send = call(
        back_kernel,
        [
            shape((dp * chunk, LANES), bf16),
            shape((half_width + 8, tokens), f32), shape((half_width + 8, tokens), f32),
        ],
        [
            grad_part, grad_far, grad_act, conv_pre, mixing, gate_low, normed, low_in, segments,
            w_xp, conv_weight, hidden_in, gain, grad_out_w, grad_dt, grad_chan, core,
        ],
        [
            pltpu.VMEM((tokens + 16, chans), f32), pltpu.VMEM((2, tokens + 16, chans), f32),
            pltpu.VMEM((tokens + 16, LANES), f32), pltpu.VMEM(square, bf16),
            pltpu.VMEM((48, chans), f32), pltpu.VMEM((2,) + square, bf16),
        ],
        scalars=1,
    )
    in_far = swap(in_send)
    gathered = lax.all_to_all(sums, "dp", 0, 0, tiled=True).reshape(dp, chunk, LANES)
    shard = jnp.sum(gathered.astype(f32), axis=0).astype(bf16)
    copies = jnp.broadcast_to(shard[None], (dp, chunk, LANES)).reshape(dp * chunk, LANES)
    totals = lax.all_to_all(copies, "dp", 0, 0, tiled=True)
    output, input_grad = call(
        outputs_kernel,
        [shape((half_width, tokens), bf16), shape((half_width, tokens), f32)],
        [hidden_in, cot_own, out_own, out_far, in_own, in_far, core],
        scalars=1,
    )

    weights = [in_weight, out_weight, w_xp, dtproj_weight, conv_weight, w_cp]
    firsts = [
        first_in_weight, first_out_weight, flip(first_xproj_weight), first_dtproj_weight,
        first_conv_weight, turn(first_chan_params),
    ]
    seconds = [
        second_in_weight, second_out_weight, flip(second_xproj_weight), second_dtproj_weight,
        second_conv_weight, turn(second_chan_params),
    ]
    same_shapes = [shape(tensor.shape, f32) for tensor in weights]
    update_shapes = [shape((2, width, chans), f32)] + same_shapes[1:]
    got = call(
        moments_kernel,
        same_shapes * 2 + update_shapes + [shape((16, LANES), f32), shape((8, chans), f32)],
        [totals, *weights, *firsts, *seconds],
    )
    new_first, new_second, updates = got[0:6], got[6:12], got[12:18]
    norms, stats = got[18], got[19]
    norms_far = swap(norms)
    pairs = []
    for tensor in weights:
        pairs += [shape(tensor.shape, f32), shape(tensor.shape, bf16)]
    done = call(
        apply_kernel,
        pairs
        + [shape((1, width), f32)] * 3
        + [shape((1, width), bf16), shape((2, 7), f32), shape((2, chans), f32)],
        [norms, norms_far, stats, *weights, *updates, gain, moments_gain[0:1], moments_gain[1:2]],
    )
    own_start = me * half_width

    def own(values):
        return lax.dynamic_slice_in_dim(values[0], own_start, half_width)

    flat = [own(done[12]), own(done[13]), own(done[14]), own(done[15])]
    for place in range(6):
        entry = [new_first[place], new_second[place], done[2 * place], done[2 * place + 1]]
        if place == 2:
            entry = [flip(tensor) for tensor in entry]
        if place == 5:
            entry = [turn(tensor) for tensor in entry]
        flat += entry
    return (output.T, input_grad.T, *flat, done[16].T, done[17])


def solution(mesh):
    rows = P("dp", None)
    cells = P("dp", "chan")
    last = P(None, None, "chan")
    first = P("chan", None)
    middle = P(None, "chan", None)
    tensors = (last, first, middle, last, last, last)
    outs = [cells, cells] + [P("chan")] * 4
    for spec in tensors:
        outs += [spec] * 4
    return jax.shard_map(
        functools.partial(program, mesh.shape["dp"]),
        mesh=mesh,
        in_specs=(rows, cells, P("dp"), P(), *tensors, P("chan"), *tensors, P("chan"), *tensors),
        out_specs=(*outs, P(), P(None, "chan")),
        check_vma=False,
    )
```

time: 895 us -> 162 us (0.18); the launches traced: 882 us -> 161 us
  other arithmetic: 378 us -> 0.23 us
  waiting for transfers between devices: 257 us -> 25.6 us
  matrix products: 126 us -> 0 us
  Pallas kernels: 0 us -> 64.8 us
  local copies, waits for them, and re-layouts: 90.9 us -> 28.7 us
  blocking collectives: 9.49 us -> 34.6 us
  between operations: 20.6 us -> 0.95 us
    psum x4 -> x0, waiting for transfers between devices: 252 us -> none  [the longest x2 236 us: shards(): lax.psum((grad_gain, grad_in_w, grad_out_w, grad_xproj_all, grad_dtproj_a...]
    dot_general x26 -> x0, matrix products: 126 us -> none  [the longest x2 29.9 us: shards(): jnp.einsum('tne,te->tn', grad_hidden, step_size * activation, precision=p...]
    unnamed x79 -> x0, other arithmetic: 121 us -> none
    add x100 -> x0, other arithmetic: 87.9 us -> none  [the longest x96 73.6 us: carry_step(): return (end_prod * carried + end_run, carried)]
    reduce_sum x19 -> x1, other arithmetic: 85.9 us -> 0.14 us  [program(): shard = jnp.sum(gathered.astype(f32), axis=0).astype(bf16)]
    pallas_call x0 -> x6, Pallas kernels: none -> 64.8 us  [call(): pl.pallas_call(kernel, out_shape=outs, in_specs=specs, out_specs=[pl.Bloc...]
    all_to_all x0 -> x1, blocking collectives: none -> 34.6 us  [program(): lax.all_to_all(sums, 'dp', 0, 0, tiled=True).reshape(dp, chunk, LANES)]
    dynamic_update_slice x96 -> x0, other arithmetic: 29.7 us -> none  [linear_scan(): lax.scan(carry_step, jnp.zeros((block_total,) + inner, jnp.float32)[0], (...]
  transfers between devices with their start and end apart: 5 -> 8, of which waited for: 4 -> 4; matrix products, arithmetic and copies ran while one was open for 5% -> 0% of each run, Pallas kernels for 0% -> 6%
where the time goes in v1:
time: 162 us; the launch traced here: 161 us
  Pallas kernels  64.8 us (40%)
  blocking collectives  34.6 us (21%)
  local copies, waits for them, and re-layouts  28.7 us (18%)
  waiting for transfers between devices  25.6 us (16%)
  starting transfers between devices  5.6 us (3%)
    pallas_call x6, Pallas kernels, call(): pl.pallas_call(kernel, out_shape=outs, in_specs=specs, out_specs=[pl.Bloc...  64.8 us
    all_to_all x1, blocking collectives, program(): lax.all_to_all(sums, 'dp', 0, 0, tiled=True).reshape(dp, chunk, LANES)  34.6 us
    unnamed x90, local copies, waits for them, and re-layouts  24.3 us
    all_to_all x1, waiting for transfers between devices, program(): totals = lax.all_to_all(copies, 'dp', 0, 0, tiled=True)  22.4 us
    all_to_all x1, starting transfers between devices, program(): totals = lax.all_to_all(copies, 'dp', 0, 0, tiled=True)  4.12 us
    ppermute x7, waiting for transfers between devices, swap(): return lax.ppermute(values, 'chan', [(0, 1), (1, 0)])  3.26 us
  transfers between devices with their start and end apart: 8, of which 4 were waited for; matrix products, arithmetic and copies ran while one was open for 0% of the time, Pallas kernels for 6%

profile of v1, /device:TPU:0, one launch (start us, length us, event | category | flops | bytes accessed | tf_op | source)
XLA Modules:
  0.0 160.5 jit_solution(13327294487389911151)
XLA Ops:
  0.7 0.7 reshape.87.gain
  1.4 0.7 reshape.86.seg.same_seg
  2.0 1.3 copy-done
  3.3 0.9 copy-done.5
  4.2 1.0 copy-done.7
  5.2 0.8 copy-done.12
  6.0 0.7 copy-done.26
  6.7 5.5 %shard_map.479 = (f32[384,384]{1,0:T(8,128)S(1)}, f32[384,384]{1,0:T(8,128)S(1)}, f32[2,384,384]{2,1,0:T(8,128)S(1)}, f32[112,384]{1,0:T(8,128)S(1)}, bf16[384,3...) custom-call(bf16[384,384]{1,0:T(8,128)(2,1)S(1)} %copy-done.7, ...), custom_call_target="tpu_custom_call" | custom-call | bytes 8388608 | tf_op jit(solution)/shard_map/pallas_call | solution.py:782
  12.2 0.0 copy-start.3
  12.2 1.0 copy-done.3
  13.2 0.8 copy-done.19
  14.0 0.7 copy-done.20
  14.8 0.5 collective-permute-start
  15.2 0.1 collective-permute-start.1
  15.3 1.3 collective-permute-done.1.cot_far
  16.6 0.0 collective-permute-done.far_part
  16.6 0.6 copy-done.42
  17.3 0.1 copy-done.41
  17.3 37.7 %shard_map.480 = (f32[112,384]{1,0:T(8,128)}, f32[2,384,384]{2,1,0:T(8,128)}, bf16[384,384]{1,0:T(8,128)(2,1)}, f32[192,384]{1,0:T(8,128)}, f32[192,384]{1,0:T(8...) custom-call(f32[112,384]{1,0:T(8,128)} %copy-done.31, f32[112,384]{1,0:T(8,128)} %copy-done.41, ...), custom_call_target="tpu_custom_call" | custom-call | bytes 8388608 | tf_op jit(solution)/shard_map/pallas_call | solution.py:782
  55.0 0.3 collective-permute-start.3
  55.3 1.4 collective-permute-done.3.far_part
  56.7 0.0 copy-start.11
  56.7 1.3 copy-done.11
  58.0 1.0 copy-done.23
  59.0 1.0 copy-done.24
  59.9 0.9 copy-done.30
  60.9 0.9 copy-done.34
  61.7 0.8 copy-done.37
  62.6 7.7 %shard_map.481 = (bf16[4096,128]{1,0:T(8,128)(2,1)S(1)}, f32[200,384]{1,0:T(8,128)S(1)}, f32[200,384]{1,0:T(8,128)S(1)}) custom-call(f32[112,384]{1,0:T(8,128)S(1)} %copy-done.30, f32[112,384]{1,0:T(8,128)S(1)} %collective-permute-done.3.far_part, f32[2,384,384]{2,1,0:T(8,128)S(1)} %copy-done.11, f32[2,384,384]{2,1,0:T(8,128)S(1)} %copy-done.4, ...), custom_call_target="tpu_custom_call" | custom-call | bytes 8388608 | tf_op jit(solution)/shard_map/pallas_call | solution.py:782
  70.3 0.7 copy-done.21
  71.0 0.7 copy-done.40
  71.7 34.6 %all_to_all.17 = bf16[16,256,128]{2,1,0:T(8,128)(2,1)S(1)} all-to-all(bf16[16,256,128]{2,1,0:T(8,128)(2,1)S(1)} %bitcast.31), channel_id=1, replica_groups=mesh['dp'=16,'chan'=2] {'dp'}, dimensions={0} | all-to-all | bytes 2097152 | tf_op jit(solution)/shard_map/all_to_all | solution.py:895
  106.3 0.1 reduce_sum.12
  106.4 1.2 broadcast_in_dim.2
  107.6 0.0 copy-start.13
  107.6 0.0 copy-start.14
  107.7 0.0 copy-start.32
  107.7 0.0 copy-start.38
  107.7 0.0 copy-start.39
  107.7 4.1 %all-to-all-start.1 = ((bf16[16,256,128]{2,1,0:T(8,128)(2,1)}), bf16[16,256,128]{2,1,0:T(8,128)(2,1)S(1)}, u32[]{:S(2)}, u32[]{:S(2)}) async-start(bf16[16,256,128]{2,1,0:T(8,128)(2,1)} %broadcast_in_dim.2), calls=%async_computation.1 | async-start | bytes 2097152 | tf_op jit(solution)/shard_map/all_to_all | solution.py:898
  111.9 0.1 collective-permute-start.6
  111.9 0.5 collective-permute-start.2
  112.4 0.1 collective-permute-start.4
  112.5 0.6 collective-permute-done.6
  113.1 0.1 maximum_select_fusion
  113.2 22.4 %all-to-all-done.1 = bf16[16,256,128]{2,1,0:T(8,128)(2,1)S(1)} async-done(((bf16[16,256,128]{2,1,0:T(8,128)(2,1)}), bf16[16,256,128]{2,1,0:T(8,128)(2,1)S(1)}, u32[]{:S(2)}, u32[]{:S(2)}) %all-to-all-start.1) | async-done | bytes 1048608 | tf_op jit(solution)/shard_map/all_to_all | solution.py:898
  135.6 0.0 copy-start.9
  135.6 1.3 copy-done.9
  136.9 1.3 copy-done.10
  138.1 1.1 copy-done.15
  139.2 1.1 copy-done.16
  140.3 0.9 copy-done.28
  141.2 0.9 copy-done.29
  142.1 0.9 copy-done.33
  143.0 0.8 copy-done.35
  143.8 0.8 copy-done.36
  144.6 7.5 %shard_map.483 = (f32[384,2,384]{2,1,0:T(2,128)}, f32[384,384]{1,0:T(8,128)}, f32[2,56,384]{2,1,0:T(8,128)}, f32[2,24,384]{2,1,0:T(8,128)}, f32[2,4,384]{2,1,0:T...) custom-call(bf16[4096,128]{1,0:T(8,128)(2,1)S(1)} %bitcast.26, ...), custom_call_target="tpu_custom_call" | custom-call | bytes 8388608 | tf_op jit(solution)/shard_map/pallas_call | solution.py:782
  152.1 0.0 collective-permute-start.5
  152.2 0.0 collective-permute-done.2.out_far
  152.2 2.1 %shard_map.482 = (bf16[192,384]{1,0:T(8,128)(2,1)}, f32[192,384]{1,0:T(8,128)}) custom-call(bf16[384,384]{1,0:T(8,128)(2,1)S(1)} %copy-done.8, bf16[192,384]{1,0:T(8,128)(2,1)S(1)} %bitcast.38, f32[192,384]{1,0:T(8,128)S(1)} %copy-done.25, f32[192,384]{1,0:T(8,128)} %collective-permute-done.2.out_far, f32[200,384]{1,0:T(8,128)S(1)} %copy-done.22, ...), custom_call_target="tpu_custom_call" | custom-call | bytes 8388608 | tf_op jit(solution)/shard_map/pallas_call | solution.py:782
  154.3 4.4 %shard_map.484 = (f32[384,2,384]{2,1,0:T(2,128)}, bf16[384,2,384]{2,1,0:T(2,128)(2,1)}, f32[384,384]{1,0:T(8,128)}, bf16[384,384]{1,0:T(8,128)(2,1)}, f32[2,56,3...) custom-call(f32[16,128]{1,0:T(8,128)S(1)} %get-tuple-element.110.nor, ...), custom_call_target="tpu_custom_call" | custom-call | bytes 8388608 | tf_op jit(solution)/shard_map/pallas_call | solution.py:782
  158.7 0.6 constant_dynamic-slice_fusion.2
  159.3 0.6 dynamic-slice_reduce_fusion
  159.9 0.6 constant_dynamic-slice_fusion
  (59 shorter events, 0.1 us)
Async XLA Ops:
  2.0 1.3 copy-start
  3.3 0.9 copy-start.5
  4.2 1.0 copy-start.7
  5.2 0.8 copy-start.12
  6.0 0.7 copy-start.26
  6.7 8.5 %copy-start.17 = (bf16[384,192]{0,1:T(8,128)(2,1)S(1)}, bf16[384,192]{0,1:T(8,128)(2,1)}, u32[]{:S(2)}) copy-start(bf16[384,192]{0,1:T(8,128)(2,1)} %param.25) | copy-start | bytes 442372
  12.2 1.0 copy-start.3
  13.2 0.8 copy-start.19
  14.0 0.7 copy-start.20
  14.8 1.8 %copy-start.31 = (f32[112,384]{1,0:T(8,128)}, f32[112,384]{1,0:T(8,128)S(1)}, u32[]{:S(2)}) copy-start(f32[112,384]{1,0:T(8,128)S(1)} %get-tuple-element.90.own_part) | copy-start | bytes 516100
  14.8 1.8 %collective-permute-start = (f32[112,384]{1,0:T(8,128)S(1)}, f32[112,384]{1,0:T(8,128)S(1)}, u32[]{:S(2)}, u32[]{:S(2)}) collective-permute-start(f32[112,384]{1,0:T(8,128)S(1)} %get-tuple-element.90.own_part), channel_id=1, source_target_pairs={{0,1},{1,0},{2,3},{3,2},{4,5},{5,4},{6,7},{7,6},{8,9},{9,8},{10,11... | collective-permute-start | bytes 516104 | tf_op jit(solution)/shard_map/ppermute | solution.py:812
  15.2 1.4 collective-permute-start.1
  16.6 0.7 copy-start.42
  16.6 0.7 copy-start.41
  17.3 39.4 %copy-start.4 = (f32[2,384,384]{2,1,0:T(8,128)S(1)}, f32[2,384,384]{2,1,0:T(8,128)}, u32[]{:S(2)}) copy-start(f32[2,384,384]{2,1,0:T(8,128)} %copy-done.3) | copy-start | bytes 3538948
  17.3 39.4 %copy-start.6 = (f32[2,384,56]{1,2,0:T(8,128)S(1)}, f32[2,384,56]{1,2,0:T(8,128)}, u32[]{:S(2)}) copy-start(f32[2,384,56]{1,2,0:T(8,128)} %param.30) | copy-start | bytes 516100
  17.3 39.4 %copy-start.8 = (bf16[384,384]{1,0:T(8,128)(2,1)S(1)}, bf16[384,384]{1,0:T(8,128)(2,1)}, u32[]{:S(2)}) copy-start(bf16[384,384]{1,0:T(8,128)(2,1)} %hid.5) | copy-start | bytes 884740
  17.3 39.4 %copy-start.27 = (f32[2,4,384]{2,1,0:T(4,128)S(1)}, f32[2,4,384]{2,1,0:T(4,128)}, u32[]{:S(2)}) copy-start(f32[2,4,384]{2,1,0:T(4,128)} %w_cv.3) | copy-start | bytes 36868
  55.0 1.7 %collective-permute-start.3 = (f32[112,384]{1,0:T(8,128)}, f32[112,384]{1,0:T(8,128)S(1)}, u32[]{:S(2)}, u32[]{:S(2)}) collective-permute-start(f32[112,384]{1,0:T(8,128)} %get-tuple-element.96.own_part), channel_id=1, source_target_pairs={{0,1},{1,0},{2,3},{3,2},{4,5},{5,4},{6,7},{7,6},{8,9},{9,8},{10,11... | collective-permute-start | bytes 516104 | tf_op jit(solution)/shard_map/ppermute | solution.py:812
  56.7 1.3 copy-start.11
  58.0 1.0 copy-start.23
  59.0 1.0 copy-start.24
  59.9 0.9 copy-start.30
  60.8 0.9 copy-start.34
  61.7 0.8 copy-start.37
  70.3 0.7 copy-start.21
  71.0 0.7 copy-start.40
  107.6 4.2 %copy-start.43 = (f32[192]{0:T(256)S(1)}, f32[192]{0:T(256)}, u32[]{:S(2)}) copy-start(f32[192]{0:T(256)} %param.41) | copy-start | bytes 2308
  107.6 4.2 %copy-start.44 = (f32[192]{0:T(256)S(1)}, f32[192]{0:T(256)}, u32[]{:S(2)}) copy-start(f32[192]{0:T(256)} %param.34) | copy-start | bytes 2308
  107.6 27.9 %copy-start.1 = (f32[384,2,384]{2,1,0:T(2,128)S(1)}, f32[384,2,384]{2,1,0:T(2,128)}, u32[]{:S(2)}) copy-start(f32[384,2,384]{2,1,0:T(2,128)} %w_in.5) | copy-start | bytes 3538948
  107.6 27.9 %copy-start.2 = (f32[384,384]{1,0:T(8,128)S(1)}, f32[384,384]{1,0:T(8,128)}, u32[]{:S(2)}) copy-start(f32[384,384]{1,0:T(8,128)} %w_out.5) | copy-start | bytes 1769476
  107.6 27.9 %copy-start.13 = (f32[2,19,384]{2,0,1:T(2,128)S(1)}, f32[2,19,384]{2,0,1:T(2,128)}, u32[]{:S(2)}) copy-start(f32[2,19,384]{2,0,1:T(2,128)} %param.33) | copy-start | bytes 175108
  107.6 27.9 %copy-start.14 = (f32[2,24,384]{2,1,0:T(8,128)S(1)}, f32[2,24,384]{2,1,0:T(8,128)}, u32[]{:S(2)}) copy-start(f32[2,24,384]{2,1,0:T(8,128)} %w_dt.5) | copy-start | bytes 221188
  107.7 27.9 %copy-start.32 = (f32[2,24,384]{2,1,0:T(8,128)S(1)}, f32[2,24,384]{2,1,0:T(8,128)}, u32[]{:S(2)}) copy-start(f32[2,24,384]{2,1,0:T(8,128)} %a_dt.1) | copy-start | bytes 221188
  107.7 27.9 %copy-start.38 = (f32[2,4,384]{2,1,0:T(4,128)S(1)}, f32[2,4,384]{2,1,0:T(4,128)}, u32[]{:S(2)}) copy-start(f32[2,4,384]{2,1,0:T(4,128)} %a_cv.1) | copy-start | bytes 36868
  107.7 27.9 %copy-start.39 = (f32[2,4,384]{2,1,0:T(4,128)S(1)}, f32[2,4,384]{2,1,0:T(4,128)}, u32[]{:S(2)}) copy-start(f32[2,4,384]{2,1,0:T(4,128)} %b_cv.1) | copy-start | bytes 36868
  107.7 27.9 %all-to-all-start.1 = ((bf16[16,256,128]{2,1,0:T(8,128)(2,1)}), bf16[16,256,128]{2,1,0:T(8,128)(2,1)S(1)}, u32[]{:S(2)}, u32[]{:S(2)}) async-start(bf16[16,256,128]{2,1,0:T(8,128)(2,1)} %broadcast_in_dim.2), calls=%async_computation.1 | async-start | bytes 2097152 | tf_op jit(solution)/shard_map/all_to_all | solution.py:898
  111.9 1.2 collective-permute-start.6
  111.9 40.2 %collective-permute-start.2 = (f32[192,384]{1,0:T(8,128)}, f32[192,384]{1,0:T(8,128)}, u32[]{:S(2)}, u32[]{:S(2)}) collective-permute-start(f32[192,384]{1,0:T(8,128)} %get-tuple-element.95), channel_id=1, source_target_pairs={{0,1},{1,0},{2,3},{3,2},{4,5},{5,4},{6,7},{7,6},{8,9},{9,8},{10,11... | collective-permute-start | bytes 884744 | tf_op jit(solution)/shard_map/ppermute | solution.py:812
  112.4 39.7 %collective-permute-start.4 = (f32[200,384]{1,0:T(8,128)}, f32[200,384]{1,0:T(8,128)}, u32[]{:S(2)}, u32[]{:S(2)}) collective-permute-start(f32[200,384]{1,0:T(8,128)} %copy-done.40), channel_id=1, source_target_pairs={{0,1},{1,0},{2,3},{3,2},{4,5},{5,4},{6,7},{7,6},{8,9},{9,8},{10,11... | collective-permute-start | bytes 921608 | tf_op jit(solution)/shard_map/ppermute | solution.py:812
  135.6 1.3 copy-start.9
  136.9 1.3 copy-start.10
  138.1 1.1 copy-start.15
  139.2 1.1 copy-start.16
  140.3 0.9 copy-start.28
  141.2 0.9 copy-start.29
  142.1 0.9 copy-start.33
  143.0 0.8 copy-start.35
  143.8 0.8 copy-start.36
  144.6 7.6 %copy-start.18 = (bf16[384,192]{0,1:T(8,128)(2,1)S(1)}, bf16[384,192]{0,1:T(8,128)(2,1)}, u32[]{:S(2)}) copy-start(bf16[384,192]{0,1:T(8,128)(2,1)} %param.25) | copy-start | bytes 442372
  144.6 7.6 %copy-start.22 = (f32[200,384]{1,0:T(8,128)S(1)}, f32[200,384]{1,0:T(8,128)}, u32[]{:S(2)}) copy-start(f32[200,384]{1,0:T(8,128)} %copy-done.21) | copy-start | bytes 921604
  144.6 7.6 %copy-start.25 = (f32[192,384]{1,0:T(8,128)S(1)}, f32[192,384]{1,0:T(8,128)}, u32[]{:S(2)}) copy-start(f32[192,384]{1,0:T(8,128)} %get-tuple-element.94.out_own) | copy-start | bytes 884740
  152.1 2.1 %collective-permute-start.5 = (f32[16,128]{1,0:T(8,128)S(1)}, f32[16,128]{1,0:T(8,128)S(1)}, u32[]{:S(2)}, u32[]{:S(2)}) collective-permute-start(f32[16,128]{1,0:T(8,128)S(1)} %get-tuple-element.110.norms_own), channel_id=1, source_target_pairs={{0,1},{1,0},{2,3},{3,2},{4,5},{5,4},{6,7},{7,6},{8,9},{9,8},{10,11... | collective-permute-start | bytes 24584 | tf_op jit(solution)/shard_map/ppermute | solution.py:812

commit v2 on v1

v2 whole, which is shorter than its diff:
```python
import functools

import jax
import jax.numpy as jnp
from jax import lax
from jax.experimental import pallas as pl
from jax.experimental.pallas import tpu as pltpu
from jax.sharding import PartitionSpec as P

STEP = 4
norm_eps = 1e-06
beta_one = 0.5
beta_two = 0.5
adam_eps = 1e-06
decay_rate = 0.01
learn_rate = 0.3
LOG2E = 1.4426950408889634
FAR = 1e30
FLOOR = -1e-26

f32 = jnp.float32
bf16 = jnp.bfloat16
HIGH = lax.Precision.HIGHEST
LANES = 128
ROWS = 16
MB = 1 << 20


def dot(left, right, dims, precision=None):
    return lax.dot_general(
        left, right, (dims, ((), ())), precision=precision, preferred_element_type=f32
    )


NN = ((1,), (0,))
TN = ((0,), (0,))
NT = ((1,), (1,))


def sigmoid(values):
    return lax.logistic(values)


def silu_slope(values, sigma):
    return sigma * (1.0 + values * (1.0 - sigma))


def softplus(values):
    return jnp.maximum(values, 0.0) + jnp.log1p(jnp.exp(-jnp.abs(values)))


def wide(tile, times):
    return jnp.concatenate([tile] * times, axis=1)


def fold(values):
    total = values[0:8]
    for start in range(8, values.shape[0], 8):
        total = total + values[start : start + 8]
    return total


def shape(dims, dtype):
    return jax.ShapeDtypeStruct(dims, dtype)


def each_rows(length, body, carry=None, rows=ROWS):
    def step(index, held):
        return body(pl.multiple_of(index * rows, rows), held)

    return lax.fori_loop(0, length // rows, step, carry)


def spread_segments(numbers, tokens):
    across = lax.broadcasted_iota(jnp.int32, (tokens, tokens), 0)
    along = lax.broadcasted_iota(jnp.int32, (tokens, tokens), 1)
    row = numbers.astype(f32).reshape(1, tokens)
    picked = jnp.where(across == along, row, 0.0).astype(bf16)
    return dot(picked, jnp.ones((tokens, LANES), bf16), NN)


def front_kernel(
    hid, seg, gain, w_in, taps, params, w_xp,
    mix_out, gate_out, conv_out, part_out, norm_out, low_out, same_out,
    padded, sgpad,
    *, need, save,
):
    tokens, width = hid.shape
    chans = mix_out.shape[1]
    tiles = chans // LANES

    need(hid, gain)
    gain_row = gain[...].reshape(1, width)

    def normalise(start, held):
        source = hid[pl.ds(start, ROWS), :].astype(f32)
        scale = lax.rsqrt(jnp.sum(source * source, axis=1, keepdims=True) / width + norm_eps)
        norm_out[pl.ds(start, ROWS), :] = (source * scale * gain_row).astype(bf16)
        return held

    each_rows(tokens, normalise, 0)
    save(norm_out)
    need()
    for half in range(2):
        low_out[half] = w_in[:, half, :].astype(bf16)
    save(low_out)
    normed = norm_out[...]
    mixing = dot(normed, low_out[0], NN)
    mix_out[...] = mixing
    padded[0:8, :] = jnp.zeros((8, chans), f32)
    padded[pl.ds(8, tokens), :] = mixing
    padded[pl.ds(8 + tokens, 8), :] = jnp.zeros((8, chans), f32)
    save(mix_out)
    gate_out[...] = dot(normed, low_out[1], NN)
    save(gate_out)
    numbers = spread_segments(seg[...], tokens)
    sgpad[0:8, :] = jnp.full((8, LANES), -1.0, f32)
    sgpad[pl.ds(8, tokens), :] = numbers
    sgpad[pl.ds(8 + tokens, 8), :] = jnp.full((8, LANES), -1.0, f32)
    width_taps = taps.shape[1]

    def convolve(start, held):
        window = padded[pl.ds(start, ROWS + 16), :]
        marks = sgpad[pl.ds(start, ROWS + 16), :]
        own = marks[8 : 8 + ROWS]
        base = window[8 : 8 + ROWS]
        for heading in range(2):
            total = params[0, heading : heading + 1, :] + taps[heading, 0:1, :] * base
            for offset in range(1, width_taps):
                begin = 8 - offset if heading == 0 else 8 + offset
                same = jnp.where(marks[begin : begin + ROWS] == own, 1.0, 0.0)
                if offset == 1:
                    same_out[heading, pl.ds(start, ROWS), :] = same
                moved = window[begin : begin + ROWS]
                total = total + taps[heading, offset : offset + 1, :] * moved * wide(same, tiles)
            conv_out[heading, pl.ds(start, ROWS), :] = total
        return held

    each_rows(tokens, convolve, 0)
    save(conv_out, same_out)
    for heading in range(2):
        pre = conv_out[heading]
        act_low = (pre * sigmoid(pre)).astype(bf16)
        rows = w_xp.shape[1]
        part_out[heading * rows : (heading + 1) * rows, :] = dot(
            w_xp[heading].astype(bf16), act_low, NT
        )


SPAN = 64


class Sizes:
    def __init__(self, tokens, chans, count, rank):
        self.tokens, self.chans, self.count, self.rank = tokens, chans, count, rank
        self.tiles = chans // LANES
        self.blocks = tokens // LANES
        self.rows = rank + 2 * count
        self.block_rows = LANES * count
        self.pairs = [(heading, tile) for heading in range(2) for tile in range(self.tiles)]

    def base(self, heading, tile):
        return (heading * self.tiles + tile) * self.tokens

    def row(self, ref, heading, tile, at):
        return ref[pl.ds(self.base(heading, tile) + at, 1), :]

    def whole(self, ref, heading):
        starts = [self.base(heading, tile) for tile in range(self.tiles)]
        return jnp.concatenate([ref[start : start + self.tokens, :] for start in starts], axis=1)


def cols(tile):
    return slice(tile * LANES, (tile + 1) * LANES)


def split(values):
    high = values.astype(bf16)
    return high, (values - high.astype(f32)).astype(bf16)


def group_maps(target, tile, heading, count):
    groups = tile.shape[1] // count
    for group in range(groups):
        block, place = divmod(group * count, LANES)
        own = tile[:, cols(block)]
        if place:
            own = pltpu.roll(own, LANES - place, 1)
        target[heading, group] = own


def diagonal_maps(target, tile, heading, count):
    tokens = tile.shape[1]
    squared = count * count
    lane = lax.broadcasted_iota(jnp.int32, (count, squared), 1)
    row = lax.broadcasted_iota(jnp.int32, (count, squared), 0)
    repeat = jnp.where(lane % count == row, 1.0, 0.0).astype(bf16)
    token = lax.broadcasted_iota(jnp.int32, (tokens, squared), 0)
    place = lax.broadcasted_iota(jnp.int32, (tokens, squared), 1)
    mine = place // count == token % count
    for number, part in enumerate(split(tile)):
        spread = jnp.where(mine, dot(part, repeat, TN), 0.0).astype(bf16)
        target[heading, :, number] = spread.reshape(tokens // count, count, squared)


def weigh_states(left, maps):
    half = maps.shape[0] // 2
    got = dot(maps, left, NN)
    return got[:half] + got[half:]


def gather_states(left, right, count):
    products = dot(left, right, NT)
    lane = lax.broadcasted_iota(jnp.int32, (count, count), 1)
    total = products[0:count]
    for place in range(1, count):
        total = jnp.where(lane == place, products[place * count : (place + 1) * count], total)
    return total


def dot3(left, right, dims):
    (left_high, left_low), (right_high, right_low) = split(left), split(right)
    return dot(left_high, right_high, dims) + (
        dot(left_low, right_high, dims) + dot(left_high, right_low, dims)
    )


def scan_kernel(
    own_part, far_part, conv_pre, gate, same, cot_own, cot_far, w_out, w_dt, params, normed, core,
    grad_part, early, out_far, out_own, grad_act, grad_dt, grad_chan, gate_low,
    proj, pre_step, grad_branch, far_step, inflow, grad_y, grad_y_low, result, decayed, branch_low,
    maps, diagonal, gathered, states, low_one, low_two, rates, rates2, inflow_low,
    *, need, save,
):
    tokens, chans = gate.shape
    z = Sizes(tokens, chans, params.shape[0] - 3, w_dt.shape[1])
    count, rank, rows, tiles = z.count, z.rank, z.rows, z.tiles
    half_width = cot_own.shape[0]
    width = 2 * half_width
    me = core[0]
    groups = tokens // count

    proj[...] = own_part[...] + far_part[...]
    need(params, w_dt, w_out, cot_own)
    low_out = w_out[...].astype(bf16)
    low_cot = jnp.where(
        me == 0,
        jnp.concatenate([cot_own[...].astype(f32), cot_far[...].astype(f32)], 0),
        jnp.concatenate([cot_far[...].astype(f32), cot_own[...].astype(f32)], 0),
    ).astype(bf16)
    grad_branch[...] = dot(low_cot, low_out, ((0,), (1,)))
    for heading in range(2):
        for n in range(count):
            value = -jnp.exp(params[3 + n, heading : heading + 1, :])
            rates[heading, n : n + 1, :] = value
            rates2[heading, n : n + 1, :] = jnp.minimum(value * LOG2E, FLOOR)
        pre_step[heading] = (
            dot3(proj[heading * rows : heading * rows + rank, :], w_dt[heading], TN)
            + params[1, heading : heading + 1, :]
        )
        first = heading * rows + rank
        group_maps(maps, proj[first : first + count, :], heading, count)
        diagonal_maps(diagonal, proj[first + count : first + 2 * count, :], heading, count)

    need(conv_pre, gate, same)
    for tile in range(tiles):

        def prepare(start, held, tile=tile):
            here = pl.ds(start, SPAN)
            for heading in range(2):
                pre = conv_pre[heading, here, cols(tile)]
                act = pre * sigmoid(pre)
                size = softplus(pre_step[heading, here, cols(tile)])
                there = pl.ds(z.base(heading, tile) + start, SPAN)
                entering = size * act
                inflow[there, :] = entering
                inflow_low[heading, here, cols(tile)] = entering.astype(bf16)
                far_step[there, :] = jnp.where(same[heading, here, :] > 0.5, size, FAR)
            gated = gate[here, cols(tile)]
            back = grad_branch[here, cols(tile)] * (gated * sigmoid(gated))
            grad_y[pl.ds(z.base(0, tile) + start, SPAN), :] = back
            grad_y_low[here, cols(tile)] = back.astype(bf16)
            return held

        each_rows(tokens, prepare, 0, SPAN)

    blank = jnp.zeros((count, LANES), f32)
    states[0, 0:count, :] = jnp.zeros((count, chans), f32)
    states[1, tokens * count : (tokens + 1) * count, :] = jnp.zeros((count, chans), f32)
    low_one[...] = jnp.zeros(low_one.shape, bf16)
    low_two[...] = jnp.zeros(low_two.shape, bf16)

    def group_of(order, heading):
        return order if heading == 0 else groups - 1 - order

    def run_forward(order, carried, low):
        carried = list(carried)
        enters = [maps[heading, group_of(order, heading)] for heading in range(2)]
        for ahead in range(count):
            for heading in range(2):
                inner = ahead if heading == 0 else count - 1 - ahead
                at = group_of(order, heading) * count + inner
                kept = pl.multiple_of((at + (1 if heading == 0 else 0)) * count, count)
                enter = jnp.broadcast_to(enters[heading][:, inner : inner + 1], (count, LANES))
                for tile in range(tiles):
                    number = heading * tiles + tile
                    decay = jnp.exp2(z.row(far_step, heading, tile, at) * rates2[heading, :, cols(tile)])
                    state = decay * carried[number] + enter * z.row(inflow, heading, tile, at)
                    carried[number] = state
                    states[heading, pl.ds(kept, count), cols(tile)] = state
                    low[heading, inner * count : (inner + 1) * count, cols(tile)] = state.astype(bf16)
        return tuple(carried)

    def rows_of(group):
        return pl.ds(pl.multiple_of(group * count, count), count)

    def post_forward(order, low):
        for heading in range(2):
            group = group_of(order, heading)
            left = low[heading]
            gathered[heading, group] = gather_states(left, grad_y_low[rows_of(group), :], count)
            result[heading, rows_of(group), :] = weigh_states(
                left, diagonal[heading, group].reshape(2 * count, count * count)
            )

    def forward(index, carried):
        order = 2 * index
        post_forward(jnp.maximum(order - 1, 0), low_two.at[0])
        carried = run_forward(order, carried, low_one.at[0])
        post_forward(order, low_one.at[0])
        return run_forward(order + 1, carried, low_two.at[0])

    lax.fori_loop(0, groups // 2, forward, (blank,) * len(z.pairs))
    post_forward(groups - 1, low_two.at[0])

    def store_gathered(target_row, heading):
        for block in range(z.blocks):
            per = LANES // count
            pieces = [gathered[heading, block * per + place] for place in range(per)]
            grad_part[target_row : target_row + count, cols(block)] = jnp.concatenate(pieces, axis=1)

    for heading in range(2):
        first = heading * rows + rank
        store_gathered(first + count, heading)
        group_maps(maps, proj[first + count : first + 2 * count, :], heading, count)
        diagonal_maps(diagonal, proj[first : first + count, :], heading, count)

    for tile in range(tiles):

        def finish(start, held, tile=tile):
            here = pl.ds(start, SPAN)
            total = jnp.zeros((SPAN, LANES), f32)
            sums = []
            back = grad_y[pl.ds(z.base(0, tile) + start, SPAN), :]
            for heading in range(2):
                pre = conv_pre[heading, here, cols(tile)]
                act = pre * sigmoid(pre)
                total = total + result[heading, here, cols(tile)]
                total = total + params[2, heading : heading + 1, cols(tile)] * act
                sums.append(held[heading] + fold(back * act))
            gated = gate[here, cols(tile)]
            sigma = sigmoid(gated)
            branch_low[here, cols(tile)] = (total * (gated * sigma)).astype(bf16)
            gate_low[here, cols(tile)] = (
                grad_branch[here, cols(tile)] * total * silu_slope(gated, sigma)
            ).astype(bf16)
            return tuple(sums)

        skips = each_rows(tokens, finish, (jnp.zeros((8, LANES), f32),) * 2, SPAN)
        for heading in range(2):
            grad_chan[2, heading : heading + 1, cols(tile)] = jnp.sum(
                skips[heading], axis=0, keepdims=True
            )
    save(gate_low)
    need(normed)
    branch = branch_low[...]
    grad_w = dot(branch, low_cot, ((0,), (1,))).astype(bf16)
    for tile in range(width // LANES):
        early[tile * chans : (tile + 1) * chans, :] = grad_w[:, cols(tile)]
    base_row = chans * (width // LANES)
    grad_w = dot(normed[...], gate_low[...], TN).astype(bf16)
    for tile in range(tiles):
        early[base_row + tile * width : base_row + (tile + 1) * width, :] = grad_w[:, cols(tile)]
    base_row += tiles * width
    if early.shape[0] > base_row:
        early[base_row:, :] = jnp.zeros((early.shape[0] - base_row, LANES), bf16)
    sent = dot(low_out, branch, ((0,), (1,)))
    out_own[...] = jnp.where(me == 0, sent[:half_width], sent[half_width:])
    out_far[...] = jnp.where(me == 0, sent[half_width:], sent[:half_width])
    save(out_own)

    def run_backward(order, held, low, products):
        waiting = list(held[: len(z.pairs)])
        totals = list(held[len(z.pairs) :])
        leaves = [maps[heading, group_of(order, 1 - heading)] for heading in range(2)]
        for ahead in range(count):
            for heading in range(2):
                inner = ahead if heading == 1 else count - 1 - ahead
                at = group_of(order, 1 - heading) * count + inner
                prior = pl.multiple_of((at + (0 if heading == 0 else 1)) * count, count)
                leave = jnp.broadcast_to(leaves[heading][:, inner : inner + 1], (count, LANES))
                here = slice(inner * count, (inner + 1) * count)
                for tile in range(tiles):
                    number = heading * tiles + tile
                    size = z.row(far_step, heading, tile, at)
                    decay = jnp.exp2(size * rates2[heading, :, cols(tile)])
                    grad = leave * z.row(grad_y, 0, tile, at) + waiting[number]
                    lead = decay * grad
                    waiting[number] = lead
                    slope = lead * states[heading, pl.ds(prior, count), cols(tile)]
                    totals[number] = totals[number] + slope * size
                    products[heading, here, cols(tile)] = (slope * rates[heading, :, cols(tile)]).astype(bf16)
                    low[heading, here, cols(tile)] = grad.astype(bf16)
        return tuple(waiting + totals)

    lane = lax.broadcasted_iota(jnp.int32, (count, count * count), 1)
    row = lax.broadcasted_iota(jnp.int32, (count, count * count), 0)
    ones = jnp.where(lane // count == row, 1.0, 0.0).astype(bf16)

    def post_backward(order, low, products):
        for heading in range(2):
            group = group_of(order, 1 - heading)
            left = low[heading]
            gathered[heading, group] = gather_states(left, inflow_low[heading, rows_of(group), :], count)
            result[heading, rows_of(group), :] = weigh_states(
                left, diagonal[heading, group].reshape(2 * count, count * count)
            )
            decayed[heading, rows_of(group), :] = dot(ones, products[heading], NN)

    def backward(index, held):
        order = 2 * index
        post_backward(jnp.maximum(order - 1, 0), low_two.at[0], low_two.at[1])
        held = run_backward(order, held, low_one.at[0], low_one.at[1])
        post_backward(order, low_one.at[0], low_one.at[1])
        return run_backward(order + 1, held, low_two.at[0], low_two.at[1])

    held = lax.fori_loop(0, groups // 2, backward, (blank,) * (2 * len(z.pairs)))
    post_backward(groups - 1, low_two.at[0], low_two.at[1])
    for number, (heading, tile) in enumerate(z.pairs):
        slopes = held[len(z.pairs) + number] * rates[heading, :, cols(tile)]
        for n in range(count):
            grad_chan[3 + n, heading : heading + 1, cols(tile)] = slopes[n : n + 1]
    for heading in range(2):
        store_gathered(heading * rows + rank, heading)

    for tile in range(tiles):

        def close(start, held, tile=tile):
            here = pl.ds(start, SPAN)
            sums = []
            back = grad_y[pl.ds(z.base(0, tile) + start, SPAN), :]
            for heading in range(2):
                pre = conv_pre[heading, here, cols(tile)]
                act = pre * sigmoid(pre)
                passed = result[heading, here, cols(tile)]
                reach = pre_step[heading, here, cols(tile)]
                grad_act[heading, here, cols(tile)] = (
                    passed * softplus(reach) + back * params[2, heading : heading + 1, cols(tile)]
                )
                grad_pre = (decayed[heading, here, cols(tile)] + passed * act) * sigmoid(reach)
                pre_step[heading, here, cols(tile)] = grad_pre
                sums.append(held[heading] + fold(grad_pre))
            return tuple(sums)

        biases = each_rows(tokens, close, (jnp.zeros((8, LANES), f32),) * 2, SPAN)
        for heading in range(2):
            grad_chan[1, heading : heading + 1, cols(tile)] = jnp.sum(
                biases[heading], axis=0, keepdims=True
            )
    save(grad_act)
    for heading in range(2):
        grad_chan[0, heading : heading + 1, :] = jnp.zeros((1, chans), f32)
        grad_pre = pre_step[heading]
        grad_part[heading * rows : heading * rows + rank, :] = dot3(w_dt[heading], grad_pre, NT)
        grad_dt[heading] = dot3(proj[heading * rows : heading * rows + rank, :], grad_pre, NN)


def scan_call(args, sizes, early_rows, half_width, limit=52):
    z = sizes
    square = (z.tokens, z.chans)
    both = (2,) + square
    flat = pltpu.VMEM((2 * z.tiles * z.tokens, LANES), f32)
    groups = z.tokens // z.count
    squared = z.count * z.count
    return call(
        scan_kernel,
        at(
            "x", shape((2 * z.rows, z.tokens), f32), shape((early_rows, LANES), bf16),
            shape((half_width, z.tokens), f32),
        )
        + at(
            "h", shape((half_width, z.tokens), f32), shape(both, f32), shape((2, z.rank, z.chans), f32),
            shape((3 + z.count, 2, z.chans), f32), shape(square, bf16),
        ),
        args,
        [
            pltpu.VMEM((2 * z.rows, z.tokens), f32), pltpu.VMEM(both, f32), pltpu.VMEM(square, f32),
            flat, flat, pltpu.VMEM((z.tiles * z.tokens, LANES), f32), pltpu.VMEM(square, bf16),
            pltpu.VMEM(both, f32), pltpu.VMEM(both, f32), pltpu.VMEM(square, bf16),
            pltpu.VMEM((2, groups, z.count, LANES), f32),
            pltpu.VMEM((2, groups, 2, z.count, squared), bf16),
            pltpu.VMEM((2, groups, z.count, z.count), f32),
            pltpu.VMEM((2, (z.tokens + 1) * z.count, z.chans), f32),
            pltpu.VMEM((2, 2, squared, z.chans), bf16), pltpu.VMEM((2, 2, squared, z.chans), bf16),
            pltpu.VMEM((2, z.count, z.chans), f32), pltpu.VMEM((2, z.count, z.chans), f32),
            pltpu.VMEM(both, bf16),
        ],
        limit=limit, micros=30,
    )


def back_kernel(
    own_part, far_part, grad_act, conv_pre, mixing, gate_low, normed, low_in, seg, w_xp, taps, hid, gain,
    grad_dt, grad_chan, core,
    sums_out, in_own, in_far,
    padded, gpad, sgpad, mixed_low, small, act_low,
    *, need, save,
):
    tokens, width = hid.shape
    chans = mixing.shape[1]
    tiles = chans // LANES
    rows = w_xp.shape[1]
    width_taps = taps.shape[1]
    me = core[0]
    half_width = in_own.shape[0] - 8
    edge = jnp.zeros((8, chans), f32)
    padded[0:8, :] = edge
    padded[pl.ds(8 + tokens, 8), :] = edge
    gpad[0, 0:8, :] = edge
    gpad[1, 0:8, :] = edge
    gpad[0, pl.ds(8 + tokens, 8), :] = edge
    gpad[1, pl.ds(8 + tokens, 8), :] = edge
    sgpad[0:8, :] = jnp.full((8, LANES), -1.0, f32)
    sgpad[pl.ds(8 + tokens, 8), :] = jnp.full((8, LANES), -1.0, f32)
    need(seg, w_xp, mixing)
    padded[pl.ds(8, tokens), :] = mixing[...]
    sgpad[pl.ds(8, tokens), :] = spread_segments(seg[...], tokens)

    parts = (own_part[...] + far_part[...]).astype(bf16)
    for heading in range(2):
        part = parts[heading * rows : (heading + 1) * rows, :]
        gpad[heading, pl.ds(8, tokens), :] = dot(part, w_xp[heading].astype(bf16), TN)

    blank = jnp.zeros((8, chans), f32)
    need()

    def through_conv(start, held):
        here = pl.ds(start, ROWS)
        window = padded[pl.ds(start, ROWS + 16), :]
        marks = sgpad[pl.ds(start, ROWS + 16), :]
        own = marks[8 : 8 + ROWS]
        base = window[8 : 8 + ROWS]
        sums = []
        for heading in range(2):
            pre = conv_pre[heading, here, :]
            sigma = sigmoid(pre)
            act_low[heading, here, :] = (pre * sigma).astype(bf16)
            inside = pl.ds(pl.multiple_of(start + 8, 8), ROWS)
            grad = (gpad[heading, inside, :] + grad_act[heading, here, :]) * silu_slope(pre, sigma)
            gpad[heading, inside, :] = grad
            sums.append(held[5 * heading] + fold(grad))
            sums.append(held[5 * heading + 1] + fold(grad * base))
            for offset in range(1, width_taps):
                begin = 8 - offset if heading == 0 else 8 + offset
                kept = jnp.where(marks[begin : begin + ROWS] == own, 1.0, 0.0)
                moved = window[begin : begin + ROWS]
                sums.append(held[5 * heading + 1 + offset] + fold(grad * moved * wide(kept, tiles)))
        return tuple(sums)

    sums = each_rows(tokens, through_conv, (blank,) * 10)
    small[...] = jnp.zeros(small.shape, f32)
    for heading in range(2):
        bias = jnp.sum(sums[5 * heading], axis=0, keepdims=True)
        for offset in range(width_taps):
            row = heading * width_taps + offset
            small[row : row + 1, :] = jnp.sum(sums[5 * heading + 1 + offset], axis=0, keepdims=True)
        for entry in range(grad_chan.shape[0]):
            row = 2 * width_taps + 2 * entry + heading
            small[row : row + 1, :] = (
                bias
                if entry == 0
                else grad_chan[entry, heading : heading + 1, :]
            )

    def mixed(start, held):
        here = pl.ds(start, ROWS)
        marks = sgpad[pl.ds(start, ROWS + 16), :]
        own = marks[8 : 8 + ROWS]
        total = jnp.zeros((ROWS, chans), f32)
        for heading in range(2):
            window = gpad[heading, pl.ds(start, ROWS + 16), :]
            total = total + window[8 : 8 + ROWS] * taps[heading, 0:1, :]
            for offset in range(1, width_taps):
                begin = 8 + offset if heading == 0 else 8 - offset
                kept = jnp.where(marks[begin : begin + ROWS] == own, 1.0, 0.0)
                total = total + window[begin : begin + ROWS] * wide(kept, tiles) * taps[
                    heading, offset : offset + 1, :
                ]
        mixed_low[here, :] = total.astype(bf16)
        return held

    each_rows(tokens, mixed, 0)

    base_row = 0

    def put(values):
        nonlocal base_row
        for tile in range(values.shape[1] // LANES):
            sums_out[base_row : base_row + values.shape[0], :] = values[
                :, tile * LANES : (tile + 1) * LANES
            ].astype(bf16)
            base_row += values.shape[0]

    put(dot(normed[...], mixed_low[...], TN))
    put(
        jnp.concatenate(
            [
                dot(parts[heading * rows : (heading + 1) * rows, :], act_low[heading], NN)
                for heading in range(2)
            ],
            axis=0,
        )
    )
    put(jnp.concatenate([grad_dt[0], grad_dt[1]], axis=0))

    partial = dot(mixed_low[...], low_in[0], NT) + dot(gate_low[...], low_in[1], NT)
    padded[pl.ds(8, tokens), :] = partial

    gain_row = gain[...].reshape(1, width)

    def gains(start, held):
        here = pl.ds(start, ROWS)
        source = hid[here, :].astype(f32)
        scale = lax.rsqrt(jnp.sum(source * source, axis=1, keepdims=True) / width + norm_eps)
        inside = pl.ds(pl.multiple_of(start + 8, 8), ROWS)
        grad = padded[inside, :]
        padded[inside, :] = grad * gain_row
        return held + fold(grad * source * scale)

    gain_sum = each_rows(tokens, gains, jnp.zeros((8, width), f32))
    small[46:47, :] = jnp.sum(gain_sum, axis=0, keepdims=True)
    put(small[...])
    sums_out[base_row:, :] = jnp.zeros((sums_out.shape[0] - base_row, LANES), bf16)

    weighted = padded[pl.ds(8, tokens), :]
    products = weighted * hid[...].astype(f32)
    turned = weighted.T
    row_dot = dot(jnp.ones((8, width), f32), products, NT, HIGH)
    in_own[0:half_width, :] = jnp.where(me == 0, turned[:half_width], turned[half_width:])
    in_far[0:half_width, :] = jnp.where(me == 0, turned[half_width:], turned[:half_width])
    in_own[pl.ds(half_width, 8), :] = row_dot
    in_far[pl.ds(half_width, 8), :] = row_dot


def outputs_kernel(hid, cot_own, out_own, out_far, in_own, in_far, core, output, input_grad, *, need, save):
    width = hid.shape[1]
    half_width = cot_own.shape[0]
    me = core[0]
    need()
    source = hid[...].astype(f32).T
    scale = lax.rsqrt(jnp.sum(source * source, axis=0, keepdims=True) / width + norm_eps)
    own = jnp.where(me == 0, source[:half_width], source[half_width:])
    output[...] = (own + (out_own[...] + out_far[...])).astype(bf16)
    weighted = in_own[0:half_width, :] + in_far[0:half_width, :]
    save(output)
    row_dot = in_own[half_width : half_width + 1, :] + in_far[half_width : half_width + 1, :]
    input_grad[...] = (
        cot_own[...].astype(f32)
        + scale * weighted
        - own * (scale * scale * scale) * (row_dot / width)
    )


def lamb_moments(weight, grad, first, second):
    first_new = beta_one * first + (1.0 - beta_one) * grad
    second_new = beta_two * second + (1.0 - beta_two) * grad * grad
    update = (
        first_new
        / (1.0 - beta_one**STEP)
        / (jnp.sqrt(second_new / (1.0 - beta_two**STEP)) + adam_eps)
        + decay_rate * weight
    )
    return (first_new, second_new, update)


def rows_sum(values):
    return jnp.sum(values, axis=0, keepdims=True)


def lanes_sum(values):
    total = rows_sum(values)
    lanes = total[:, 0:LANES]
    for tile in range(1, values.shape[1] // LANES):
        lanes = lanes + total[:, cols(tile)]
    return lanes


def fetch(sums, base, stride, start, count, number):
    return jnp.concatenate(
        [sums[pl.ds(base + tile * stride + start, count), :].astype(f32) for tile in range(number)], axis=1
    )


def spread_of(update, mean, length):
    def step(start, kept):
        away = update[pl.ds(start, ROWS), :] - mean
        return kept + fold(away * away)

    return rows_sum(each_rows(length, step, jnp.zeros((8, update.shape[1]), f32)))


def half_update(half, sums, base, stride, weights, a_ref, b_ref, x_ref, y_ref, u_ref):
    length, _, chans = weights.shape
    zero = jnp.zeros((8, chans), f32)

    def step(start, kept):
        here = pl.ds(start, ROWS)
        grad = fetch(sums, base, stride, start, ROWS, chans // LANES)
        weight = weights[here, half, :]
        first, second, update = lamb_moments(weight, grad, a_ref[here, half, :], b_ref[here, half, :])
        x_ref[here, :] = first
        y_ref[here, :] = second
        u_ref[here, :] = update
        return (
            kept[0] + fold(weight * weight), kept[1] + fold(update * update), kept[2] + fold(update)
        )

    return each_rows(length, step, (zero, zero, zero))


def early_kernel(
    sums, w_in, a_in, b_in, w_out, a_out, b_out,
    x_out, y_out, x_gate, y_gate, u_gate, u_out, norms, stats,
    *, need, save,
):
    width, _, chans = w_in.shape
    tiles = width // LANES
    norms[...] = jnp.zeros(norms.shape, f32)
    zero = jnp.zeros((8, width), f32)
    need(w_out, a_out, b_out)

    def one_out(start, kept):
        here = pl.ds(start, ROWS)
        grad = fetch(sums, 0, chans, start, ROWS, tiles)
        weight = w_out[here, :]
        first, second, update = lamb_moments(weight, grad, a_out[here, :], b_out[here, :])
        x_out[here, :] = first
        y_out[here, :] = second
        u_out[here, :] = update
        return (kept[0] + fold(weight * weight), kept[1] + fold(update * update))

    weight_sq, update_sq = each_rows(chans, one_out, (zero, zero))
    norms[1:2, :] = lanes_sum(weight_sq)
    norms[7:8, :] = lanes_sum(update_sq)
    save(x_out, y_out, u_out)
    need()
    weight_sq, update_sq, total = half_update(
        1, sums, chans * tiles, width, w_in, a_in, b_in, x_gate, y_gate, u_gate
    )
    norms[0:1, :] = lanes_sum(weight_sq)
    norms[6:7, :] = lanes_sum(update_sq)
    save(x_gate, y_gate, u_gate)
    gate_mean = rows_sum(total) / width
    stats[0:1, :] = gate_mean
    stats[1:2, :] = spread_of(u_gate, gate_mean, width)
    ones = jnp.ones((8, width), f32)
    out_all = u_out[...]
    out_mean = jnp.sum(out_all, axis=1, keepdims=True) / width
    away = out_all - out_mean
    stats[2:3, :] = dot(ones, out_all, NT, HIGH)[0:1] / width
    stats[3:4, :] = dot(ones, away * away, NT, HIGH)[0:1]
    stats[4:8, :] = jnp.zeros((4, chans), f32)


def late_kernel(
    sums, x_gate, y_gate, early_norms, early_stats,
    w_in, a_in, b_in, w_xp, a_xp, b_xp, w_dt, a_dt, b_dt, w_cv, a_cv, b_cv, w_cp, a_cp, b_cp,
    x_in, y_in, x_xp, y_xp, x_dt, y_dt, x_cv, y_cv, x_cp, y_cp,
    u_mix, u_xp, u_dt, u_cv, u_cp, norms, stats,
    x_mix, y_mix,
    *, need, save,
):
    width, _, chans = w_in.shape
    tiles = chans // LANES
    need(early_norms, early_stats, w_in, a_in, b_in)
    norms[...] = early_norms[...]
    stats[...] = early_stats[...]
    weight_sq, update_sq, total = half_update(
        0, sums, 0, width, w_in, a_in, b_in, x_mix, y_mix, u_mix
    )
    save(u_mix)
    need()
    x_in[:, 0, :] = x_mix[...]
    x_in[:, 1, :] = x_gate[...]
    y_in[:, 0, :] = y_mix[...]
    y_in[:, 1, :] = y_gate[...]
    save(x_in, y_in)
    norms[0:1, :] += lanes_sum(weight_sq)
    norms[6:7, :] += lanes_sum(update_sq)
    mix_mean = rows_sum(total) / width
    stats[4:5, :] = mix_mean
    stats[5:6, :] = spread_of(u_mix, mix_mean, width)
    base = tiles * width

    def small(place, items, weight, a_ref, b_ref, x_ref, y_ref, u_ref):
        weight_sq, update_sq = jnp.zeros((1, LANES), f32), jnp.zeros((1, LANES), f32)
        for index, grad in enumerate(items):
            held = weight[index]
            first, second, update = lamb_moments(held, grad, a_ref[index], b_ref[index])
            x_ref[index] = first
            y_ref[index] = second
            u_ref[index] = update
            weight_sq = weight_sq + lanes_sum(held * held)
            update_sq = update_sq + lanes_sum(update * update)
        norms[place : place + 1, :] = weight_sq
        norms[6 + place : 7 + place, :] = update_sq

    rows = w_xp.shape[1]
    grads = fetch(sums, base, 2 * rows, 0, 2 * rows, tiles)
    small(2, [grads[:rows], grads[rows:]], w_xp, a_xp, b_xp, x_xp, y_xp, u_xp)
    base += 2 * rows * tiles
    rank = w_dt.shape[1]
    grads = fetch(sums, base, 2 * rank, 0, 2 * rank, tiles)
    small(3, [grads[:rank], grads[rank:]], w_dt, a_dt, b_dt, x_dt, y_dt, u_dt)
    base += 2 * rank * tiles
    grads = fetch(sums, base, 48, 0, 48, tiles)
    taps = w_cv.shape[1]
    small(4, [grads[:taps], grads[taps : 2 * taps]], w_cv, a_cv, b_cv, x_cv, y_cv, u_cv)
    entries = w_cp.shape[0]
    items = [grads[2 * (taps + entry) : 2 * (taps + entry) + 2] for entry in range(entries)]
    small(5, items, w_cp, a_cp, b_cp, x_cp, y_cp, u_cp)
    for tile in range(tiles):
        norms[12 + tile : 13 + tile, :] = grads[46:47, cols(tile)]


def apply_kernel(
    norms_own, norms_far, stats,
    w_in, w_out, w_xp, w_dt, w_cv, w_cp,
    u_mix, u_gate, u_out, u_xp, u_dt, u_cv, u_cp,
    gain, gain_first, gain_second, core,
    n_in, c_in, n_out, c_out, n_xp, c_xp, n_dt, c_dt, n_cv, c_cv, n_cp, c_cp,
    g_first, g_second, g_new, g_copy, norms_out, stats_out,
    *, need, save,
):
    width, _, chans = w_in.shape
    half_width = g_new.shape[0]
    me = core[0]
    need(norms_own, gain, stats)
    totals = norms_own[...] + norms_far[...]
    gain_grad = jnp.concatenate(
        [totals[12 + tile : 13 + tile, :] for tile in range(width // LANES)], axis=1
    )
    gain_row = gain[...].reshape(1, width)
    first, second, update = lamb_moments(gain_row, gain_grad, gain_first[...], gain_second[...])
    sums = jnp.sum(totals, axis=1, keepdims=True)
    weight_sq = [jnp.sum(gain_row * gain_row, axis=1, keepdims=True)] + [
        sums[place : place + 1] for place in range(6)
    ]
    update_sq = [jnp.sum(update * update, axis=1, keepdims=True)] + [
        sums[6 + place : 7 + place] for place in range(6)
    ]
    scales = []
    for place in range(7):
        weight_norm = jnp.sqrt(weight_sq[place])
        update_norm = jnp.sqrt(update_sq[place])
        scales.append(learn_rate * weight_norm / (update_norm + adam_eps))
        norms_out[0:1, place : place + 1] = weight_norm
        norms_out[1:2, place : place + 1] = update_norm
    fresh = gain_row - scales[0] * update

    def own(row):
        return jnp.where(me == 0, row[:, :half_width], row[:, half_width:]).reshape(half_width)

    g_first[...] = own(first)
    g_second[...] = own(second)
    g_new[...] = own(fresh)
    g_copy[...] = own(fresh).astype(bf16)

    need(w_in, u_mix, u_gate)

    def one_in(start, held):
        here = pl.ds(start, ROWS)
        for half, change in ((0, u_mix), (1, u_gate)):
            fresh = w_in[here, half, :] - scales[1] * change[here, :]
            n_in[here, half, :] = fresh
            c_in[here, half, :] = fresh.astype(bf16)
        return held

    each_rows(width, one_in, 0)
    save(n_in, c_in)
    need()

    def one_out(start, held):
        here = pl.ds(start, ROWS)
        fresh = w_out[here, :] - scales[2] * u_out[here, :]
        n_out[here, :] = fresh
        c_out[here, :] = fresh.astype(bf16)
        return held

    each_rows(chans, one_out, 0)
    save(n_out, c_out)
    for place, weight, change, fresh_ref, copy in (
        (3, w_xp, u_xp, n_xp, c_xp),
        (4, w_dt, u_dt, n_dt, c_dt),
        (5, w_cv, u_cv, n_cv, c_cv),
        (6, w_cp, u_cp, n_cp, c_cp),
    ):
        for index in range(weight.shape[0]):
            fresh = weight[index] - scales[place] * change[index]
            fresh_ref[index] = fresh
            copy[index] = fresh.astype(bf16)
    parts = [
        (scales[1], stats[4:5, :], stats[5:6, :]),
        (scales[1], stats[0:1, :], stats[1:2, :]),
        (scales[2], stats[2:3, :], stats[3:4, :]),
    ]
    means = [scale * part_mean for scale, part_mean, _ in parts]
    mean = (means[0] + means[1] + means[2]) / 3.0
    spread = jnp.zeros_like(mean)
    for (scale, _, squares), part_mean in zip(parts, means):
        gap = part_mean - mean
        spread = spread + scale * scale * squares + width * gap * gap
    stats_out[0:1, :] = mean
    stats_out[1:2, :] = spread / (3.0 * width)


def join_kernel(pieces, copies, *, need, save):
    total = pieces[0].astype(f32)
    for place in range(1, pieces.shape[0]):
        total = total + pieces[place].astype(f32)
    low = total.astype(bf16)
    for place in range(pieces.shape[0]):
        copies[place] = low


def send_pieces(values, dp):
    chunk = values.shape[0] // dp
    return lax.all_to_all(values, "dp", 0, 0, tiled=True).reshape(dp, chunk, LANES)


def join_pieces(pieces):
    copies = call(join_kernel, at("x", shape(pieces.shape, bf16)), at("x", pieces), limit=8)[0]
    return copies.reshape(-1, LANES)


def call(kernel, outs, args, scratch=(), limit=32, micros=1):
    given = [array for array, _ in args]
    kinds = [kind for _, kind in args]
    out_kinds = [kind for _, kind in outs]
    fetched = [place for place, kind in enumerate(kinds) if kind == "h"]
    stored = [place for place, kind in enumerate(out_kinds) if kind == "h"]
    staging = [pltpu.VMEM(given[place].shape, given[place].dtype) for place in fetched]
    staging += [pltpu.VMEM(outs[place][0].shape, outs[place][0].dtype) for place in stored]
    moves = max(1, len(staging))

    def body(*refs):
        ins = list(refs[: len(given)])
        results = list(refs[len(given) : len(given) + len(outs)])
        rest = refs[len(given) + len(outs) :]
        stage, sems, own = rest[: len(staging)], rest[len(staging)], rest[len(staging) + 1 :]
        loads, saves = {}, {}
        for number, place in enumerate(fetched):
            loads[id(stage[number])] = pltpu.make_async_copy(ins[place], stage[number], sems.at[number])
            ins[place] = stage[number]
        for load in loads.values():
            load.start()
        for number, place in enumerate(stored, len(fetched)):
            saves[id(stage[number])] = pltpu.make_async_copy(stage[number], results[place], sems.at[number])
            results[place] = stage[number]
        begun = []

        def need(*wanted):
            for key in [id(ref) for ref in wanted] or list(loads):
                if key in loads:
                    loads.pop(key).wait()

        def save(*ready):
            for key in [id(ref) for ref in ready] or list(saves):
                if key in saves:
                    begun.append(saves.pop(key))
                    begun[-1].start()

        kernel(*ins, *results, *own, need=need, save=save)
        need()
        save()
        for move in begun:
            move.wait()

    spaces = {"x": pltpu.VMEM, "h": pltpu.HBM, "m": pltpu.HBM, "s": pltpu.SMEM}
    placed = [
        pltpu.with_memory_space_constraint(array, pltpu.HBM) if kind in "hm" else array for array, kind in args
    ]
    return pl.pallas_call(
        body,
        out_shape=[pltpu.HBM(out.shape, out.dtype) if kind in "hm" else out for out, kind in outs],
        in_specs=[pl.BlockSpec(memory_space=spaces[kind]) for kind in kinds],
        out_specs=[pl.BlockSpec(memory_space=spaces[kind]) for kind in out_kinds],
        scratch_shapes=[*staging, pltpu.SemaphoreType.DMA((moves,)), *scratch],
        compiler_params=pltpu.CompilerParams(vmem_limit_bytes=limit * MB),
        cost_estimate=pl.CostEstimate(flops=micros * 10**9, bytes_accessed=MB, transcendentals=0),
    )(*placed)


def at(kind, *things):
    return [(thing, kind) for thing in things]


def program(
    dp,
    hidden_in, out_cot, segment_ids,
    norm_gain, in_weight, out_weight, xproj_weight, dtproj_weight, conv_weight, chan_params,
    first_norm_gain, first_in_weight, first_out_weight, first_xproj_weight,
    first_dtproj_weight, first_conv_weight, first_chan_params,
    second_norm_gain, second_in_weight, second_out_weight, second_xproj_weight,
    second_dtproj_weight, second_conv_weight, second_chan_params,
):
    tokens, width = hidden_in.shape
    chans = in_weight.shape[2]
    half_width = first_norm_gain.shape[0]
    tiles = chans // LANES
    rank = dtproj_weight.shape[1]
    count = chan_params.shape[1] - 3
    rows = rank + 2 * count
    taps = conv_weight.shape[1]

    def swap(values):
        return lax.ppermute(values, "chan", [(0, 1), (1, 0)])

    me = lax.axis_index("chan")
    core = me.astype(jnp.int32).reshape(1)
    cot_own = out_cot.T
    cot_far = swap(cot_own)
    moments_own = jnp.stack([first_norm_gain, second_norm_gain])
    moments_far = swap(moments_own)
    moments_gain = jnp.where(
        me == 0,
        jnp.concatenate([moments_own, moments_far], 1),
        jnp.concatenate([moments_far, moments_own], 1),
    )

    def flip(values):
        return jnp.swapaxes(values, 1, 2)

    def turn(values):
        return jnp.swapaxes(values, 0, 1)

    w_xp = flip(xproj_weight)
    w_cp = turn(chan_params)
    square = (tokens, chans)
    z = Sizes(tokens, chans, count, rank)
    smem = at("s", core)

    def padded_rows(amount):
        return -(-amount // (dp * 16)) * 16 * dp

    mixing, gate, conv_pre, part, normed, low_in, same = call(
        front_kernel,
        at("h", shape(square, f32), shape(square, f32), shape((2,) + square, f32))
        + at("x", shape((2 * rows, tokens), f32))
        + at(
            "h", shape((tokens, width), bf16), shape((2, width, chans), bf16),
            shape((2, tokens, LANES), f32),
        ),
        at("h", hidden_in, segment_ids, norm_gain, in_weight, conv_weight, w_cp, w_xp),
        [pltpu.VMEM((tokens + 16, chans), f32), pltpu.VMEM((tokens + 16, LANES), f32)],
        limit=16, micros=7,
    )
    part_far = swap(part)
    early_rows = padded_rows(tiles * width + (width // LANES) * chans)
    grad_part, early, out_send, out_own, grad_act, grad_dt, grad_chan, gate_low = scan_call(
        at("x", part, part_far) + at("h", conv_pre, gate, same, cot_own) + at("x", cot_far)
        + at("h", out_weight, dtproj_weight, w_cp, normed) + smem,
        z, early_rows, half_width,
    )
    early_pieces = send_pieces(early, dp)
    grad_far = swap(grad_part)
    early_sums = lax.all_to_all(join_pieces(early_pieces), "dp", 0, 0, tiled=True)
    out_far = swap(out_send)
    late_rows = padded_rows(tiles * (width + 2 * rows + 2 * rank + 48))
    late, in_own, in_send = call(
        back_kernel,
        at("x", shape((late_rows, LANES), bf16))
        + at("h", shape((half_width + 8, tokens), f32))
        + at("x", shape((half_width + 8, tokens), f32)),
        at("x", grad_part, grad_far)
        + at("h", grad_act, conv_pre, mixing, gate_low, normed, low_in)
        + at("h", segment_ids, w_xp, conv_weight, hidden_in, norm_gain, grad_dt, grad_chan)
        + smem,
        [
            pltpu.VMEM((tokens + 16, chans), f32), pltpu.VMEM((2, tokens + 16, chans), f32),
            pltpu.VMEM((tokens + 16, LANES), f32), pltpu.VMEM(square, bf16),
            pltpu.VMEM((48, chans), f32), pltpu.VMEM((2,) + square, bf16),
        ],
        limit=20, micros=8,
    )
    in_far = swap(in_send)
    late_pieces = send_pieces(late, dp)
    output, input_grad = call(
        outputs_kernel,
        at("h", shape((half_width, tokens), bf16), shape((half_width, tokens), f32)),
        at("h", hidden_in, cot_own, out_own) + at("x", out_far) + at("h", in_own) + at("x", in_far) + smem,
        limit=16, micros=3,
    )
    firsts = [first_xproj_weight, first_dtproj_weight, first_conv_weight, first_chan_params]
    seconds = [second_xproj_weight, second_dtproj_weight, second_conv_weight, second_chan_params]
    for group in (firsts, seconds):
        group[0], group[3] = flip(group[0]), turn(group[3])
    weights = [w_xp, dtproj_weight, conv_weight, w_cp]
    small = [tensor for trio in zip(weights, firsts, seconds) for tensor in trio]
    half = shape((width, chans), f32)
    whole_in, whole_out = shape(in_weight.shape, f32), shape(out_weight.shape, f32)
    x_out, y_out, x_gate, y_gate, u_gate, u_out, early_norms, early_stats = call(
        early_kernel,
        at(
            "h", whole_out, whole_out, half, half, half, whole_out, shape((16, LANES), f32),
            shape((8, chans), f32),
        ),
        at("x", early_sums)
        + at(
            "h", in_weight, first_in_weight, second_in_weight, out_weight, first_out_weight,
            second_out_weight,
        ),
        limit=24, micros=5,
    )
    late_sums = lax.all_to_all(join_pieces(late_pieces), "dp", 0, 0, tiled=True)
    shapes = [shape(tensor.shape, f32) for tensor in weights]
    late_outs = [whole_in, whole_in]
    for entry in shapes:
        late_outs += [entry, entry]
    got = call(
        late_kernel,
        at("h", *late_outs, half, *shapes)
        + at("x", shape((16, LANES), f32))
        + at("h", shape((8, chans), f32)),
        at("x", late_sums)
        + at("h", x_gate, y_gate, early_norms, early_stats, in_weight, first_in_weight, second_in_weight)
        + at("h", *small),
        [pltpu.VMEM((width, chans), f32), pltpu.VMEM((width, chans), f32)],
        limit=24, micros=5,
    )
    moments, updates, norms, stats = got[:10], got[10:15], got[15], got[16]
    norms_far = swap(norms)
    pairs = []
    for entry in [whole_in, whole_out, *shapes]:
        pairs += [entry, shape(entry.shape, bf16)]
    row = shape((half_width,), f32)
    done = call(
        apply_kernel,
        at(
            "h", *pairs, row, row, row, shape((half_width,), bf16), shape((2, 7), f32),
            shape((2, chans), f32),
        ),
        at("x", norms, norms_far)
        + at("h", stats, in_weight, out_weight, *weights, updates[0], u_gate, u_out, *updates[1:])
        + at("h", norm_gain) + at("x", moments_gain[0:1], moments_gain[1:2]) + smem,
        limit=24, micros=5,
    )
    flat = list(done[12:16])
    firsts_out = [moments[0], x_out, *moments[2::2]]
    seconds_out = [moments[1], y_out, *moments[3::2]]
    for place in range(6):
        entry = [firsts_out[place], seconds_out[place], done[2 * place], done[2 * place + 1]]
        if place == 2:
            entry = [flip(tensor) for tensor in entry]
        if place == 5:
            entry = [turn(tensor) for tensor in entry]
        flat += entry
    return (output.T, input_grad.T, *flat, done[16].T, done[17])


def solution(mesh):
    rows = P("dp", None)
    cells = P("dp", "chan")
    last = P(None, None, "chan")
    first = P("chan", None)
    middle = P(None, "chan", None)
    tensors = (last, first, middle, last, last, last)
    outs = [cells, cells] + [P("chan")] * 4
    for spec in tensors:
        outs += [spec] * 4
    return jax.shard_map(
        functools.partial(program, mesh.shape["dp"]),
        mesh=mesh,
        in_specs=(rows, cells, P("dp"), P(), *tensors, P("chan"), *tensors, P("chan"), *tensors),
        out_specs=(*outs, P(), P(None, "chan")),
        check_vma=False,
    )
```

time: 162 us -> 132 us (0.81)
  blocking collectives: 34.6 us -> 0 us
  local copies, waits for them, and re-layouts: 28.7 us -> 0.03 us
  starting transfers between devices: 5.6 us -> 21.5 us
  waiting for transfers between devices: 25.6 us -> 38.5 us
  Pallas kernels: 64.8 us -> 70.2 us
    all_to_all x1 -> x0, blocking collectives: 34.6 us -> none  [program(): lax.all_to_all(sums, 'dp', 0, 0, tiled=True).reshape(dp, chunk, LANES)]
    unnamed x90 -> x6, local copies, waits for them, and re-layouts: 24.3 us -> 0.02 us
    all_to_all x1 -> x4, starting transfers between devices: 4.12 us -> 20.1 us  [the longest x2 12.4 us: send_pieces(): lax.all_to_all(values, 'dp', 0, 0, tiled=True).reshape(dp, chunk, LANES)]
    all_to_all x1 -> x4, waiting for transfers between devices: 22.4 us -> 34.7 us  [the longest x2 16.1 us: send_pieces(): lax.all_to_all(values, 'dp', 0, 0, tiled=True).reshape(dp, chunk, LANES)]
    pallas_call x6 -> x9, Pallas kernels: 64.8 us -> 70.2 us  [call(): pl.pallas_call(body, out_shape=[pltpu.HBM(out.shape, out.dtype) if kind i...]
    dynamic_slice x3 -> x0, local copies, waits for them, and re-layouts: 1.88 us -> none  [own(): return lax.dynamic_slice_in_dim(values[0], own_start, half_width)]
  transfers between devices with their start and end apart: 8 -> 11, of which waited for: 4 -> 7; matrix products, arithmetic and copies ran while one was open for 0% -> 0% of each run, Pallas kernels for 6% -> 21%
where the time goes in v2:
time: 132 us; the launch traced here: 131 us
  Pallas kernels  70.2 us (53%)
  waiting for transfers between devices  38.5 us (29%)
  starting transfers between devices  21.5 us (16%)
    pallas_call x9, Pallas kernels, call(): pl.pallas_call(body, out_shape=[pltpu.HBM(out.shape, out.dtype) if kind i...  70.2 us
    all_to_all x2, waiting for transfers between devices, send_pieces(): lax.all_to_all(values, 'dp', 0, 0, tiled=True).reshape(dp, chunk, LANES)  16.1 us
    all_to_all x1, waiting for transfers between devices, program(): lax.all_to_all(join_pieces(early_pieces), 'dp', 0, 0, tiled=True)  14.5 us
    all_to_all x2, starting transfers between devices, send_pieces(): lax.all_to_all(values, 'dp', 0, 0, tiled=True).reshape(dp, chunk, LANES)  12.4 us
    all_to_all x1, waiting for transfers between devices, program(): late_sums = lax.all_to_all(join_pieces(late_pieces), 'dp', 0, 0, tiled=True)  4.19 us
    all_to_all x1, starting transfers between devices, program(): late_sums = lax.all_to_all(join_pieces(late_pieces), 'dp', 0, 0, tiled=True)  4 us
    ppermute x7, waiting for transfers between devices, swap(): return lax.ppermute(values, 'chan', [(0, 1), (1, 0)])  3.83 us
    all_to_all x1, starting transfers between devices, program(): lax.all_to_all(join_pieces(early_pieces), 'dp', 0, 0, tiled=True)  3.71 us
  transfers between devices with their start and end apart: 11, of which 7 were waited for; matrix products, arithmetic and copies ran while one was open for 0% of the time, Pallas kernels for 21%

profile of v2, /device:TPU:0, one launch (start us, length us, event | category | flops | bytes accessed | tf_op | source)
XLA Modules:
  0.0 131.4 jit_solution(17383621697751750172)
XLA Ops:
  0.7 0.0 copy-start.2
  0.7 7.3 %shard_map.479 = (f32[384,384]{1,0:T(8,128)}, f32[384,384]{1,0:T(8,128)}, f32[2,384,384]{2,1,0:T(8,128)}, f32[112,384]{1,0:T(8,128)S(1)}, bf16[384,384]{1,0:T(8,...) custom-call(bf16[384,384]{1,0:T(8,128)(2,1)} %refs_0_.3, s32[384]{0:T(512)} %refs_8_.3, f32[384]{0:T(512)} %refs_16_.3, ...), custom_call_target="tpu_custom_call" | custom-call | flops 7000000000 | bytes 1048576 | tf_op jit(solution)/shard_map/pallas_call | solution.py:993
  8.0 0.5 collective-permute-start
  8.5 0.0 copy-done.2
  8.5 0.1 collective-permute-start.1
  8.6 1.3 collective-permute-done.1.refs_6_
  9.9 0.0 collective-permute-done.refs_1_
  9.9 28.6 %shard_map.480 = (f32[112,384]{1,0:T(8,128)S(1)}, bf16[2304,128]{1,0:T(8,128)(2,1)}, f32[192,384]{1,0:T(8,128)S(1)}, f32[192,384]{1,0:T(8,128)}, f32[2,384,384]{...) custom-call(f32[112,384]{1,0:T(8,128)S(1)} %get-tuple-element.95.refs_0_, ...), custom_call_target="tpu_custom_call" | custom-call | flops 30000001024 | bytes 1048576 | tf_op jit(solution)/shard_map/pallas_call | solution.py:993
  38.5 8.1 %all-to-all-start.2 = ((bf16[16,144,128]{2,1,0:T(8,128)(2,1)}), bf16[16,144,128]{2,1,0:T(8,128)(2,1)S(1)}, u32[]{:S(2)}, u32[]{:S(2)}) async-start(bf16[16,144,128]{2,1,0:T(8,128)(2,1)} %bitcast.8), calls=%async_computation.2 | async-start | bytes 1179648 | tf_op jit(solution)/shard_map/all_to_all | solution.py:938
  46.6 0.1 collective-permute-start.3
  46.7 1.4 %collective-permute-done.3.refs_1_ = f32[112,384]{1,0:T(8,128)S(1)} collective-permute-done((f32[112,384]{1,0:T(8,128)S(1)}, f32[112,384]{1,0:T(8,128)S(1)}, u32[]{:S(2)}, u32[]{:S(2)}) %collective-permute-start.3) | collective-permute-done | bytes 172064 | tf_op jit(solution)/shard_map/ppermute | solution.py:1027
  48.1 11.2 %shard_map.481 = (bf16[1792,128]{1,0:T(8,128)(2,1)}, f32[200,384]{1,0:T(8,128)}, f32[200,384]{1,0:T(8,128)S(1)}) custom-call(f32[112,384]{1,0:T(8,128)S(1)} %get-tuple-element.102.refs_0_, f32[112,384]{1,0:T(8,128)S(1)} %collective-permute-done.3.refs_1_, f32[2,384,384]{2,1,0:T(8,128)} %get-tuple-element.103.refs_2_, ...), custom_call_target="tpu_custom_call" | custom-call | flops 8000000000 | bytes 1048576 | tf_op jit(solution)/shard_map/pallas_call | solution.py:993
  59.3 3.9 %all-to-all-done.2.refs_0_ = bf16[16,144,128]{2,1,0:T(8,128)(2,1)S(1)} async-done(((bf16[16,144,128]{2,1,0:T(8,128)(2,1)}), bf16[16,144,128]{2,1,0:T(8,128)(2,1)S(1)}, u32[]{:S(2)}, u32[]{:S(2)}) %all-to-all-start.2) | async-done | bytes 589856 | tf_op jit(solution)/shard_map/all_to_all | solution.py:938
  63.2 4.2 %all-to-all-start = ((bf16[16,112,128]{2,1,0:T(8,128)(2,1)}), bf16[16,112,128]{2,1,0:T(8,128)(2,1)S(1)}, u32[]{:S(2)}, u32[]{:S(2)}) async-start(bf16[16,112,128]{2,1,0:T(8,128)(2,1)} %bitcast.6), calls=%async_computation | async-start | bytes 917504 | tf_op jit(solution)/shard_map/all_to_all | solution.py:938
  67.5 0.9 shard_map.484
  68.4 12.2 %all-to-all-done.refs_0_ = bf16[16,112,128]{2,1,0:T(8,128)(2,1)S(1)} async-done(((bf16[16,112,128]{2,1,0:T(8,128)(2,1)}), bf16[16,112,128]{2,1,0:T(8,128)(2,1)S(1)}, u32[]{:S(2)}, u32[]{:S(2)}) %all-to-all-start) | async-done | bytes 458784 | tf_op jit(solution)/shard_map/all_to_all | solution.py:938
  80.5 3.7 %all-to-all-start.3 = ((bf16[16,144,128]{2,1,0:T(8,128)(2,1)}), bf16[16,144,128]{2,1,0:T(8,128)(2,1)S(1)}, u32[]{:S(2)}, u32[]{:S(2)}) async-start(bf16[16,144,128]{2,1,0:T(8,128)(2,1)} %shard_map.484), calls=%async_computation.3 | async-start | bytes 1179648 | tf_op jit(solution)/shard_map/all_to_all | solution.py:1077
  84.3 0.0 copy-start
  84.3 0.0 copy-start.1
  84.3 0.8 shard_map.483
  85.1 14.5 %all-to-all-done.3 = bf16[16,144,128]{2,1,0:T(8,128)(2,1)S(1)} async-done(((bf16[16,144,128]{2,1,0:T(8,128)(2,1)}), bf16[16,144,128]{2,1,0:T(8,128)(2,1)S(1)}, u32[]{:S(2)}, u32[]{:S(2)}) %all-to-all-start.3) | async-done | bytes 589856 | tf_op jit(solution)/shard_map/all_to_all | solution.py:1077
  99.6 4.0 %all-to-all-start.1 = ((bf16[16,112,128]{2,1,0:T(8,128)(2,1)}), bf16[16,112,128]{2,1,0:T(8,128)(2,1)S(1)}, u32[]{:S(2)}, u32[]{:S(2)}) async-start(bf16[16,112,128]{2,1,0:T(8,128)(2,1)} %shard_map.483), calls=%async_computation.1 | async-start | bytes 917504 | tf_op jit(solution)/shard_map/all_to_all | solution.py:1125
  103.6 0.0 copy-done
  103.6 0.0 copy-done.1
  103.7 0.1 collective-permute-start.6
  103.7 1.1 collective-permute-done.6
  104.9 0.1 maximum_select_fusion
  105.0 0.2 collective-permute-start.2
  105.2 0.3 collective-permute-start.4
  105.5 6.8 %shard_map.485 = (f32[384,384]{1,0:T(8,128)}, f32[384,384]{1,0:T(8,128)}, f32[384,384]{1,0:T(8,128)}, f32[384,384]{1,0:T(8,128)}, f32[384,384]{1,0:T(8,128)}, /*...) custom-call(bf16[2304,128]{1,0:T(8,128)(2,1)S(1)} %bitcast.25, f32[384,2,384]{2,1,0:T(2,128)} %refs_3_.5, ...), custom_call_target="tpu_custom_call" | custom-call | flops 5000000000 | bytes 1048576 | tf_op jit(solution)/shard_map/pallas_call | solution.py:993
  112.3 4.2 %all-to-all-done.1 = bf16[16,112,128]{2,1,0:T(8,128)(2,1)S(1)} async-done(((bf16[16,112,128]{2,1,0:T(8,128)(2,1)}), bf16[16,112,128]{2,1,0:T(8,128)(2,1)S(1)}, u32[]{:S(2)}, u32[]{:S(2)}) %all-to-all-start.1) | async-done | bytes 458784 | tf_op jit(solution)/shard_map/all_to_all | solution.py:1125
  116.5 6.1 %shard_map.486 = (f32[384,2,384]{2,1,0:T(2,128)}, f32[384,2,384]{2,1,0:T(2,128)}, f32[2,56,384]{2,1,0:T(8,128)}, f32[2,56,384]{2,1,0:T(8,128)}, f32[2,24,384]{2,...) custom-call(bf16[1792,128]{1,0:T(8,128)(2,1)S(1)} %bitcast.26, ...), custom_call_target="tpu_custom_call" | custom-call | flops 5000000000 | bytes 1048576 | tf_op jit(solution)/shard_map/pallas_call | solution.py:993
  122.6 0.1 collective-permute-start.5
  122.7 0.0 collective-permute-done.2.refs_3_
  122.7 0.0 collective-permute-done.4.refs_5_
  122.7 2.3 %shard_map.482 = (bf16[192,384]{1,0:T(8,128)(2,1)}, f32[192,384]{1,0:T(8,128)}) custom-call(bf16[384,384]{1,0:T(8,128)(2,1)} %refs_0_.3, bf16[192,384]{1,0:T(8,128)(2,1)} %bitcast.38, f32[192,384]{1,0:T(8,128)} %get-tuple-element.100.refs_2_, f32[192,384]{1,0:T(8,128)S(1)} %collective-permute-done.2.refs_3_, f32[200,384]{1,0:T(8,128)} %get-tuple-element.109.refs_4_, ...), custom_call_target="tpu_custom_call" | custom-call | flops 3000000000 | bytes 1048576 | tf_op jit(solution)/shard_map/pallas_call | solution.py:993
  125.0 0.0 collective-permute-done.5.refs_1_
  125.0 6.2 %shard_map.487 = (f32[384,2,384]{2,1,0:T(2,128)}, bf16[384,2,384]{2,1,0:T(2,128)(2,1)}, f32[384,384]{1,0:T(8,128)}, bf16[384,384]{1,0:T(8,128)(2,1)}, f32[2,56,3...) custom-call(f32[16,128]{1,0:T(8,128)S(1)} %get-tuple-element.119.ref, ...), custom_call_target="tpu_custom_call" | custom-call | flops 5000000000 | bytes 1048576 | tf_op jit(solution)/shard_map/pallas_call | solution.py:993
  (2 shorter events, 0.0 us)
Async XLA Ops:
  0.7 7.8 %copy-start.2 = (bf16[384,192]{0,1:T(8,128)(2,1)S(1)}, bf16[384,192]{0,1:T(8,128)(2,1)}, u32[]{:S(2)}) copy-start(bf16[384,192]{0,1:T(8,128)(2,1)} %param.25) | copy-start | bytes 442372
  8.0 1.9 %collective-permute-start = (f32[112,384]{1,0:T(8,128)S(1)}, f32[112,384]{1,0:T(8,128)S(1)}, u32[]{:S(2)}, u32[]{:S(2)}) collective-permute-start(f32[112,384]{1,0:T(8,128)S(1)} %get-tuple-element.95.refs_0_), channel_id=1, source_target_pairs={{0,1},{1,0},{2,3},{3,2},{4,5},{5,4},{6,7},{7,6},{8,9},{9,8},{10,11... | collective-permute-start | bytes 516104 | tf_op jit(solution)/shard_map/ppermute | solution.py:1027
  8.5 1.4 %collective-permute-start.1 = (bf16[192,384]{1,0:T(8,128)(2,1)S(1)}, bf16[192,384]{1,0:T(8,128)(2,1)S(1)}, u32[]{:S(2)}, u32[]{:S(2)}) collective-permute-start(bf16[192,384]{1,0:T(8,128)(2,1)S(1)} %bitcast.39), channel_id=1, source_target_pairs={{0,1},{1,0},{2,3},{3,2},{4,5},{5,4},{6,7},{7,6},{8,9},{9,8},{10,11... | collective-permute-start | bytes 442376 | tf_op jit(solution)/shard_map/ppermute | solution.py:1027
  38.5 24.7 %all-to-all-start.2 = ((bf16[16,144,128]{2,1,0:T(8,128)(2,1)}), bf16[16,144,128]{2,1,0:T(8,128)(2,1)S(1)}, u32[]{:S(2)}, u32[]{:S(2)}) async-start(bf16[16,144,128]{2,1,0:T(8,128)(2,1)} %bitcast.8), calls=%async_computation.2 | async-start | bytes 1179648 | tf_op jit(solution)/shard_map/all_to_all | solution.py:938
  46.6 1.5 %collective-permute-start.3 = (f32[112,384]{1,0:T(8,128)S(1)}, f32[112,384]{1,0:T(8,128)S(1)}, u32[]{:S(2)}, u32[]{:S(2)}) collective-permute-start(f32[112,384]{1,0:T(8,128)S(1)} %get-tuple-element.102.refs_0_), channel_id=1, source_target_pairs={{0,1},{1,0},{2,3},{3,2},{4,5},{5,4},{6,7},{7,6},{8,9},{9,8},{10,11... | collective-permute-start | bytes 516104 | tf_op jit(solution)/shard_map/ppermute | solution.py:1027
  63.2 17.3 %all-to-all-start = ((bf16[16,112,128]{2,1,0:T(8,128)(2,1)}), bf16[16,112,128]{2,1,0:T(8,128)(2,1)S(1)}, u32[]{:S(2)}, u32[]{:S(2)}) async-start(bf16[16,112,128]{2,1,0:T(8,128)(2,1)} %bitcast.6), calls=%async_computation | async-start | bytes 917504 | tf_op jit(solution)/shard_map/all_to_all | solution.py:938
  80.5 19.1 %all-to-all-start.3 = ((bf16[16,144,128]{2,1,0:T(8,128)(2,1)}), bf16[16,144,128]{2,1,0:T(8,128)(2,1)S(1)}, u32[]{:S(2)}, u32[]{:S(2)}) async-start(bf16[16,144,128]{2,1,0:T(8,128)(2,1)} %shard_map.484), calls=%async_computation.3 | async-start | bytes 1179648 | tf_op jit(solution)/shard_map/all_to_all | solution.py:1077
  84.3 19.4 %copy-start = (f32[192]{0:T(256)S(1)}, f32[192]{0:T(256)}, u32[]{:S(2)}) copy-start(f32[192]{0:T(256)} %param.41) | copy-start | bytes 2308
  84.3 19.4 %copy-start.1 = (f32[192]{0:T(256)S(1)}, f32[192]{0:T(256)}, u32[]{:S(2)}) copy-start(f32[192]{0:T(256)} %param.34) | copy-start | bytes 2308
  99.6 16.9 %all-to-all-start.1 = ((bf16[16,112,128]{2,1,0:T(8,128)(2,1)}), bf16[16,112,128]{2,1,0:T(8,128)(2,1)S(1)}, u32[]{:S(2)}, u32[]{:S(2)}) async-start(bf16[16,112,128]{2,1,0:T(8,128)(2,1)} %shard_map.483), calls=%async_computation.1 | async-start | bytes 917504 | tf_op jit(solution)/shard_map/all_to_all | solution.py:1125
  103.7 1.2 collective-permute-start.6
  105.0 17.7 %collective-permute-start.2 = (f32[192,384]{1,0:T(8,128)S(1)}, f32[192,384]{1,0:T(8,128)S(1)}, u32[]{:S(2)}, u32[]{:S(2)}) collective-permute-start(f32[192,384]{1,0:T(8,128)S(1)} %get-tuple-element.101), channel_id=1, source_target_pairs={{0,1},{1,0},{2,3},{3,2},{4,5},{5,4},{6,7},{7,6},{8,9},{9,8},{10,11... | collective-permute-start | bytes 884744 | tf_op jit(solution)/shard_map/ppermute | solution.py:1027
  105.2 17.5 %collective-permute-start.4 = (f32[200,384]{1,0:T(8,128)S(1)}, f32[200,384]{1,0:T(8,128)S(1)}, u32[]{:S(2)}, u32[]{:S(2)}) collective-permute-start(f32[200,384]{1,0:T(8,128)S(1)} %get-tuple-element.110), channel_id=1, source_target_pairs={{0,1},{1,0},{2,3},{3,2},{4,5},{5,4},{6,7},{7,6},{8,9},{9,8},{10,11... | collective-permute-start | bytes 921608 | tf_op jit(solution)/shard_map/ppermute | solution.py:1027
  122.6 2.4 %collective-permute-start.5 = (f32[16,128]{1,0:T(8,128)S(1)}, f32[16,128]{1,0:T(8,128)S(1)}, u32[]{:S(2)}, u32[]{:S(2)}) collective-permute-start(f32[16,128]{1,0:T(8,128)S(1)} %get-tuple-element.119.refs_0_), channel_id=1, source_target_pairs={{0,1},{1,0},{2,3},{3,2},{4,5},{5,4},{6,7},{7,6},{8,9},{9,8},{10,11... | collective-permute-start | bytes 24584 | tf_op jit(solution)/shard_map/ppermute | solution.py:1027

commit v3 on v2

--- a/solution.py
+++ b/solution.py
@@ -80,7 +80,7 @@
 
 
 def front_kernel(
-    hid, seg, gain, w_in, taps, params, w_xp,
+    hid, gain, w_mix, w_gate, seg, taps, params, w_xp,
     mix_out, gate_out, conv_out, part_out, norm_out, low_out, same_out,
     padded, sgpad,
     *, need, save,
@@ -99,10 +99,9 @@
         return held
 
     each_rows(tokens, normalise, 0)
-    save(norm_out)
-    need()
-    for half in range(2):
-        low_out[half] = w_in[:, half, :].astype(bf16)
+    need(w_mix, w_gate)
+    low_out[0] = w_mix[...].astype(bf16)
+    low_out[1] = w_gate[...].astype(bf16)
     save(low_out)
     normed = norm_out[...]
     mixing = dot(normed, low_out[0], NN)
@@ -112,7 +111,7 @@
     padded[pl.ds(8 + tokens, 8), :] = jnp.zeros((8, chans), f32)
     save(mix_out)
     gate_out[...] = dot(normed, low_out[1], NN)
-    save(gate_out)
+    need(seg, taps, w_xp, params)
     numbers = spread_segments(seg[...], tokens)
     sgpad[0:8, :] = jnp.full((8, LANES), -1.0, f32)
     sgpad[pl.ds(8, tokens), :] = numbers
@@ -137,7 +136,6 @@
         return held
 
     each_rows(tokens, convolve, 0)
-    save(conv_out, same_out)
     for heading in range(2):
         pre = conv_out[heading]
         act_low = (pre * sigmoid(pre)).astype(bf16)
@@ -220,16 +218,68 @@
 
 def dot3(left, right, dims):
     (left_high, left_low), (right_high, right_low) = split(left), split(right)
-    return dot(left_high, right_high, dims) + (
-        dot(left_low, right_high, dims) + dot(left_high, right_low, dims)
-    )
-
-
-def scan_kernel(
-    own_part, far_part, conv_pre, gate, same, cot_own, cot_far, w_out, w_dt, params, normed, core,
-    grad_part, early, out_far, out_own, grad_act, grad_dt, grad_chan, gate_low,
-    proj, pre_step, grad_branch, far_step, inflow, grad_y, grad_y_low, result, decayed, branch_low,
-    maps, diagonal, gathered, states, low_one, low_two, rates, rates2, inflow_low,
+    if dims == TN:
+        lefts = jnp.concatenate([left_high, left_low, left_high], axis=0)
+        return dot(lefts, jnp.concatenate([right_high, right_high, right_low], axis=0), dims)
+    rows = left.shape[0]
+    both = dot(jnp.concatenate([left_high, left_low], axis=0), right_high, dims)
+    return both[:rows] + both[rows:] + dot(left_high, right_low, dims)
+
+
+class Sweep:
+    def __init__(self, z, turned):
+        self.z, self.turned = z, turned
+        self.groups = z.tokens // z.count
+        self.stage_groups = self.groups // z.blocks
+
+    def group(self, order, heading):
+        return self.groups - 1 - order if heading == self.turned else order
+
+    def block(self, stage, heading):
+        return self.z.blocks - 1 - stage if heading == self.turned else stage
+
+    def inner(self, ahead, heading):
+        return self.z.count - 1 - ahead if heading == self.turned else ahead
+
+    def rows(self, group):
+        return pl.ds(pl.multiple_of(group * self.z.count, self.z.count), self.z.count)
+
+    def run(self, z, carried, scan, post, between):
+        def step(index, held):
+            order = 2 * index
+            post(jnp.maximum(order - 1, 0), 1)
+            held = scan(order, held, 0)
+            post(order, 0)
+            return scan(order + 1, held, 1)
+
+        per = self.stage_groups // 2
+        for stage in range(z.blocks):
+            between(stage, True)
+            carried = lax.fori_loop(stage * per, (stage + 1) * per, step, carried)
+            between(stage, False)
+        post(self.groups - 1, 1)
+        return carried
+
+
+def store_gathered(target, target_row, gathered, heading, z):
+    per = LANES // z.count
+    for block in range(z.blocks):
+        pieces = [gathered[heading, block * per + place] for place in range(per)]
+        target[target_row : target_row + z.count, cols(block)] = jnp.concatenate(pieces, axis=1)
+
+
+def fill_rates(rates, params, count):
+    for heading in range(2):
+        for n in range(count):
+            value = -jnp.exp(params[3 + n, heading : heading + 1, :])
+            rates[heading, n : n + 1, :] = jnp.minimum(value, FLOOR)
+
+
+def forward_kernel(
+    own_part, far_part, params, w_dt, cot_own, cot_far, w_out, conv_pre, gate, same, normed, core,
+    states_out, proj, grad_maps, skips, far_step, grad_y, pre_step, inflow_low, gate_low, early, out_far, out_own,
+    grad_branch, inflow, grad_y_low, result, branch_low, maps, diagonal, gathered, states, low_one, low_two,
+    rates, sems,
     *, need, save,
 ):
     tokens, chans = gate.shape
@@ -238,10 +288,24 @@
     half_width = cot_own.shape[0]
     width = 2 * half_width
     me = core[0]
-    groups = tokens // count
+    sweep = Sweep(z, 1)
+    lows = (low_one, low_two)
 
     proj[...] = own_part[...] + far_part[...]
-    need(params, w_dt, w_out, cot_own)
+    save(proj)
+    for heading in range(2):
+        first = heading * rows + rank
+        group_maps(maps, proj[first : first + count, :], heading, count)
+        diagonal_maps(diagonal, proj[first + count : first + 2 * count, :], heading, count)
+    need(params, w_dt)
+    fill_rates(rates, params, count)
+    for heading in range(2):
+        pre_step[heading] = (
+            dot3(proj[heading * rows : heading * rows + rank, :], w_dt[heading], TN)
+            + params[1, heading : heading + 1, :]
+        )
+    save(pre_step)
+    need(w_out, cot_own)
     low_out = w_out[...].astype(bf16)
     low_cot = jnp.where(
         me == 0,
@@ -249,20 +313,7 @@
         jnp.concatenate([cot_far[...].astype(f32), cot_own[...].astype(f32)], 0),
     ).astype(bf16)
     grad_branch[...] = dot(low_cot, low_out, ((0,), (1,)))
-    for heading in range(2):
-        for n in range(count):
-            value = -jnp.exp(params[3 + n, heading : heading + 1, :])
-            rates[heading, n : n + 1, :] = value
-            rates2[heading, n : n + 1, :] = jnp.minimum(value * LOG2E, FLOOR)
-        pre_step[heading] = (
-            dot3(proj[heading * rows : heading * rows + rank, :], w_dt[heading], TN)
-            + params[1, heading : heading + 1, :]
-        )
-        first = heading * rows + rank
-        group_maps(maps, proj[first : first + count, :], heading, count)
-        diagonal_maps(diagonal, proj[first + count : first + 2 * count, :], heading, count)
-
-    need(conv_pre, gate, same)
+
     for tile in range(tiles):
 
         def prepare(start, held, tile=tile):
@@ -275,7 +326,7 @@
                 entering = size * act
                 inflow[there, :] = entering
                 inflow_low[heading, here, cols(tile)] = entering.astype(bf16)
-                far_step[there, :] = jnp.where(same[heading, here, :] > 0.5, size, FAR)
+                far_step[there, :] = jnp.where(same[heading, here, :] > 0.5, size * LOG2E, FAR)
             gated = gate[here, cols(tile)]
             back = grad_branch[here, cols(tile)] * (gated * sigmoid(gated))
             grad_y[pl.ds(z.base(0, tile) + start, SPAN), :] = back
@@ -283,68 +334,64 @@
             return held
 
         each_rows(tokens, prepare, 0, SPAN)
+    save(far_step, inflow_low, grad_y)
 
     blank = jnp.zeros((count, LANES), f32)
-    states[0, 0:count, :] = jnp.zeros((count, chans), f32)
-    states[1, tokens * count : (tokens + 1) * count, :] = jnp.zeros((count, chans), f32)
-    low_one[...] = jnp.zeros(low_one.shape, bf16)
+    states[0, 0:count, :] = jnp.zeros((count, chans), bf16)
+    states[1, tokens * count : (tokens + 1) * count, :] = jnp.zeros((count, chans), bf16)
     low_two[...] = jnp.zeros(low_two.shape, bf16)
-
-    def group_of(order, heading):
-        return order if heading == 0 else groups - 1 - order
-
-    def run_forward(order, carried, low):
+    speeds = [rates[heading, :, cols(tile)] for heading, tile in z.pairs]
+
+    def scan(order, carried, slot):
         carried = list(carried)
-        enters = [maps[heading, group_of(order, heading)] for heading in range(2)]
-        for ahead in range(count):
-            for heading in range(2):
-                inner = ahead if heading == 0 else count - 1 - ahead
-                at = group_of(order, heading) * count + inner
+        enters = [maps[heading, sweep.group(order, heading)] for heading in range(2)]
+        for heading in range(2):
+            for ahead in range(count):
+                inner = sweep.inner(ahead, heading)
+                at = sweep.group(order, heading) * count + inner
                 kept = pl.multiple_of((at + (1 if heading == 0 else 0)) * count, count)
                 enter = jnp.broadcast_to(enters[heading][:, inner : inner + 1], (count, LANES))
                 for tile in range(tiles):
                     number = heading * tiles + tile
-                    decay = jnp.exp2(z.row(far_step, heading, tile, at) * rates2[heading, :, cols(tile)])
+                    decay = jnp.exp2(z.row(far_step, heading, tile, at) * speeds[number])
                     state = decay * carried[number] + enter * z.row(inflow, heading, tile, at)
                     carried[number] = state
-                    states[heading, pl.ds(kept, count), cols(tile)] = state
-                    low[heading, inner * count : (inner + 1) * count, cols(tile)] = state.astype(bf16)
+                    low = state.astype(bf16)
+                    states[heading, pl.ds(kept, count), cols(tile)] = low
+                    lows[slot][heading, inner * count : (inner + 1) * count, cols(tile)] = low
         return tuple(carried)
 
-    def rows_of(group):
-        return pl.ds(pl.multiple_of(group * count, count), count)
-
-    def post_forward(order, low):
+    def post(order, slot):
         for heading in range(2):
-            group = group_of(order, heading)
-            left = low[heading]
-            gathered[heading, group] = gather_states(left, grad_y_low[rows_of(group), :], count)
-            result[heading, rows_of(group), :] = weigh_states(
+            group = sweep.group(order, heading)
+            left = lows[slot][heading]
+            gathered[heading, group] = gather_states(left, grad_y_low[sweep.rows(group), :], count)
+            result[heading, sweep.rows(group), :] = weigh_states(
                 left, diagonal[heading, group].reshape(2 * count, count * count)
             )
 
-    def forward(index, carried):
-        order = 2 * index
-        post_forward(jnp.maximum(order - 1, 0), low_two.at[0])
-        carried = run_forward(order, carried, low_one.at[0])
-        post_forward(order, low_one.at[0])
-        return run_forward(order + 1, carried, low_two.at[0])
-
-    lax.fori_loop(0, groups // 2, forward, (blank,) * len(z.pairs))
-    post_forward(groups - 1, low_two.at[0])
-
-    def store_gathered(target_row, heading):
-        for block in range(z.blocks):
-            per = LANES // count
-            pieces = [gathered[heading, block * per + place] for place in range(per)]
-            grad_part[target_row : target_row + count, cols(block)] = jnp.concatenate(pieces, axis=1)
-
+    keeps = []
+
+    def between(stage, before):
+        if before:
+            return
+        for heading in range(2):
+            begin, extent = sweep.block(stage, heading) * z.block_rows, z.block_rows
+            if stage == 0:
+                extent += count
+            elif heading == 0:
+                begin += count
+            piece = pl.ds(begin, extent)
+            keep = pltpu.make_async_copy(
+                states.at[heading, piece, :], states_out.at[heading, piece, :], sems.at[heading, stage]
+            )
+            keep.start()
+            keeps.append(keep)
+
+    sweep.run(z, (blank,) * len(z.pairs), scan, post, between)
     for heading in range(2):
-        first = heading * rows + rank
-        store_gathered(first + count, heading)
-        group_maps(maps, proj[first + count : first + 2 * count, :], heading, count)
-        diagonal_maps(diagonal, proj[first : first + count, :], heading, count)
-
+        store_gathered(grad_maps, heading * count, gathered, heading, z)
+    skips[...] = jnp.zeros(skips.shape, f32)
     for tile in range(tiles):
 
         def finish(start, held, tile=tile):
@@ -366,14 +413,15 @@
             ).astype(bf16)
             return tuple(sums)
 
-        skips = each_rows(tokens, finish, (jnp.zeros((8, LANES), f32),) * 2, SPAN)
+        sums = each_rows(tokens, finish, (jnp.zeros((8, LANES), f32),) * 2, SPAN)
         for heading in range(2):
-            grad_chan[2, heading : heading + 1, cols(tile)] = jnp.sum(
-                skips[heading], axis=0, keepdims=True
-            )
-    save(gate_low)
-    need(normed)
+            skips[heading : heading + 1, cols(tile)] = jnp.sum(sums[heading], axis=0, keepdims=True)
+    save(gate_low, grad_maps, skips)
     branch = branch_low[...]
+    sent = dot(low_out, branch, ((0,), (1,)))
+    out_own[...] = jnp.where(me == 0, sent[:half_width], sent[half_width:])
+    out_far[...] = jnp.where(me == 0, sent[half_width:], sent[:half_width])
+    save(out_own)
     grad_w = dot(branch, low_cot, ((0,), (1,))).astype(bf16)
     for tile in range(width // LANES):
         early[tile * chans : (tile + 1) * chans, :] = grad_w[:, cols(tile)]
@@ -384,64 +432,101 @@
     base_row += tiles * width
     if early.shape[0] > base_row:
         early[base_row:, :] = jnp.zeros((early.shape[0] - base_row, LANES), bf16)
-    sent = dot(low_out, branch, ((0,), (1,)))
-    out_own[...] = jnp.where(me == 0, sent[:half_width], sent[half_width:])
-    out_far[...] = jnp.where(me == 0, sent[half_width:], sent[:half_width])
-    save(out_own)
-
-    def run_backward(order, held, low, products):
+    for keep in keeps:
+        keep.wait()
+
+
+def backward_kernel(
+    states_in, params, proj, far_step, grad_y, inflow_low, pre_step, conv_pre, grad_maps, skips, w_dt,
+    grad_part, grad_act, grad_dt, grad_chan,
+    result, decayed, maps, diagonal, gathered, states, low_one, low_two, products_one, products_two, rates, sems,
+    *, need, save,
+):
+    _, tokens, chans = conv_pre.shape
+    z = Sizes(tokens, chans, params.shape[0] - 3, w_dt.shape[1])
+    count, rank, rows, tiles = z.count, z.rank, z.rows, z.tiles
+    sweep = Sweep(z, 0)
+    lows, products = (low_one, low_two), (products_one, products_two)
+    loads = {}
+    for stage in range(z.blocks):
+        for heading in range(2):
+            begin = sweep.block(stage, heading) * z.block_rows + (count if heading == 1 else 0)
+            piece = pl.ds(begin, z.block_rows)
+            load = pltpu.make_async_copy(
+                states_in.at[heading, piece, :], states.at[heading, piece, :], sems.at[heading, stage]
+            )
+            load.start()
+            loads[stage, heading] = load
+    need(params, proj)
+    fill_rates(rates, params, count)
+    for heading in range(2):
+        first = heading * rows + rank
+        group_maps(maps, proj[first + count : first + 2 * count, :], heading, count)
+        diagonal_maps(diagonal, proj[first : first + count, :], heading, count)
+    for low in (low_two, products_two):
+        low[...] = jnp.zeros(low.shape, bf16)
+    blank = jnp.zeros((count, LANES), f32)
+    speeds = [rates[heading, :, cols(tile)] for heading, tile in z.pairs]
+
+    def scan(order, held, slot):
         waiting = list(held[: len(z.pairs)])
         totals = list(held[len(z.pairs) :])
-        leaves = [maps[heading, group_of(order, 1 - heading)] for heading in range(2)]
-        for ahead in range(count):
-            for heading in range(2):
-                inner = ahead if heading == 1 else count - 1 - ahead
-                at = group_of(order, 1 - heading) * count + inner
+        leaves = [maps[heading, sweep.group(order, heading)] for heading in range(2)]
+        for heading in range(2):
+            for ahead in range(count):
+                inner = sweep.inner(ahead, heading)
+                at = sweep.group(order, heading) * count + inner
                 prior = pl.multiple_of((at + (0 if heading == 0 else 1)) * count, count)
                 leave = jnp.broadcast_to(leaves[heading][:, inner : inner + 1], (count, LANES))
                 here = slice(inner * count, (inner + 1) * count)
                 for tile in range(tiles):
                     number = heading * tiles + tile
                     size = z.row(far_step, heading, tile, at)
-                    decay = jnp.exp2(size * rates2[heading, :, cols(tile)])
+                    decay = jnp.exp2(size * speeds[number])
                     grad = leave * z.row(grad_y, 0, tile, at) + waiting[number]
                     lead = decay * grad
                     waiting[number] = lead
-                    slope = lead * states[heading, pl.ds(prior, count), cols(tile)]
+                    slope = lead * states[heading, pl.ds(prior, count), cols(tile)].astype(f32)
                     totals[number] = totals[number] + slope * size
-                    products[heading, here, cols(tile)] = (slope * rates[heading, :, cols(tile)]).astype(bf16)
-                    low[heading, here, cols(tile)] = grad.astype(bf16)
+                    products[slot][heading, here, cols(tile)] = (slope * speeds[number]).astype(bf16)
+                    lows[slot][heading, here, cols(tile)] = grad.astype(bf16)
         return tuple(waiting + totals)
 
     lane = lax.broadcasted_iota(jnp.int32, (count, count * count), 1)
     row = lax.broadcasted_iota(jnp.int32, (count, count * count), 0)
     ones = jnp.where(lane // count == row, 1.0, 0.0).astype(bf16)
 
-    def post_backward(order, low, products):
+    def post(order, slot):
         for heading in range(2):
-            group = group_of(order, 1 - heading)
-            left = low[heading]
-            gathered[heading, group] = gather_states(left, inflow_low[heading, rows_of(group), :], count)
-            result[heading, rows_of(group), :] = weigh_states(
+            group = sweep.group(order, heading)
+            left = lows[slot][heading]
+            gathered[heading, group] = gather_states(left, inflow_low[heading, sweep.rows(group), :], count)
+            result[heading, sweep.rows(group), :] = weigh_states(
                 left, diagonal[heading, group].reshape(2 * count, count * count)
             )
-            decayed[heading, rows_of(group), :] = dot(ones, products[heading], NN)
-
-    def backward(index, held):
-        order = 2 * index
-        post_backward(jnp.maximum(order - 1, 0), low_two.at[0], low_two.at[1])
-        held = run_backward(order, held, low_one.at[0], low_one.at[1])
-        post_backward(order, low_one.at[0], low_one.at[1])
-        return run_backward(order + 1, held, low_two.at[0], low_two.at[1])
-
-    held = lax.fori_loop(0, groups // 2, backward, (blank,) * (2 * len(z.pairs)))
-    post_backward(groups - 1, low_two.at[0], low_two.at[1])
+            decayed[heading, sweep.rows(group), :] = dot(ones, products[slot][heading], NN)
+
+    def between(stage, before):
+        if before:
+            if stage == 0:
+                need(far_step, grad_y, inflow_low)
+            for heading in range(2):
+                loads[stage, heading].wait()
+
+    held = sweep.run(z, (blank,) * (2 * len(z.pairs)), scan, post, between)
     for number, (heading, tile) in enumerate(z.pairs):
-        slopes = held[len(z.pairs) + number] * rates[heading, :, cols(tile)]
+        slopes = held[len(z.pairs) + number] / LOG2E
         for n in range(count):
-            grad_chan[3 + n, heading : heading + 1, cols(tile)] = slopes[n : n + 1]
+            grad_chan[3 + n, heading : heading + 1, cols(tile)] = slopes[n : n + 1] * -jnp.exp(
+                params[3 + n, heading : heading + 1, cols(tile)]
+            )
+    need()
     for heading in range(2):
-        store_gathered(heading * rows + rank, heading)
+        first = heading * rows + rank
+        store_gathered(grad_part, first, gathered, heading, z)
+        grad_part[first + count : first + 2 * count, :] = grad_maps[
+            heading * count : (heading + 1) * count, :
+        ]
 
     for tile in range(tiles):
 
@@ -470,48 +555,70 @@
     save(grad_act)
     for heading in range(2):
         grad_chan[0, heading : heading + 1, :] = jnp.zeros((1, chans), f32)
+        grad_chan[2, heading : heading + 1, :] = skips[heading : heading + 1, :]
         grad_pre = pre_step[heading]
         grad_part[heading * rows : heading * rows + rank, :] = dot3(w_dt[heading], grad_pre, NT)
         grad_dt[heading] = dot3(proj[heading * rows : heading * rows + rank, :], grad_pre, NN)
 
 
-def scan_call(args, sizes, early_rows, half_width, limit=52):
+def forward_call(args, sizes, early_rows, half_width, kept, limit=30):
     z = sizes
     square = (z.tokens, z.chans)
     both = (2,) + square
-    flat = pltpu.VMEM((2 * z.tiles * z.tokens, LANES), f32)
+    flat = (2 * z.tiles * z.tokens, LANES)
     groups = z.tokens // z.count
     squared = z.count * z.count
+    states = (2, (z.tokens + 1) * z.count, z.chans)
+    slot = pltpu.VMEM((2, squared, z.chans), bf16)
     return call(
-        scan_kernel,
+        forward_kernel,
+        at("m", shape(states, bf16))
+        + at(
+            "h", shape((2 * z.rows, z.tokens), f32), shape((2 * z.count, z.tokens), f32), shape((8, z.chans), f32),
+            shape(flat, f32), shape((z.tiles * z.tokens, LANES), f32), shape(both, f32), shape(both, bf16),
+            shape(square, bf16),
+        )
+        + at("x", shape((early_rows, LANES), bf16), shape((half_width, z.tokens), f32))
+        + at("h", shape((half_width, z.tokens), f32)),
+        args,
+        [
+            pltpu.VMEM(square, f32), pltpu.VMEM(flat, f32), pltpu.VMEM(square, bf16), pltpu.VMEM(both, f32),
+            pltpu.VMEM(square, bf16), pltpu.VMEM((2, groups, z.count, LANES), f32),
+            pltpu.VMEM((2, groups, 2, z.count, squared), bf16), pltpu.VMEM((2, groups, z.count, z.count), f32),
+            pltpu.VMEM(states, bf16), slot, slot, pltpu.VMEM((2, z.count, z.chans), f32),
+            pltpu.SemaphoreType.DMA((2, z.blocks)),
+        ],
+        limit=limit, micros=15, kept=kept,
+    )
+
+
+def backward_call(args, sizes, limit=30):
+    z = sizes
+    square = (z.tokens, z.chans)
+    both = (2,) + square
+    groups = z.tokens // z.count
+    squared = z.count * z.count
+    slot = pltpu.VMEM((2, squared, z.chans), bf16)
+    return call(
+        backward_kernel,
         at(
-            "x", shape((2 * z.rows, z.tokens), f32), shape((early_rows, LANES), bf16),
-            shape((half_width, z.tokens), f32),
-        )
-        + at(
-            "h", shape((half_width, z.tokens), f32), shape(both, f32), shape((2, z.rank, z.chans), f32),
-            shape((3 + z.count, 2, z.chans), f32), shape(square, bf16),
+            "x", shape((2 * z.rows, z.tokens), f32), shape(both, f32), shape((2, z.rank, z.chans), f32),
+            shape((3 + z.count, 2, z.chans), f32),
         ),
         args,
         [
-            pltpu.VMEM((2 * z.rows, z.tokens), f32), pltpu.VMEM(both, f32), pltpu.VMEM(square, f32),
-            flat, flat, pltpu.VMEM((z.tiles * z.tokens, LANES), f32), pltpu.VMEM(square, bf16),
-            pltpu.VMEM(both, f32), pltpu.VMEM(both, f32), pltpu.VMEM(square, bf16),
-            pltpu.VMEM((2, groups, z.count, LANES), f32),
-            pltpu.VMEM((2, groups, 2, z.count, squared), bf16),
-            pltpu.VMEM((2, groups, z.count, z.count), f32),
-            pltpu.VMEM((2, (z.tokens + 1) * z.count, z.chans), f32),
-            pltpu.VMEM((2, 2, squared, z.chans), bf16), pltpu.VMEM((2, 2, squared, z.chans), bf16),
-            pltpu.VMEM((2, z.count, z.chans), f32), pltpu.VMEM((2, z.count, z.chans), f32),
-            pltpu.VMEM(both, bf16),
+            pltpu.VMEM(both, f32), pltpu.VMEM(both, f32), pltpu.VMEM((2, groups, z.count, LANES), f32),
+            pltpu.VMEM((2, groups, 2, z.count, squared), bf16), pltpu.VMEM((2, groups, z.count, z.count), f32),
+            pltpu.VMEM((2, (z.tokens + 1) * z.count, z.chans), bf16), slot, slot, slot, slot,
+            pltpu.VMEM((2, z.count, z.chans), f32), pltpu.SemaphoreType.DMA((2, z.blocks)),
         ],
-        limit=limit, micros=30,
+        limit=limit, micros=15,
     )
 
 
 def back_kernel(
-    own_part, far_part, grad_act, conv_pre, mixing, gate_low, normed, low_in, seg, w_xp, taps, hid, gain,
-    grad_dt, grad_chan, core,
+    own_part, far_part, seg, w_xp, taps, mixing, conv_pre, grad_act, grad_chan, normed, gate_low,
+    low_in, hid, gain, grad_dt, core,
     sums_out, in_own, in_far,
     padded, gpad, sgpad, mixed_low, small, act_low,
     *, need, save,
@@ -542,7 +649,7 @@
         gpad[heading, pl.ds(8, tokens), :] = dot(part, w_xp[heading].astype(bf16), TN)
 
     blank = jnp.zeros((8, chans), f32)
-    need()
+    need(taps, conv_pre, grad_act, grad_chan)
 
     def through_conv(start, held):
         here = pl.ds(start, ROWS)
@@ -611,6 +718,32 @@
             ].astype(bf16)
             base_row += values.shape[0]
 
+    need()
+    partial = dot(mixed_low[...], low_in[0], NT) + dot(gate_low[...], low_in[1], NT)
+    padded[pl.ds(8, tokens), :] = partial
+
+    gain_row = gain[...].reshape(1, width)
+
+    def gains(start, held):
+        here = pl.ds(start, ROWS)
+        source = hid[here, :].astype(f32)
+        scale = lax.rsqrt(jnp.sum(source * source, axis=1, keepdims=True) / width + norm_eps)
+        inside = pl.ds(pl.multiple_of(start + 8, 8), ROWS)
+        grad = padded[inside, :]
+        padded[inside, :] = grad * gain_row
+        return held + fold(grad * source * scale)
+
+    gain_sum = each_rows(tokens, gains, jnp.zeros((8, width), f32))
+    small[46:47, :] = jnp.sum(gain_sum, axis=0, keepdims=True)
+    weighted = padded[pl.ds(8, tokens), :]
+    products = weighted * hid[...].astype(f32)
+    turned = weighted.T
+    row_dot = dot(jnp.ones((8, width), f32), products, NT, HIGH)
+    in_own[0:half_width, :] = jnp.where(me == 0, turned[:half_width], turned[half_width:])
+    in_far[0:half_width, :] = jnp.where(me == 0, turned[half_width:], turned[:half_width])
+    in_own[pl.ds(half_width, 8), :] = row_dot
+    in_far[pl.ds(half_width, 8), :] = row_dot
+    save(in_own)
     put(dot(normed[...], mixed_low[...], TN))
     put(
         jnp.concatenate(
@@ -623,33 +756,8 @@
     )
     put(jnp.concatenate([grad_dt[0], grad_dt[1]], axis=0))
 
-    partial = dot(mixed_low[...], low_in[0], NT) + dot(gate_low[...], low_in[1], NT)
-    padded[pl.ds(8, tokens), :] = partial
-
-    gain_row = gain[...].reshape(1, width)
-
-    def gains(start, held):
-        here = pl.ds(start, ROWS)
-        source = hid[here, :].astype(f32)
-        scale = lax.rsqrt(jnp.sum(source * source, axis=1, keepdims=True) / width + norm_eps)
-        inside = pl.ds(pl.multiple_of(start + 8, 8), ROWS)
-        grad = padded[inside, :]
-        padded[inside, :] = grad * gain_row
-        return held + fold(grad * source * scale)
-
-    gain_sum = each_rows(tokens, gains, jnp.zeros((8, width), f32))
-    small[46:47, :] = jnp.sum(gain_sum, axis=0, keepdims=True)
     put(small[...])
     sums_out[base_row:, :] = jnp.zeros((sums_out.shape[0] - base_row, LANES), bf16)
-
-    weighted = padded[pl.ds(8, tokens), :]
-    products = weighted * hid[...].astype(f32)
-    turned = weighted.T
-    row_dot = dot(jnp.ones((8, width), f32), products, NT, HIGH)
-    in_own[0:half_width, :] = jnp.where(me == 0, turned[:half_width], turned[half_width:])
-    in_far[0:half_width, :] = jnp.where(me == 0, turned[half_width:], turned[:half_width])
-    in_own[pl.ds(half_width, 8), :] = row_dot
-    in_far[pl.ds(half_width, 8), :] = row_dot
 
 
 def outputs_kernel(hid, cot_own, out_own, out_far, in_own, in_far, core, output, input_grad, *, need, save):
@@ -674,12 +782,8 @@
 def lamb_moments(weight, grad, first, second):
     first_new = beta_one * first + (1.0 - beta_one) * grad
     second_new = beta_two * second + (1.0 - beta_two) * grad * grad
-    update = (
-        first_new
-        / (1.0 - beta_one**STEP)
-        / (jnp.sqrt(second_new / (1.0 - beta_two**STEP)) + adam_eps)
-        + decay_rate * weight
-    )
+    root = jnp.sqrt(second_new * (1.0 / (1.0 - beta_two**STEP)))
+    update = first_new * (1.0 / (1.0 - beta_one**STEP)) / (root + adam_eps) + decay_rate * weight
     return (first_new, second_new, update)
 
 
@@ -709,15 +813,15 @@
     return rows_sum(each_rows(length, step, jnp.zeros((8, update.shape[1]), f32)))
 
 
-def half_update(half, sums, base, stride, weights, a_ref, b_ref, x_ref, y_ref, u_ref):
-    length, _, chans = weights.shape
+def half_update(sums, base, stride, weights, a_ref, b_ref, x_ref, y_ref, u_ref):
+    length, chans = weights.shape
     zero = jnp.zeros((8, chans), f32)
 
     def step(start, kept):
         here = pl.ds(start, ROWS)
         grad = fetch(sums, base, stride, start, ROWS, chans // LANES)
-        weight = weights[here, half, :]
-        first, second, update = lamb_moments(weight, grad, a_ref[here, half, :], b_ref[here, half, :])
+        weight = weights[here, :]
+        first, second, update = lamb_moments(weight, grad, a_ref[here, :], b_ref[here, :])
         x_ref[here, :] = first
         y_ref[here, :] = second
         u_ref[here, :] = update
@@ -729,11 +833,11 @@
 
 
 def early_kernel(
-    sums, w_in, a_in, b_in, w_out, a_out, b_out,
+    sums, w_out, a_out, b_out, w_gate, a_gate, b_gate,
     x_out, y_out, x_gate, y_gate, u_gate, u_out, norms, stats,
     *, need, save,
 ):
-    width, _, chans = w_in.shape
+    width, chans = w_gate.shape
     tiles = width // LANES
     norms[...] = jnp.zeros(norms.shape, f32)
     zero = jnp.zeros((8, width), f32)
@@ -755,7 +859,7 @@
     save(x_out, y_out, u_out)
     need()
     weight_sq, update_sq, total = half_update(
-        1, sums, chans * tiles, width, w_in, a_in, b_in, x_gate, y_gate, u_gate
+        sums, chans * tiles, width, w_gate, a_gate, b_gate, x_gate, y_gate, u_gate
     )
     norms[0:1, :] = lanes_sum(weight_sq)
     norms[6:7, :] = lanes_sum(update_sq)
@@ -773,34 +877,18 @@
 
 
 def late_kernel(
-    sums, x_gate, y_gate, early_norms, early_stats,
-    w_in, a_in, b_in, w_xp, a_xp, b_xp, w_dt, a_dt, b_dt, w_cv, a_cv, b_cv, w_cp, a_cp, b_cp,
-    x_in, y_in, x_xp, y_xp, x_dt, y_dt, x_cv, y_cv, x_cp, y_cp,
-    u_mix, u_xp, u_dt, u_cv, u_cp, norms, stats,
-    x_mix, y_mix,
-    *, need, save,
+    sums, early_norms, early_stats, *rest, need, save
 ):
-    width, _, chans = w_in.shape
+    small_in, (a_mix, b_mix), rest = rest[:8], rest[8:10], rest[10:]
+    x_mix, y_mix, x_xp, y_xp, x_dt, y_dt, x_cv, y_cv, x_cp, y_cp, *rest = rest
+    u_mix, u_xp, u_dt, u_cv, u_cp, norms, stats, w_xp, w_dt, w_cv, w_cp, w_mix, *_ = rest
+    a_xp, b_xp, a_dt, b_dt, a_cv, b_cv, a_cp, b_cp = small_in
+    width, chans = w_mix.shape
     tiles = chans // LANES
-    need(early_norms, early_stats, w_in, a_in, b_in)
+    base = tiles * width
+    need(early_norms, early_stats, *small_in, w_xp, w_dt, w_cv, w_cp)
     norms[...] = early_norms[...]
     stats[...] = early_stats[...]
-    weight_sq, update_sq, total = half_update(
-        0, sums, 0, width, w_in, a_in, b_in, x_mix, y_mix, u_mix
-    )
-    save(u_mix)
-    need()
-    x_in[:, 0, :] = x_mix[...]
-    x_in[:, 1, :] = x_gate[...]
-    y_in[:, 0, :] = y_mix[...]
-    y_in[:, 1, :] = y_gate[...]
-    save(x_in, y_in)
-    norms[0:1, :] += lanes_sum(weight_sq)
-    norms[6:7, :] += lanes_sum(update_sq)
-    mix_mean = rows_sum(total) / width
-    stats[4:5, :] = mix_mean
-    stats[5:6, :] = spread_of(u_mix, mix_mean, width)
-    base = tiles * width
 
     def small(place, items, weight, a_ref, b_ref, x_ref, y_ref, u_ref):
         weight_sq, update_sq = jnp.zeros((1, LANES), f32), jnp.zeros((1, LANES), f32)
@@ -831,64 +919,59 @@
     small(5, items, w_cp, a_cp, b_cp, x_cp, y_cp, u_cp)
     for tile in range(tiles):
         norms[12 + tile : 13 + tile, :] = grads[46:47, cols(tile)]
+    save()
+    need(a_mix, b_mix, w_mix)
+    weight_sq, update_sq, total = half_update(
+        sums, 0, width, w_mix, a_mix, b_mix, x_mix, y_mix, u_mix
+    )
+    norms[0:1, :] += lanes_sum(weight_sq)
+    norms[6:7, :] += lanes_sum(update_sq)
+    mix_mean = rows_sum(total) / width
+    stats[4:5, :] = mix_mean
+    stats[5:6, :] = spread_of(u_mix, mix_mean, width)
 
 
 def apply_kernel(
     norms_own, norms_far, stats,
-    w_in, w_out, w_xp, w_dt, w_cv, w_cp,
+    w_mix, w_gate, w_out, w_xp, w_dt, w_cv, w_cp,
     u_mix, u_gate, u_out, u_xp, u_dt, u_cv, u_cp,
-    gain, gain_first, gain_second, core,
+    gain, gain_first, gain_second, x_mix, y_mix, core, x_given, y_given,
     n_in, c_in, n_out, c_out, n_xp, c_xp, n_dt, c_dt, n_cv, c_cv, n_cp, c_cp,
-    g_first, g_second, g_new, g_copy, norms_out, stats_out,
+    g_first, g_second, g_new, g_copy, norms_out, stats_out, x_in, y_in,
+    sems,
     *, need, save,
 ):
-    width, _, chans = w_in.shape
+    width, chans = w_mix.shape
+    moves = [
+        pltpu.make_async_copy(held, target.at[:, 0, :], sems.at[number])
+        for number, (held, target) in enumerate(((x_mix, x_in), (y_mix, y_in)))
+    ]
+    for move in moves:
+        move.start()
     half_width = g_new.shape[0]
     me = core[0]
-    need(norms_own, gain, stats)
     totals = norms_own[...] + norms_far[...]
-    gain_grad = jnp.concatenate(
-        [totals[12 + tile : 13 + tile, :] for tile in range(width // LANES)], axis=1
-    )
-    gain_row = gain[...].reshape(1, width)
-    first, second, update = lamb_moments(gain_row, gain_grad, gain_first[...], gain_second[...])
     sums = jnp.sum(totals, axis=1, keepdims=True)
-    weight_sq = [jnp.sum(gain_row * gain_row, axis=1, keepdims=True)] + [
-        sums[place : place + 1] for place in range(6)
-    ]
-    update_sq = [jnp.sum(update * update, axis=1, keepdims=True)] + [
-        sums[6 + place : 7 + place] for place in range(6)
-    ]
-    scales = []
-    for place in range(7):
-        weight_norm = jnp.sqrt(weight_sq[place])
-        update_norm = jnp.sqrt(update_sq[place])
+    scales = [None]
+    for place in range(6):
+        weight_norm = jnp.sqrt(sums[place : place + 1])
+        update_norm = jnp.sqrt(sums[6 + place : 7 + place])
         scales.append(learn_rate * weight_norm / (update_norm + adam_eps))
-        norms_out[0:1, place : place + 1] = weight_norm
-        norms_out[1:2, place : place + 1] = update_norm
-    fresh = gain_row - scales[0] * update
-
-    def own(row):
-        return jnp.where(me == 0, row[:, :half_width], row[:, half_width:]).reshape(half_width)
-
-    g_first[...] = own(first)
-    g_second[...] = own(second)
-    g_new[...] = own(fresh)
-    g_copy[...] = own(fresh).astype(bf16)
-
-    need(w_in, u_mix, u_gate)
+        norms_out[0:1, place + 1 : place + 2] = weight_norm
+        norms_out[1:2, place + 1 : place + 2] = update_norm
+
+    need(w_mix, w_gate)
 
     def one_in(start, held):
         here = pl.ds(start, ROWS)
-        for half, change in ((0, u_mix), (1, u_gate)):
-            fresh = w_in[here, half, :] - scales[1] * change[here, :]
-            n_in[here, half, :] = fresh
+        for half, weight, change in ((0, w_mix, u_mix), (1, w_gate, u_gate)):
+            fresh = weight[here, :] - scales[1] * change[here, :]
+            n_in[half, here, :] = fresh
             c_in[here, half, :] = fresh.astype(bf16)
         return held
 
     each_rows(width, one_in, 0)
     save(n_in, c_in)
-    need()
 
     def one_out(start, held):
         here = pl.ds(start, ROWS)
@@ -899,6 +982,25 @@
 
     each_rows(chans, one_out, 0)
     save(n_out, c_out)
+    need()
+    gain_grad = jnp.concatenate(
+        [totals[12 + tile : 13 + tile, :] for tile in range(width // LANES)], axis=1
+    )
+    gain_row = gain[...].reshape(1, width)
+    first, second, update = lamb_moments(gain_row, gain_grad, gain_first[...], gain_second[...])
+    weight_norm = jnp.sqrt(jnp.sum(gain_row * gain_row, axis=1, keepdims=True))
+    update_norm = jnp.sqrt(jnp.sum(update * update, axis=1, keepdims=True))
+    norms_out[0:1, 0:1] = weight_norm
+    norms_out[1:2, 0:1] = update_norm
+    fresh = gain_row - learn_rate * weight_norm / (update_norm + adam_eps) * update
+
+    def own(row):
+        return jnp.where(me == 0, row[:, :half_width], row[:, half_width:]).reshape(half_width)
+
+    g_first[...] = own(first)
+    g_second[...] = own(second)
+    g_new[...] = own(fresh)
+    g_copy[...] = own(fresh).astype(bf16)
     for place, weight, change, fresh_ref, copy in (
         (3, w_xp, u_xp, n_xp, c_xp),
         (4, w_dt, u_dt, n_dt, c_dt),
@@ -922,6 +1024,8 @@
         spread = spread + scale * scale * squares + width * gap * gap
     stats_out[0:1, :] = mean
     stats_out[1:2, :] = spread / (3.0 * width)
+    for move in moves:
+        move.wait()
 
 
 def join_kernel(pieces, copies, *, need, save):
@@ -943,15 +1047,27 @@
     return copies.reshape(-1, LANES)
 
 
-def call(kernel, outs, args, scratch=(), limit=32, micros=1):
-    given = [array for array, _ in args]
-    kinds = [kind for _, kind in args]
+def call(kernel, outs, args, scratch=(), limit=32, micros=1, passed=(), kept=(), aliases=None):
+    given = [array for array, _ in args] + [array for array, _ in passed]
+    kinds = [kind for _, kind in args] + ["m"] * len(passed)
+    n_own = len(outs)
+    outs = list(outs)
+    for array, kind in passed:
+        dims = array.shape if kind == "h" else (array.shape[0], array.shape[-1])
+        outs += at("x", shape(dims, array.dtype))
+    outs += at("m", *[shape(given[place].shape, given[place].dtype) for place in kept])
     out_kinds = [kind for _, kind in outs]
-    fetched = [place for place, kind in enumerate(kinds) if kind == "h"]
-    stored = [place for place, kind in enumerate(out_kinds) if kind == "h"]
-    staging = [pltpu.VMEM(given[place].shape, given[place].dtype) for place in fetched]
-    staging += [pltpu.VMEM(outs[place][0].shape, outs[place][0].dtype) for place in stored]
-    moves = max(1, len(staging))
+    fetched = [place for place, kind in enumerate(kinds) if kind in "h01"]
+    stored = [place for place, kind in enumerate(out_kinds) if kind in "h12"]
+
+    def staged(array, kind):
+        rows, columns = array.shape[0], array.shape[-1]
+        dims = {"h": array.shape, "2": (2, rows, columns)}.get(kind, (rows, columns))
+        return pltpu.VMEM(dims, array.dtype)
+
+    staging = [staged(given[place], kinds[place]) for place in fetched]
+    staging += [staged(outs[place][0], out_kinds[place]) for place in stored]
+    moves = max(1, 2 * len(staging) + len(passed) + len(kept))
 
     def body(*refs):
         ins = list(refs[: len(given)])
@@ -960,41 +1076,73 @@
         stage, sems, own = rest[: len(staging)], rest[len(staging)], rest[len(staging) + 1 :]
         loads, saves = {}, {}
         for number, place in enumerate(fetched):
-            loads[id(stage[number])] = pltpu.make_async_copy(ins[place], stage[number], sems.at[number])
+            source = ins[place] if kinds[place] == "h" else ins[place].at[:, int(kinds[place]), :]
+            loads[id(stage[number])] = pltpu.make_async_copy(source, stage[number], sems.at[number])
             ins[place] = stage[number]
         for load in loads.values():
             load.start()
         for number, place in enumerate(stored, len(fetched)):
-            saves[id(stage[number])] = pltpu.make_async_copy(stage[number], results[place], sems.at[number])
-            results[place] = stage[number]
+            held, target, kind = stage[number], results[place], out_kinds[place]
+            parts = [(held, target)]
+            if kind == "1":
+                parts = [(held, target.at[:, 1, :])]
+            if kind == "2":
+                parts = [(held.at[half], target.at[:, half, :]) for half in range(2)]
+            saves[id(held)] = [
+                pltpu.make_async_copy(*pair, sems.at[moves - 1 - 2 * (number - len(fetched)) - half]) for half, pair in enumerate(parts)
+            ]
+            results[place] = held
+        follow = []
+        for number in range(len(passed)):
+            held = results[n_own + number]
+            source, kind = ins[len(args) + number], passed[number][1]
+            source = source if kind == "h" else source.at[:, int(kind), :]
+            loads[id(held)] = pltpu.make_async_copy(source, held, sems.at[len(staging) + number])
+            follow.append(id(held))
         begun = []
+        for number, place in enumerate(kept):
+            begun.append(
+                pltpu.make_async_copy(
+                    ins[place], results[n_own + len(passed) + number],
+                    sems.at[len(staging) + len(passed) + number],
+                )
+            )
+            begun[-1].start()
 
         def need(*wanted):
-            for key in [id(ref) for ref in wanted] or list(loads):
+            keys = [id(ref) for ref in wanted] or list(loads)
+            for key in keys:
+                if key in loads and key not in follow:
+                    loads.pop(key).wait()
+            while follow:
+                loads[follow.pop(0)].start()
+            for key in keys:
                 if key in loads:
                     loads.pop(key).wait()
 
         def save(*ready):
             for key in [id(ref) for ref in ready] or list(saves):
-                if key in saves:
-                    begun.append(saves.pop(key))
-                    begun[-1].start()
-
-        kernel(*ins, *results, *own, need=need, save=save)
+                for move in saves.pop(key, ()):
+                    move.start()
+                    begun.append(move)
+
+        kernel(*ins[: len(args)], *results[: n_own + len(passed)], *own, need=need, save=save)
         need()
         save()
         for move in begun:
             move.wait()
 
-    spaces = {"x": pltpu.VMEM, "h": pltpu.HBM, "m": pltpu.HBM, "s": pltpu.SMEM}
+    spaces = {"x": pltpu.VMEM, "s": pltpu.SMEM}
     placed = [
-        pltpu.with_memory_space_constraint(array, pltpu.HBM) if kind in "hm" else array for array, kind in args
+        pltpu.with_memory_space_constraint(array, pltpu.HBM) if kind in "hm01" else array
+        for array, kind in zip(given, kinds)
     ]
     return pl.pallas_call(
         body,
-        out_shape=[pltpu.HBM(out.shape, out.dtype) if kind in "hm" else out for out, kind in outs],
-        in_specs=[pl.BlockSpec(memory_space=spaces[kind]) for kind in kinds],
-        out_specs=[pl.BlockSpec(memory_space=spaces[kind]) for kind in out_kinds],
+        out_shape=[out if kind == "x" else pltpu.HBM(out.shape, out.dtype) for out, kind in outs],
+        in_specs=[pl.BlockSpec(memory_space=spaces.get(kind, pltpu.HBM)) for kind in kinds],
+        out_specs=[pl.BlockSpec(memory_space=spaces.get(kind, pltpu.HBM)) for kind in out_kinds],
+        input_output_aliases=aliases or {},
         scratch_shapes=[*staging, pltpu.SemaphoreType.DMA((moves,)), *scratch],
         compiler_params=pltpu.CompilerParams(vmem_limit_bytes=limit * MB),
         cost_estimate=pl.CostEstimate(flops=micros * 10**9, bytes_accessed=MB, transcendentals=0),
@@ -1055,26 +1203,37 @@
 
     mixing, gate, conv_pre, part, normed, low_in, same = call(
         front_kernel,
-        at("h", shape(square, f32), shape(square, f32), shape((2,) + square, f32))
-        + at("x", shape((2 * rows, tokens), f32))
+        at("h", shape(square, f32))
         + at(
-            "h", shape((tokens, width), bf16), shape((2, width, chans), bf16),
-            shape((2, tokens, LANES), f32),
-        ),
-        at("h", hidden_in, segment_ids, norm_gain, in_weight, conv_weight, w_cp, w_xp),
+            "x", shape(square, f32), shape((2,) + square, f32), shape((2 * rows, tokens), f32),
+            shape((tokens, width), bf16),
+        )
+        + at("h", shape((2, width, chans), bf16))
+        + at("x", shape((2, tokens, LANES), f32)),
+        at("h", hidden_in, norm_gain) + at("0", in_weight) + at("1", in_weight)
+        + at("h", segment_ids, conv_weight, w_cp, w_xp),
         [pltpu.VMEM((tokens + 16, chans), f32), pltpu.VMEM((tokens + 16, LANES), f32)],
-        limit=16, micros=7,
+        limit=14, micros=7,
     )
     part_far = swap(part)
     early_rows = padded_rows(tiles * width + (width // LANES) * chans)
-    grad_part, early, out_send, out_own, grad_act, grad_dt, grad_chan, gate_low = scan_call(
-        at("x", part, part_far) + at("h", conv_pre, gate, same, cot_own) + at("x", cot_far)
-        + at("h", out_weight, dtproj_weight, w_cp, normed) + smem,
-        z, early_rows, half_width,
+    (
+        states, proj, grad_maps, skips, far_step, grad_y, pre_step, inflow_low, gate_low, early, out_send, out_own,
+        conv_kept, normed_kept,
+    ) = forward_call(
+        at("x", part, part_far) + at("h", w_cp, dtproj_weight, cot_own) + at("x", cot_far) + at("h", out_weight)
+        + at("x", conv_pre, gate, same, normed) + smem,
+        z, early_rows, half_width, (7, 10),
     )
     early_pieces = send_pieces(early, dp)
+    grad_part, grad_act, grad_dt, grad_chan = backward_call(
+        at("m", states) + at("h", w_cp, proj, far_step, grad_y, inflow_low, pre_step, conv_kept)
+        + at("h", grad_maps, skips, dtproj_weight),
+        z,
+    )
+    early_copies, grad_part = lax.optimization_barrier((join_pieces(early_pieces), grad_part))
+    early_sums = lax.all_to_all(early_copies, "dp", 0, 0, tiled=True)
     grad_far = swap(grad_part)
-    early_sums = lax.all_to_all(join_pieces(early_pieces), "dp", 0, 0, tiled=True)
     out_far = swap(out_send)
     late_rows = padded_rows(tiles * (width + 2 * rows + 2 * rank + 48))
     late, in_own, in_send = call(
@@ -1083,17 +1242,18 @@
         + at("h", shape((half_width + 8, tokens), f32))
         + at("x", shape((half_width + 8, tokens), f32)),
         at("x", grad_part, grad_far)
-        + at("h", grad_act, conv_pre, mixing, gate_low, normed, low_in)
-        + at("h", segment_ids, w_xp, conv_weight, hidden_in, norm_gain, grad_dt, grad_chan)
+        + at("h", segment_ids, w_xp, conv_weight, mixing, conv_kept) + at("x", grad_act, grad_chan)
+        + at("h", normed_kept, gate_low, low_in, hidden_in, norm_gain) + at("x", grad_dt)
         + smem,
         [
             pltpu.VMEM((tokens + 16, chans), f32), pltpu.VMEM((2, tokens + 16, chans), f32),
             pltpu.VMEM((tokens + 16, LANES), f32), pltpu.VMEM(square, bf16),
             pltpu.VMEM((48, chans), f32), pltpu.VMEM((2,) + square, bf16),
         ],
-        limit=20, micros=8,
+        limit=20, micros=2,
     )
     in_far = swap(in_send)
+    late, early_sums = lax.optimization_barrier((late, early_sums))
     late_pieces = send_pieces(late, dp)
     output, input_grad = call(
         outputs_kernel,
@@ -1106,58 +1266,57 @@
     for group in (firsts, seconds):
         group[0], group[3] = flip(group[0]), turn(group[3])
     weights = [w_xp, dtproj_weight, conv_weight, w_cp]
-    small = [tensor for trio in zip(weights, firsts, seconds) for tensor in trio]
     half = shape((width, chans), f32)
     whole_in, whole_out = shape(in_weight.shape, f32), shape(out_weight.shape, f32)
-    x_out, y_out, x_gate, y_gate, u_gate, u_out, early_norms, early_stats = call(
+    x_out, y_out, x_in, y_in, u_gate, u_out, early_norms, early_stats = call(
         early_kernel,
-        at(
-            "h", whole_out, whole_out, half, half, half, whole_out, shape((16, LANES), f32),
-            shape((8, chans), f32),
-        ),
-        at("x", early_sums)
-        + at(
-            "h", in_weight, first_in_weight, second_in_weight, out_weight, first_out_weight,
-            second_out_weight,
-        ),
-        limit=24, micros=5,
-    )
-    late_sums = lax.all_to_all(join_pieces(late_pieces), "dp", 0, 0, tiled=True)
+        at("h", whole_out, whole_out) + at("1", whole_in, whole_in)
+        + at("h", half, whole_out, shape((16, LANES), f32), shape((8, chans), f32)),
+        at("x", early_sums) + at("h", out_weight, first_out_weight, second_out_weight)
+        + at("1", in_weight, first_in_weight, second_in_weight),
+        limit=12, micros=5,
+    )
+    late_copies, output, input_grad = lax.optimization_barrier((join_pieces(late_pieces), output, input_grad))
+    late_sums = lax.all_to_all(late_copies, "dp", 0, 0, tiled=True)
     shapes = [shape(tensor.shape, f32) for tensor in weights]
-    late_outs = [whole_in, whole_in]
+    late_outs = []
     for entry in shapes:
         late_outs += [entry, entry]
+    moments_in = [tensor for pair in zip(firsts, seconds) for tensor in pair]
     got = call(
         late_kernel,
-        at("h", *late_outs, half, *shapes)
-        + at("x", shape((16, LANES), f32))
-        + at("h", shape((8, chans), f32)),
-        at("x", late_sums)
-        + at("h", x_gate, y_gate, early_norms, early_stats, in_weight, first_in_weight, second_in_weight)
-        + at("h", *small),
-        [pltpu.VMEM((width, chans), f32), pltpu.VMEM((width, chans), f32)],
-        limit=24, micros=5,
-    )
-    moments, updates, norms, stats = got[:10], got[10:15], got[15], got[16]
+        at("x", half, half) + at("h", *late_outs)
+        + at("x", half, *shapes, shape((16, LANES), f32), shape((8, chans), f32)),
+        at("x", late_sums) + at("h", early_norms, early_stats, *moments_in)
+        + at("0", first_in_weight, second_in_weight),
+        limit=12, micros=5,
+        passed=at("h", *weights) + at("0", in_weight) + at("1", in_weight) + at("h", out_weight, u_gate, u_out),
+    )
+    moments, updates, norms, stats, kept = got[:10], got[10:15], got[15], got[16], got[17:]
+    kept_small, (kept_mix, kept_gate, kept_out, changed_gate, changed_out) = kept[0:4], kept[4:]
     norms_far = swap(norms)
     pairs = []
     for entry in [whole_in, whole_out, *shapes]:
         pairs += [entry, shape(entry.shape, bf16)]
     row = shape((half_width,), f32)
+    whole_low = shape(whole_in.shape, bf16)
     done = call(
         apply_kernel,
-        at(
-            "h", *pairs, row, row, row, shape((half_width,), bf16), shape((2, 7), f32),
+        at("2", whole_in) + at("h", whole_low)
+        + at(
+            "h", *pairs[2:], row, row, row, shape((half_width,), bf16), shape((2, 7), f32),
             shape((2, chans), f32),
-        ),
-        at("x", norms, norms_far)
-        + at("h", stats, in_weight, out_weight, *weights, updates[0], u_gate, u_out, *updates[1:])
-        + at("h", norm_gain) + at("x", moments_gain[0:1], moments_gain[1:2]) + smem,
-        limit=24, micros=5,
+        )
+        + at("m", whole_in, whole_in),
+        at("x", norms, norms_far, stats, kept_mix, kept_gate, kept_out, *kept_small, updates[0], changed_gate, changed_out, *updates[1:])
+        + at("h", norm_gain) + at("x", moments_gain[0:1], moments_gain[1:2], moments[0], moments[1])
+        + smem + at("m", x_in, y_in),
+        [pltpu.SemaphoreType.DMA((2,))],
+        limit=14, micros=5, aliases={23: 18, 24: 19},
     )
     flat = list(done[12:16])
-    firsts_out = [moments[0], x_out, *moments[2::2]]
-    seconds_out = [moments[1], y_out, *moments[3::2]]
+    firsts_out = [done[18], x_out, *moments[2::2]]
+    seconds_out = [done[19], y_out, *moments[3::2]]
     for place in range(6):
         entry = [firsts_out[place], seconds_out[place], done[2 * place], done[2 * place + 1]]
         if place == 2:

time: 132 us -> 116 us (0.88)
  waiting for transfers between devices: 38.5 us -> 26 us
  Pallas kernels: 70.2 us -> 63.7 us
  starting transfers between devices: 21.5 us -> 24.1 us
    all_to_all x2, waiting for transfers between devices: 18.7 us -> 10.7 us  [the longest x1 6.21 us: program(): late_sums = lax.all_to_all(late_copies, 'dp', 0, 0, tiled=True)]
    all_to_all x2, waiting for transfers between devices: 16.1 us -> 8.8 us  [send_pieces(): lax.all_to_all(values, 'dp', 0, 0, tiled=True).reshape(dp, chunk, LANES)]
    pallas_call x9 -> x10, Pallas kernels: 70.2 us -> 63.7 us  [call(): pl.pallas_call(body, out_shape=[out if kind == 'x' else pltpu.HBM(out.sha...]
    all_to_all x2, starting transfers between devices: 7.71 us -> 10.5 us  [the longest x1 6.75 us: program(): early_sums = lax.all_to_all(early_copies, 'dp', 0, 0, tiled=True)]
    ppermute x7, waiting for transfers between devices: 3.83 us -> 6.48 us  [swap(): return lax.ppermute(values, 'chan', [(0, 1), (1, 0)])]
  transfers between devices with their start and end apart: 11 -> 11, of which waited for: 7 -> 9; matrix products, arithmetic and copies ran while one was open for 0% -> 0% of each run, Pallas kernels for 21% -> 30%
where the time goes in v3:
time: 116 us; the launch traced here: 115 us
  Pallas kernels  63.7 us (55%)
  waiting for transfers between devices  26 us (22%)
  starting transfers between devices  24.1 us (21%)
    pallas_call x10, Pallas kernels, call(): pl.pallas_call(body, out_shape=[out if kind == 'x' else pltpu.HBM(out.sha...  63.7 us
    all_to_all x2, starting transfers between devices, send_pieces(): lax.all_to_all(values, 'dp', 0, 0, tiled=True).reshape(dp, chunk, LANES)  12.3 us
    all_to_all x2, waiting for transfers between devices, send_pieces(): lax.all_to_all(values, 'dp', 0, 0, tiled=True).reshape(dp, chunk, LANES)  8.8 us
    all_to_all x1, starting transfers between devices, program(): early_sums = lax.all_to_all(early_copies, 'dp', 0, 0, tiled=True)  6.75 us
    ppermute x7, waiting for transfers between devices, swap(): return lax.ppermute(values, 'chan', [(0, 1), (1, 0)])  6.48 us
    all_to_all x1, waiting for transfers between devices, program(): late_sums = lax.all_to_all(late_copies, 'dp', 0, 0, tiled=True)  6.21 us
    all_to_all x1, waiting for transfers between devices, program(): early_sums = lax.all_to_all(early_copies, 'dp', 0, 0, tiled=True)  4.51 us
    all_to_all x1, starting transfers between devices, program(): late_sums = lax.all_to_all(late_copies, 'dp', 0, 0, tiled=True)  3.73 us
  transfers between devices with their start and end apart: 11, of which 9 were waited for; matrix products, arithmetic and copies ran while one was open for 0% of the time, Pallas kernels for 30%

profile of v3, /device:TPU:0, one launch (start us, length us, event | category | flops | bytes accessed | tf_op | source)
XLA Modules:
  0.0 115.0 jit_solution(17177966209382494296)
XLA Ops:
  0.7 0.0 copy-start.2
  0.7 5.8 %shard_map.479 = (f32[384,384]{1,0:T(8,128)}, f32[384,384]{1,0:T(8,128)S(1)}, f32[2,384,384]{2,1,0:T(8,128)S(1)}, f32[112,384]{1,0:T(8,128)S(1)}, bf16[384,384]{...) custom-call(bf16[384,384]{1,0:T(8,128)(2,1)} %refs_0_.3, f32[384]{0:T(512)} %refs_17_.3, ...), custom_call_target="tpu_custom_call" | custom-call | flops 7000000000 | bytes 1048576 | tf_op jit(solution)/shard_map/pallas_call | solution.py:1140
  6.5 0.5 collective-permute-start
  7.0 0.0 copy-done.2
  7.0 0.1 collective-permute-start.1
  7.1 1.3 %collective-permute-done.1.refs_5_ = bf16[192,384]{1,0:T(8,128)(2,1)S(1)} collective-permute-done((bf16[192,384]{1,0:T(8,128)(2,1)S(1)}, bf16[192,384]{1,0:T(8,128)(2,1)S(1)}, u32[]{:S(2)}, u32[]{:S(2)}) %collective-permute-start.1) | collective-permute-done | bytes 147488 | tf_op jit(solution)/shard_map/ppermute | solution.py:1175
  8.4 0.0 collective-permute-done.refs_1_
  8.4 13.9 %shard_map.480 = (bf16[2,6160,384]{2,1,0:T(8,128)(2,1)}, f32[112,384]{1,0:T(8,128)}, f32[32,384]{1,0:T(8,128)}, f32[8,384]{1,0:T(8,128)}, f32[2304,128]{1,0:T(8,...) custom-call(f32[112,384]{1,0:T(8,128)S(1)} %get-tuple-element.123.re, ...), custom_call_target="tpu_custom_call" | custom-call | flops 15000000512 | bytes 1048576 | tf_op jit(solution)/shard_map/pallas_call | solution.py:1140
  22.3 8.1 %all-to-all-start = ((bf16[16,144,128]{2,1,0:T(8,128)(2,1)}), bf16[16,144,128]{2,1,0:T(8,128)(2,1)S(1)}, u32[]{:S(2)}, u32[]{:S(2)}) async-start(bf16[16,144,128]{2,1,0:T(8,128)(2,1)} %bitcast.4), calls=%async_computation | async-start | bytes 1179648 | tf_op jit(solution)/shard_map/all_to_all | solution.py:1042
  30.4 16.4 %shard_map.482 = (f32[112,384]{1,0:T(8,128)S(1)}, f32[2,384,384]{2,1,0:T(8,128)S(1)}, f32[2,24,384]{2,1,0:T(8,128)S(1)}, f32[19,2,384]{2,1,0:T(2,128)S(1)}) custom-call(bf16[2,6160,384]{2,1,0:T(8,128)(2,1)} %get-tuple-element.129.refs_0_, f32[19,2,384]{2,1,0:T(2,128)} %bitcast.45, f32[112,384]{1,0:T(8,128)} %get-tuple-element.130.refs_2_, ...), custom_call_target="tpu_custom_call" | custom-call | flops 15000000512 | bytes 1048576 | tf_op jit(solution)/shard_map/pallas_call | solution.py:1140
  46.8 0.2 all-to-all-done.refs_0_
  47.0 0.9 shard_map.481
  47.9 6.8 %all-to-all-start.1 = ((bf16[16,144,128]{2,1,0:T(8,128)(2,1)}), bf16[16,144,128]{2,1,0:T(8,128)(2,1)S(1)}, u32[]{:S(2)}, u32[]{:S(2)}) async-start(bf16[16,144,128]{2,1,0:T(8,128)(2,1)} %bitcast.6), calls=%async_computation.1 | async-start | bytes 1179648 | tf_op jit(solution)/shard_map/all_to_all | solution.py:1235
  54.7 0.1 collective-permute-start.2
  54.8 1.4 %collective-permute-done.2.refs_1_ = f32[112,384]{1,0:T(8,128)S(1)} collective-permute-done((f32[112,384]{1,0:T(8,128)S(1)}, f32[112,384]{1,0:T(8,128)S(1)}, u32[]{:S(2)}, u32[]{:S(2)}) %collective-permute-start.2) | collective-permute-done | bytes 172064 | tf_op jit(solution)/shard_map/ppermute | solution.py:1175
  56.2 10.2 %shard_map.483 = (bf16[1792,128]{1,0:T(8,128)(2,1)}, f32[200,384]{1,0:T(8,128)}, f32[200,384]{1,0:T(8,128)S(1)}) custom-call(f32[112,384]{1,0:T(8,128)S(1)} %get-tuple-element.139.refs_0_, f32[112,384]{1,0:T(8,128)S(1)} %collective-permute-done.2.refs_1_, s32[384]{0:T(512)} %refs_2_.4, f32[2,56,384]{2,1,0:T(8,128)} %bitcast.36, f32[2,4,384]{2,1,0:T(4,128)} %refs_15_.1, ...), custom_call_target="tpu_custom_call" | custom-call | flops 2000000000 | bytes 1048576 | tf_op jit(solution)/shard_map/pallas_call | solution.py:1140
  66.3 4.5 %all-to-all-done.1 = bf16[16,144,128]{2,1,0:T(8,128)(2,1)S(1)} async-done(((bf16[16,144,128]{2,1,0:T(8,128)(2,1)}), bf16[16,144,128]{2,1,0:T(8,128)(2,1)S(1)}, u32[]{:S(2)}, u32[]{:S(2)}) %all-to-all-start.1) | async-done | bytes 589856 | tf_op jit(solution)/shard_map/all_to_all | solution.py:1235
  70.8 4.1 %all-to-all-start.2 = ((bf16[16,112,128]{2,1,0:T(8,128)(2,1)}), bf16[16,112,128]{2,1,0:T(8,128)(2,1)S(1)}, u32[]{:S(2)}, u32[]{:S(2)}) async-start(bf16[16,112,128]{2,1,0:T(8,128)(2,1)} %bitcast.8), calls=%async_computation.2 | async-start | bytes 917504 | tf_op jit(solution)/shard_map/all_to_all | solution.py:1042
  75.0 0.1 collective-permute-start.4
  75.1 0.5 collective-permute-start.3
  75.6 1.5 %collective-permute-done.3.refs_3_ = f32[192,384]{1,0:T(8,128)S(1)} collective-permute-done((f32[192,384]{1,0:T(8,128)S(1)}, f32[192,384]{1,0:T(8,128)S(1)}, u32[]{:S(2)}, u32[]{:S(2)}) %collective-permute-start.3) | collective-permute-done | bytes 294944 | tf_op jit(solution)/shard_map/ppermute | solution.py:1175
  77.1 0.0 collective-permute-done.4.refs_5_
  77.1 2.3 %shard_map.485 = (bf16[192,384]{1,0:T(8,128)(2,1)}, f32[192,384]{1,0:T(8,128)}) custom-call(bf16[384,384]{1,0:T(8,128)(2,1)} %refs_0_.3, bf16[192,384]{1,0:T(8,128)(2,1)} %bitcast.41, f32[192,384]{1,0:T(8,128)} %get-tuple-element.150.refs_2_, f32[192,384]{1,0:T(8,128)S(1)} %collective-permute-done.3.refs_3_, f32[200,384]{1,0:T(8,128)} %get-tuple-element.152.refs_4_, ...), custom_call_target="tpu_custom_call" | custom-call | flops 3000000000 | bytes 1048576 | tf_op jit(solution)/shard_map/pallas_call | solution.py:1140
  79.4 0.0 copy-start
  79.4 0.0 copy-start.1
  79.4 8.6 %all-to-all-done.2.refs_0_ = bf16[16,112,128]{2,1,0:T(8,128)(2,1)S(1)} async-done(((bf16[16,112,128]{2,1,0:T(8,128)(2,1)}), bf16[16,112,128]{2,1,0:T(8,128)(2,1)S(1)}, u32[]{:S(2)}, u32[]{:S(2)}) %all-to-all-start.2) | async-done | bytes 458784 | tf_op jit(solution)/shard_map/all_to_all | solution.py:1042
  88.0 0.8 shard_map.484
  88.9 3.7 %all-to-all-start.3 = ((bf16[16,112,128]{2,1,0:T(8,128)(2,1)}), bf16[16,112,128]{2,1,0:T(8,128)(2,1)S(1)}, u32[]{:S(2)}, u32[]{:S(2)}) async-start(bf16[16,112,128]{2,1,0:T(8,128)(2,1)} %bitcast.12), calls=%async_computation.3 | async-start | bytes 917504 | tf_op jit(solution)/shard_map/all_to_all | solution.py:1280
  92.6 0.0 copy-done
  92.6 0.0 copy-done.1
  92.7 0.1 collective-permute-start.6
  92.8 1.1 collective-permute-done.6
  93.9 0.1 maximum_select_fusion
  94.0 5.2 %shard_map.486 = (f32[384,384]{1,0:T(8,128)}, f32[384,384]{1,0:T(8,128)}, f32[384,2,384]{2,1,0:T(2,128)}, f32[384,2,384]{2,1,0:T(2,128)}, f32[384,384]{1,0:T(8,1...) custom-call(bf16[2304,128]{1,0:T(8,128)(2,1)S(1)} %bitcast.29, f32[384,384]{1,0:T(8,128)} %refs_19_.1, ...), custom_call_target="tpu_custom_call" | custom-call | flops 5000000000 | bytes 1048576 | tf_op jit(solution)/shard_map/pallas_call | solution.py:1140
  99.2 6.2 %all-to-all-done.3 = bf16[16,112,128]{2,1,0:T(8,128)(2,1)S(1)} async-done(((bf16[16,112,128]{2,1,0:T(8,128)(2,1)}), bf16[16,112,128]{2,1,0:T(8,128)(2,1)S(1)}, u32[]{:S(2)}, u32[]{:S(2)}) %all-to-all-start.3) | async-done | bytes 458784 | tf_op jit(solution)/shard_map/all_to_all | solution.py:1280
  105.4 4.2 %shard_map.487 = (f32[384,384]{1,0:T(8,128)S(1)}, f32[384,384]{1,0:T(8,128)S(1)}, f32[2,56,384]{2,1,0:T(8,128)}, f32[2,56,384]{2,1,0:T(8,128)}, f32[2,24,384]{2,...) custom-call(bf16[1792,128]{1,0:T(8,128)(2,1)S(1)} %bitcast.30, ...), custom_call_target="tpu_custom_call" | custom-call | flops 5000000000 | bytes 1048576 | tf_op jit(solution)/shard_map/pallas_call | solution.py:1140
  109.6 0.1 collective-permute-start.5
  109.7 1.1 collective-permute-done.5.refs_1_
  110.9 3.9 %shard_map.488 = (f32[384,2,384]{2,1,0:T(2,128)}, bf16[384,2,384]{2,1,0:T(2,128)(2,1)}, f32[384,384]{1,0:T(8,128)}, bf16[384,384]{1,0:T(8,128)(2,1)}, f32[2,56,3...) custom-call(f32[16,128]{1,0:T(8,128)S(1)} %get-tuple-element.164.ref, ...), custom_call_target="tpu_custom_call", output_to_operand_aliasing={{18}: (23, {}), {19}: (24, {})} | custom-call | flops 5000000000 | bytes 1048576 | tf_op jit(solution)/shard_map/pallas_call | solution.py:1140
  (2 shorter events, 0.0 us)
Async XLA Ops:
  0.7 6.3 %copy-start.2 = (bf16[384,192]{0,1:T(8,128)(2,1)S(1)}, bf16[384,192]{0,1:T(8,128)(2,1)}, u32[]{:S(2)}) copy-start(bf16[384,192]{0,1:T(8,128)(2,1)} %param.25) | copy-start | bytes 442372
  6.5 1.9 %collective-permute-start = (f32[112,384]{1,0:T(8,128)S(1)}, f32[112,384]{1,0:T(8,128)S(1)}, u32[]{:S(2)}, u32[]{:S(2)}) collective-permute-start(f32[112,384]{1,0:T(8,128)S(1)} %get-tuple-element.123.refs_0_), channel_id=1, source_target_pairs={{0,1},{1,0},{2,3},{3,2},{4,5},{5,4},{6,7},{7,6},{8,9},{9,8},{10,11... | collective-permute-start | bytes 516104 | tf_op jit(solution)/shard_map/ppermute | solution.py:1175
  7.0 1.4 %collective-permute-start.1 = (bf16[192,384]{1,0:T(8,128)(2,1)S(1)}, bf16[192,384]{1,0:T(8,128)(2,1)S(1)}, u32[]{:S(2)}, u32[]{:S(2)}) collective-permute-start(bf16[192,384]{1,0:T(8,128)(2,1)S(1)} %bitcast.42), channel_id=1, source_target_pairs={{0,1},{1,0},{2,3},{3,2},{4,5},{5,4},{6,7},{7,6},{8,9},{9,8},{10,11... | collective-permute-start | bytes 442376 | tf_op jit(solution)/shard_map/ppermute | solution.py:1175
  22.3 24.7 %all-to-all-start = ((bf16[16,144,128]{2,1,0:T(8,128)(2,1)}), bf16[16,144,128]{2,1,0:T(8,128)(2,1)S(1)}, u32[]{:S(2)}, u32[]{:S(2)}) async-start(bf16[16,144,128]{2,1,0:T(8,128)(2,1)} %bitcast.4), calls=%async_computation | async-start | bytes 1179648 | tf_op jit(solution)/shard_map/all_to_all | solution.py:1042
  47.9 22.9 %all-to-all-start.1 = ((bf16[16,144,128]{2,1,0:T(8,128)(2,1)}), bf16[16,144,128]{2,1,0:T(8,128)(2,1)S(1)}, u32[]{:S(2)}, u32[]{:S(2)}) async-start(bf16[16,144,128]{2,1,0:T(8,128)(2,1)} %bitcast.6), calls=%async_computation.1 | async-start | bytes 1179648 | tf_op jit(solution)/shard_map/all_to_all | solution.py:1235
  54.7 1.5 %collective-permute-start.2 = (f32[112,384]{1,0:T(8,128)S(1)}, f32[112,384]{1,0:T(8,128)S(1)}, u32[]{:S(2)}, u32[]{:S(2)}) collective-permute-start(f32[112,384]{1,0:T(8,128)S(1)} %get-tuple-element.139.refs_0_), channel_id=1, source_target_pairs={{0,1},{1,0},{2,3},{3,2},{4,5},{5,4},{6,7},{7,6},{8,9},{9,8},{10,11... | collective-permute-start | bytes 516104 | tf_op jit(solution)/shard_map/ppermute | solution.py:1175
  70.8 17.2 %all-to-all-start.2 = ((bf16[16,112,128]{2,1,0:T(8,128)(2,1)}), bf16[16,112,128]{2,1,0:T(8,128)(2,1)S(1)}, u32[]{:S(2)}, u32[]{:S(2)}) async-start(bf16[16,112,128]{2,1,0:T(8,128)(2,1)} %bitcast.8), calls=%async_computation.2 | async-start | bytes 917504 | tf_op jit(solution)/shard_map/all_to_all | solution.py:1042
  75.0 2.1 %collective-permute-start.4 = (f32[200,384]{1,0:T(8,128)S(1)}, f32[200,384]{1,0:T(8,128)S(1)}, u32[]{:S(2)}, u32[]{:S(2)}) collective-permute-start(f32[200,384]{1,0:T(8,128)S(1)} %get-tuple-element.153), channel_id=1, source_target_pairs={{0,1},{1,0},{2,3},{3,2},{4,5},{5,4},{6,7},{7,6},{8,9},{9,8},{10,11... | collective-permute-start | bytes 921608 | tf_op jit(solution)/shard_map/ppermute | solution.py:1175
  75.1 2.0 %collective-permute-start.3 = (f32[192,384]{1,0:T(8,128)S(1)}, f32[192,384]{1,0:T(8,128)S(1)}, u32[]{:S(2)}, u32[]{:S(2)}) collective-permute-start(f32[192,384]{1,0:T(8,128)S(1)} %get-tuple-element.151), channel_id=1, source_target_pairs={{0,1},{1,0},{2,3},{3,2},{4,5},{5,4},{6,7},{7,6},{8,9},{9,8},{10,11... | collective-permute-start | bytes 884744 | tf_op jit(solution)/shard_map/ppermute | solution.py:1175
  79.4 13.2 %copy-start = (f32[192]{0:T(256)S(1)}, f32[192]{0:T(256)}, u32[]{:S(2)}) copy-start(f32[192]{0:T(256)} %param.41) | copy-start | bytes 2308
  79.4 13.2 %copy-start.1 = (f32[192]{0:T(256)S(1)}, f32[192]{0:T(256)}, u32[]{:S(2)}) copy-start(f32[192]{0:T(256)} %param.34) | copy-start | bytes 2308
  88.9 16.5 %all-to-all-start.3 = ((bf16[16,112,128]{2,1,0:T(8,128)(2,1)}), bf16[16,112,128]{2,1,0:T(8,128)(2,1)S(1)}, u32[]{:S(2)}, u32[]{:S(2)}) async-start(bf16[16,112,128]{2,1,0:T(8,128)(2,1)} %bitcast.12), calls=%async_computation.3 | async-start | bytes 917504 | tf_op jit(solution)/shard_map/all_to_all | solution.py:1280
  92.7 1.2 %collective-permute-start.6 = (f32[2,192]{1,0:T(2,128)S(1)}, f32[2,192]{1,0:T(2,128)S(1)}, u32[]{:S(2)}, u32[]{:S(2)}) collective-permute-start(f32[2,192]{1,0:T(2,128)S(1)} %pad_maximum_fusion), channel_id=1, source_target_pairs={{0,1},{1,0},{2,3},{3,2},{4,5},{5,4},{6,7},{7,6},{8,9},{9,8},{10,11... | collective-permute-start | bytes 4616 | tf_op jit(solution)/shard_map/ppermute | solution.py:1175
  109.6 1.2 %collective-permute-start.5 = (f32[16,128]{1,0:T(8,128)S(1)}, f32[16,128]{1,0:T(8,128)S(1)}, u32[]{:S(2)}, u32[]{:S(2)}) collective-permute-start(f32[16,128]{1,0:T(8,128)S(1)} %get-tuple-element.164.refs_0_), channel_id=1, source_target_pairs={{0,1},{1,0},{2,3},{3,2},{4,5},{5,4},{6,7},{7,6},{8,9},{9,8},{10,11... | collective-permute-start | bytes 24584 | tf_op jit(solution)/shard_map/ppermute | solution.py:1175

commit v4 on v3

--- a/solution.py
+++ b/solution.py
@@ -23,6 +23,9 @@
 HIGH = lax.Precision.HIGHEST
 LANES = 128
 ROWS = 16
+NORM_ROWS = 192
+CONV_ROWS = 96
+LAMB_ROWS = 32
 MB = 1 << 20
 
 
@@ -93,12 +96,12 @@
     gain_row = gain[...].reshape(1, width)
 
     def normalise(start, held):
-        source = hid[pl.ds(start, ROWS), :].astype(f32)
+        source = hid[pl.ds(start, NORM_ROWS), :].astype(f32)
         scale = lax.rsqrt(jnp.sum(source * source, axis=1, keepdims=True) / width + norm_eps)
-        norm_out[pl.ds(start, ROWS), :] = (source * scale * gain_row).astype(bf16)
+        norm_out[pl.ds(start, NORM_ROWS), :] = (source * scale * gain_row).astype(bf16)
         return held
 
-    each_rows(tokens, normalise, 0)
+    each_rows(tokens, normalise, 0, NORM_ROWS)
     need(w_mix, w_gate)
     low_out[0] = w_mix[...].astype(bf16)
     low_out[1] = w_gate[...].astype(bf16)
@@ -119,23 +122,23 @@
     width_taps = taps.shape[1]
 
     def convolve(start, held):
-        window = padded[pl.ds(start, ROWS + 16), :]
-        marks = sgpad[pl.ds(start, ROWS + 16), :]
-        own = marks[8 : 8 + ROWS]
-        base = window[8 : 8 + ROWS]
+        window = padded[pl.ds(start, CONV_ROWS + 16), :]
+        marks = sgpad[pl.ds(start, CONV_ROWS + 16), :]
+        own = marks[8 : 8 + CONV_ROWS]
+        base = window[8 : 8 + CONV_ROWS]
         for heading in range(2):
             total = params[0, heading : heading + 1, :] + taps[heading, 0:1, :] * base
             for offset in range(1, width_taps):
                 begin = 8 - offset if heading == 0 else 8 + offset
-                same = jnp.where(marks[begin : begin + ROWS] == own, 1.0, 0.0)
+                same = jnp.where(marks[begin : begin + CONV_ROWS] == own, 1.0, 0.0)
                 if offset == 1:
-                    same_out[heading, pl.ds(start, ROWS), :] = same
-                moved = window[begin : begin + ROWS]
+                    same_out[heading, pl.ds(start, CONV_ROWS), :] = same
+                moved = window[begin : begin + CONV_ROWS]
                 total = total + taps[heading, offset : offset + 1, :] * moved * wide(same, tiles)
-            conv_out[heading, pl.ds(start, ROWS), :] = total
+            conv_out[heading, pl.ds(start, CONV_ROWS), :] = total
         return held
 
-    each_rows(tokens, convolve, 0)
+    each_rows(tokens, convolve, 0, CONV_ROWS)
     for heading in range(2):
         pre = conv_out[heading]
         act_low = (pre * sigmoid(pre)).astype(bf16)
@@ -277,8 +280,8 @@
 
 def forward_kernel(
     own_part, far_part, params, w_dt, cot_own, cot_far, w_out, conv_pre, gate, same, normed, core,
-    states_out, proj, grad_maps, skips, far_step, grad_y, pre_step, inflow_low, gate_low, early, out_far, out_own,
-    grad_branch, inflow, grad_y_low, result, branch_low, maps, diagonal, gathered, states, low_one, low_two,
+    states_out, proj, grad_maps, skips, far_step, grad_y, pre_step, inflow_low, gate_low, branch_low, early,
+    grad_branch, inflow, grad_y_low, act, result, maps, diagonal, gathered, states, low_one, low_two,
     rates, sems,
     *, need, save,
 ):
@@ -297,6 +300,16 @@
         first = heading * rows + rank
         group_maps(maps, proj[first : first + count, :], heading, count)
         diagonal_maps(diagonal, proj[first + count : first + 2 * count, :], heading, count)
+    for tile in range(tiles):
+
+        def activate(start, held, tile=tile):
+            here = pl.ds(start, SPAN)
+            for heading in range(2):
+                pre = conv_pre[heading, here, cols(tile)]
+                act[heading, here, cols(tile)] = pre * sigmoid(pre)
+            return held
+
+        each_rows(tokens, activate, 0, SPAN)
     need(params, w_dt)
     fill_rates(rates, params, count)
     for heading in range(2):
@@ -319,11 +332,9 @@
         def prepare(start, held, tile=tile):
             here = pl.ds(start, SPAN)
             for heading in range(2):
-                pre = conv_pre[heading, here, cols(tile)]
-                act = pre * sigmoid(pre)
                 size = softplus(pre_step[heading, here, cols(tile)])
                 there = pl.ds(z.base(heading, tile) + start, SPAN)
-                entering = size * act
+                entering = size * act[heading, here, cols(tile)]
                 inflow[there, :] = entering
                 inflow_low[heading, here, cols(tile)] = entering.astype(bf16)
                 far_step[there, :] = jnp.where(same[heading, here, :] > 0.5, size * LOG2E, FAR)
@@ -400,11 +411,10 @@
             sums = []
             back = grad_y[pl.ds(z.base(0, tile) + start, SPAN), :]
             for heading in range(2):
-                pre = conv_pre[heading, here, cols(tile)]
-                act = pre * sigmoid(pre)
+                active = act[heading, here, cols(tile)]
                 total = total + result[heading, here, cols(tile)]
-                total = total + params[2, heading : heading + 1, cols(tile)] * act
-                sums.append(held[heading] + fold(back * act))
+                total = total + params[2, heading : heading + 1, cols(tile)] * active
+                sums.append(held[heading] + fold(back * active))
             gated = gate[here, cols(tile)]
             sigma = sigmoid(gated)
             branch_low[here, cols(tile)] = (total * (gated * sigma)).astype(bf16)
@@ -416,12 +426,8 @@
         sums = each_rows(tokens, finish, (jnp.zeros((8, LANES), f32),) * 2, SPAN)
         for heading in range(2):
             skips[heading : heading + 1, cols(tile)] = jnp.sum(sums[heading], axis=0, keepdims=True)
-    save(gate_low, grad_maps, skips)
+    save(gate_low, branch_low, grad_maps, skips)
     branch = branch_low[...]
-    sent = dot(low_out, branch, ((0,), (1,)))
-    out_own[...] = jnp.where(me == 0, sent[:half_width], sent[half_width:])
-    out_far[...] = jnp.where(me == 0, sent[half_width:], sent[:half_width])
-    save(out_own)
     grad_w = dot(branch, low_cot, ((0,), (1,))).astype(bf16)
     for tile in range(width // LANES):
         early[tile * chans : (tile + 1) * chans, :] = grad_w[:, cols(tile)]
@@ -576,14 +582,13 @@
         + at(
             "h", shape((2 * z.rows, z.tokens), f32), shape((2 * z.count, z.tokens), f32), shape((8, z.chans), f32),
             shape(flat, f32), shape((z.tiles * z.tokens, LANES), f32), shape(both, f32), shape(both, bf16),
-            shape(square, bf16),
+            shape(square, bf16), shape(square, bf16),
         )
-        + at("x", shape((early_rows, LANES), bf16), shape((half_width, z.tokens), f32))
-        + at("h", shape((half_width, z.tokens), f32)),
+        + at("x", shape((early_rows, LANES), bf16)),
         args,
         [
             pltpu.VMEM(square, f32), pltpu.VMEM(flat, f32), pltpu.VMEM(square, bf16), pltpu.VMEM(both, f32),
-            pltpu.VMEM(square, bf16), pltpu.VMEM((2, groups, z.count, LANES), f32),
+            pltpu.VMEM(both, f32), pltpu.VMEM((2, groups, z.count, LANES), f32),
             pltpu.VMEM((2, groups, 2, z.count, squared), bf16), pltpu.VMEM((2, groups, z.count, z.count), f32),
             pltpu.VMEM(states, bf16), slot, slot, pltpu.VMEM((2, z.count, z.chans), f32),
             pltpu.SemaphoreType.DMA((2, z.blocks)),
@@ -618,8 +623,8 @@
 
 def back_kernel(
     own_part, far_part, seg, w_xp, taps, mixing, conv_pre, grad_act, grad_chan, normed, gate_low,
-    low_in, hid, gain, grad_dt, core,
-    sums_out, in_own, in_far,
+    low_in, hid, gain, grad_dt, branch, w_out, core,
+    sums_out, in_own, in_far, out_own, out_far,
     padded, gpad, sgpad, mixed_low, small, act_low,
     *, need, save,
 ):
@@ -652,29 +657,29 @@
     need(taps, conv_pre, grad_act, grad_chan)
 
     def through_conv(start, held):
-        here = pl.ds(start, ROWS)
-        window = padded[pl.ds(start, ROWS + 16), :]
-        marks = sgpad[pl.ds(start, ROWS + 16), :]
-        own = marks[8 : 8 + ROWS]
-        base = window[8 : 8 + ROWS]
+        here = pl.ds(start, CONV_ROWS)
+        window = padded[pl.ds(start, CONV_ROWS + 16), :]
+        marks = sgpad[pl.ds(start, CONV_ROWS + 16), :]
+        own = marks[8 : 8 + CONV_ROWS]
+        base = window[8 : 8 + CONV_ROWS]
         sums = []
         for heading in range(2):
             pre = conv_pre[heading, here, :]
             sigma = sigmoid(pre)
             act_low[heading, here, :] = (pre * sigma).astype(bf16)
-            inside = pl.ds(pl.multiple_of(start + 8, 8), ROWS)
+            inside = pl.ds(pl.multiple_of(start + 8, 8), CONV_ROWS)
             grad = (gpad[heading, inside, :] + grad_act[heading, here, :]) * silu_slope(pre, sigma)
             gpad[heading, inside, :] = grad
             sums.append(held[5 * heading] + fold(grad))
             sums.append(held[5 * heading + 1] + fold(grad * base))
             for offset in range(1, width_taps):
                 begin = 8 - offset if heading == 0 else 8 + offset
-                kept = jnp.where(marks[begin : begin + ROWS] == own, 1.0, 0.0)
-                moved = window[begin : begin + ROWS]
+                kept = jnp.where(marks[begin : begin + CONV_ROWS] == own, 1.0, 0.0)
+                moved = window[begin : begin + CONV_ROWS]
                 sums.append(held[5 * heading + 1 + offset] + fold(grad * moved * wide(kept, tiles)))
         return tuple(sums)
 
-    sums = each_rows(tokens, through_conv, (blank,) * 10)
+    sums = each_rows(tokens, through_conv, (blank,) * 10, CONV_ROWS)
     small[...] = jnp.zeros(small.shape, f32)
     for heading in range(2):
         bias = jnp.sum(sums[5 * heading], axis=0, keepdims=True)
@@ -690,23 +695,23 @@
             )
 
     def mixed(start, held):
-        here = pl.ds(start, ROWS)
-        marks = sgpad[pl.ds(start, ROWS + 16), :]
-        own = marks[8 : 8 + ROWS]
-        total = jnp.zeros((ROWS, chans), f32)
+        here = pl.ds(start, CONV_ROWS)
+        marks = sgpad[pl.ds(start, CONV_ROWS + 16), :]
+        own = marks[8 : 8 + CONV_ROWS]
+        total = jnp.zeros((CONV_ROWS, chans), f32)
         for heading in range(2):
-            window = gpad[heading, pl.ds(start, ROWS + 16), :]
-            total = total + window[8 : 8 + ROWS] * taps[heading, 0:1, :]
+            window = gpad[heading, pl.ds(start, CONV_ROWS + 16), :]
+            total = total + window[8 : 8 + CONV_ROWS] * taps[heading, 0:1, :]
             for offset in range(1, width_taps):
                 begin = 8 + offset if heading == 0 else 8 - offset
-                kept = jnp.where(marks[begin : begin + ROWS] == own, 1.0, 0.0)
-                total = total + window[begin : begin + ROWS] * wide(kept, tiles) * taps[
+                kept = jnp.where(marks[begin : begin + CONV_ROWS] == own, 1.0, 0.0)
+                total = total + window[begin : begin + CONV_ROWS] * wide(kept, tiles) * taps[
                     heading, offset : offset + 1, :
                 ]
         mixed_low[here, :] = total.astype(bf16)
         return held
 
-    each_rows(tokens, mixed, 0)
+    each_rows(tokens, mixed, 0, CONV_ROWS)
 
     base_row = 0
 
@@ -725,15 +730,15 @@
     gain_row = gain[...].reshape(1, width)
 
     def gains(start, held):
-        here = pl.ds(start, ROWS)
+        here = pl.ds(start, NORM_ROWS)
         source = hid[here, :].astype(f32)
         scale = lax.rsqrt(jnp.sum(source * source, axis=1, keepdims=True) / width + norm_eps)
-        inside = pl.ds(pl.multiple_of(start + 8, 8), ROWS)
+        inside = pl.ds(pl.multiple_of(start + 8, 8), NORM_ROWS)
         grad = padded[inside, :]
         padded[inside, :] = grad * gain_row
         return held + fold(grad * source * scale)
 
-    gain_sum = each_rows(tokens, gains, jnp.zeros((8, width), f32))
+    gain_sum = each_rows(tokens, gains, jnp.zeros((8, width), f32), NORM_ROWS)
     small[46:47, :] = jnp.sum(gain_sum, axis=0, keepdims=True)
     weighted = padded[pl.ds(8, tokens), :]
     products = weighted * hid[...].astype(f32)
@@ -744,6 +749,10 @@
     in_own[pl.ds(half_width, 8), :] = row_dot
     in_far[pl.ds(half_width, 8), :] = row_dot
     save(in_own)
+    sent = dot(w_out[...].astype(bf16), branch[...], ((0,), (1,)))
+    out_own[...] = jnp.where(me == 0, sent[:half_width], sent[half_width:])
+    out_far[...] = jnp.where(me == 0, sent[half_width:], sent[:half_width])
+    save(out_own)
     put(dot(normed[...], mixed_low[...], TN))
     put(
         jnp.concatenate(
@@ -807,10 +816,10 @@
 
 def spread_of(update, mean, length):
     def step(start, kept):
-        away = update[pl.ds(start, ROWS), :] - mean
+        away = update[pl.ds(start, LAMB_ROWS), :] - mean
         return kept + fold(away * away)
 
-    return rows_sum(each_rows(length, step, jnp.zeros((8, update.shape[1]), f32)))
+    return rows_sum(each_rows(length, step, jnp.zeros((8, update.shape[1]), f32), LAMB_ROWS))
 
 
 def half_update(sums, base, stride, weights, a_ref, b_ref, x_ref, y_ref, u_ref):
@@ -818,8 +827,8 @@
     zero = jnp.zeros((8, chans), f32)
 
     def step(start, kept):
-        here = pl.ds(start, ROWS)
-        grad = fetch(sums, base, stride, start, ROWS, chans // LANES)
+        here = pl.ds(start, LAMB_ROWS)
+        grad = fetch(sums, base, stride, start, LAMB_ROWS, chans // LANES)
         weight = weights[here, :]
         first, second, update = lamb_moments(weight, grad, a_ref[here, :], b_ref[here, :])
         x_ref[here, :] = first
@@ -829,7 +838,7 @@
             kept[0] + fold(weight * weight), kept[1] + fold(update * update), kept[2] + fold(update)
         )
 
-    return each_rows(length, step, (zero, zero, zero))
+    return each_rows(length, step, (zero, zero, zero), LAMB_ROWS)
 
 
 def early_kernel(
@@ -844,8 +853,8 @@
     need(w_out, a_out, b_out)
 
     def one_out(start, kept):
-        here = pl.ds(start, ROWS)
-        grad = fetch(sums, 0, chans, start, ROWS, tiles)
+        here = pl.ds(start, LAMB_ROWS)
+        grad = fetch(sums, 0, chans, start, LAMB_ROWS, tiles)
         weight = w_out[here, :]
         first, second, update = lamb_moments(weight, grad, a_out[here, :], b_out[here, :])
         x_out[here, :] = first
@@ -853,7 +862,7 @@
         u_out[here, :] = update
         return (kept[0] + fold(weight * weight), kept[1] + fold(update * update))
 
-    weight_sq, update_sq = each_rows(chans, one_out, (zero, zero))
+    weight_sq, update_sq = each_rows(chans, one_out, (zero, zero), LAMB_ROWS)
     norms[1:2, :] = lanes_sum(weight_sq)
     norms[7:8, :] = lanes_sum(update_sq)
     save(x_out, y_out, u_out)
@@ -928,11 +937,14 @@
     norms[6:7, :] += lanes_sum(update_sq)
     mix_mean = rows_sum(total) / width
     stats[4:5, :] = mix_mean
-    stats[5:6, :] = spread_of(u_mix, mix_mean, width)
+
+
+def spread_kernel(u_mix, stats, spread, *, need, save):
+    spread[...] = jnp.broadcast_to(spread_of(u_mix, stats[4:5, :], u_mix.shape[0]), spread.shape)
 
 
 def apply_kernel(
-    norms_own, norms_far, stats,
+    norms_own, norms_far, stats, mix_spread,
     w_mix, w_gate, w_out, w_xp, w_dt, w_cv, w_cp,
     u_mix, u_gate, u_out, u_xp, u_dt, u_cv, u_cp,
     gain, gain_first, gain_second, x_mix, y_mix, core, x_given, y_given,
@@ -963,24 +975,24 @@
     need(w_mix, w_gate)
 
     def one_in(start, held):
-        here = pl.ds(start, ROWS)
+        here = pl.ds(start, LAMB_ROWS)
         for half, weight, change in ((0, w_mix, u_mix), (1, w_gate, u_gate)):
             fresh = weight[here, :] - scales[1] * change[here, :]
             n_in[half, here, :] = fresh
             c_in[here, half, :] = fresh.astype(bf16)
         return held
 
-    each_rows(width, one_in, 0)
+    each_rows(width, one_in, 0, LAMB_ROWS)
     save(n_in, c_in)
 
     def one_out(start, held):
-        here = pl.ds(start, ROWS)
+        here = pl.ds(start, LAMB_ROWS)
         fresh = w_out[here, :] - scales[2] * u_out[here, :]
         n_out[here, :] = fresh
         c_out[here, :] = fresh.astype(bf16)
         return held
 
-    each_rows(chans, one_out, 0)
+    each_rows(chans, one_out, 0, LAMB_ROWS)
     save(n_out, c_out)
     need()
     gain_grad = jnp.concatenate(
@@ -1012,7 +1024,7 @@
             fresh_ref[index] = fresh
             copy[index] = fresh.astype(bf16)
     parts = [
-        (scales[1], stats[4:5, :], stats[5:6, :]),
+        (scales[1], stats[4:5, :], mix_spread[0:1, :]),
         (scales[1], stats[0:1, :], stats[1:2, :]),
         (scales[2], stats[2:3, :], stats[3:4, :]),
     ]
@@ -1218,7 +1230,7 @@
     part_far = swap(part)
     early_rows = padded_rows(tiles * width + (width // LANES) * chans)
     (
-        states, proj, grad_maps, skips, far_step, grad_y, pre_step, inflow_low, gate_low, early, out_send, out_own,
+        states, proj, grad_maps, skips, far_step, grad_y, pre_step, inflow_low, gate_low, branch_low, early,
         conv_kept, normed_kept,
     ) = forward_call(
         at("x", part, part_far) + at("h", w_cp, dtproj_weight, cot_own) + at("x", cot_far) + at("h", out_weight)
@@ -1234,16 +1246,18 @@
     early_copies, grad_part = lax.optimization_barrier((join_pieces(early_pieces), grad_part))
     early_sums = lax.all_to_all(early_copies, "dp", 0, 0, tiled=True)
     grad_far = swap(grad_part)
-    out_far = swap(out_send)
     late_rows = padded_rows(tiles * (width + 2 * rows + 2 * rank + 48))
-    late, in_own, in_send = call(
+    late, in_own, in_send, out_own, out_send = call(
         back_kernel,
         at("x", shape((late_rows, LANES), bf16))
         + at("h", shape((half_width + 8, tokens), f32))
-        + at("x", shape((half_width + 8, tokens), f32)),
+        + at("x", shape((half_width + 8, tokens), f32))
+        + at("h", shape((half_width, tokens), f32))
+        + at("x", shape((half_width, tokens), f32)),
         at("x", grad_part, grad_far)
         + at("h", segment_ids, w_xp, conv_weight, mixing, conv_kept) + at("x", grad_act, grad_chan)
         + at("h", normed_kept, gate_low, low_in, hidden_in, norm_gain) + at("x", grad_dt)
+        + at("h", branch_low, out_weight)
         + smem,
         [
             pltpu.VMEM((tokens + 16, chans), f32), pltpu.VMEM((2, tokens + 16, chans), f32),
@@ -1253,6 +1267,7 @@
         limit=20, micros=2,
     )
     in_far = swap(in_send)
+    out_far = swap(out_send)
     late, early_sums = lax.optimization_barrier((late, early_sums))
     late_pieces = send_pieces(late, dp)
     output, input_grad = call(
@@ -1295,6 +1310,9 @@
     moments, updates, norms, stats, kept = got[:10], got[10:15], got[15], got[16], got[17:]
     kept_small, (kept_mix, kept_gate, kept_out, changed_gate, changed_out) = kept[0:4], kept[4:]
     norms_far = swap(norms)
+    mix_spread = call(
+        spread_kernel, at("x", shape((8, chans), f32)), at("x", updates[0], stats), limit=8, micros=1
+    )[0]
     pairs = []
     for entry in [whole_in, whole_out, *shapes]:
         pairs += [entry, shape(entry.shape, bf16)]
@@ -1308,11 +1326,11 @@
             shape((2, chans), f32),
         )
         + at("m", whole_in, whole_in),
-        at("x", norms, norms_far, stats, kept_mix, kept_gate, kept_out, *kept_small, updates[0], changed_gate, changed_out, *updates[1:])
+        at("x", norms, norms_far, stats, mix_spread, kept_mix, kept_gate, kept_out, *kept_small, updates[0], changed_gate, changed_out, *updates[1:])
         + at("h", norm_gain) + at("x", moments_gain[0:1], moments_gain[1:2], moments[0], moments[1])
         + smem + at("m", x_in, y_in),
         [pltpu.SemaphoreType.DMA((2,))],
-        limit=14, micros=5, aliases={23: 18, 24: 19},
+        limit=14, micros=5, aliases={24: 18, 25: 19},
     )
     flat = list(done[12:16])
     firsts_out = [done[18], x_out, *moments[2::2]]

time: 116 us -> 112 us (0.966)
  Pallas kernels: 63.7 us -> 57.4 us
  waiting for transfers between devices: 26 us -> 28.3 us
    pallas_call x10 -> x11, Pallas kernels: 63.7 us -> 57.4 us  [call(): pl.pallas_call(body, out_shape=[out if kind == 'x' else pltpu.HBM(out.sha...]
    all_to_all x1, waiting for transfers between devices: 4.51 us -> 6.64 us  [program(): early_sums = lax.all_to_all(early_copies, 'dp', 0, 0, tiled=True)]
  transfers between devices with their start and end apart: 11 -> 11, of which waited for: 9 -> 9; matrix products, arithmetic and copies ran while one was open for 0% -> 0% of each run, Pallas kernels for 30% -> 29%
where the time goes in v4:
time: 112 us; the launch traced here: 111 us
  Pallas kernels  57.4 us (51%)
  waiting for transfers between devices  28.3 us (25%)
  starting transfers between devices  24.1 us (22%)
    pallas_call x11, Pallas kernels, call(): pl.pallas_call(body, out_shape=[out if kind == 'x' else pltpu.HBM(out.sha...  57.4 us
    all_to_all x2, starting transfers between devices, send_pieces(): lax.all_to_all(values, 'dp', 0, 0, tiled=True).reshape(dp, chunk, LANES)  12.3 us
    all_to_all x2, waiting for transfers between devices, send_pieces(): lax.all_to_all(values, 'dp', 0, 0, tiled=True).reshape(dp, chunk, LANES)  8.8 us
    all_to_all x1, starting transfers between devices, program(): early_sums = lax.all_to_all(early_copies, 'dp', 0, 0, tiled=True)  6.76 us
    all_to_all x1, waiting for transfers between devices, program(): early_sums = lax.all_to_all(early_copies, 'dp', 0, 0, tiled=True)  6.64 us
    all_to_all x1, waiting for transfers between devices, program(): late_sums = lax.all_to_all(late_copies, 'dp', 0, 0, tiled=True)  6.57 us
    ppermute x7, waiting for transfers between devices, swap(): return lax.ppermute(values, 'chan', [(0, 1), (1, 0)])  6.33 us
    all_to_all x1, starting transfers between devices, program(): late_sums = lax.all_to_all(late_copies, 'dp', 0, 0, tiled=True)  3.73 us
  transfers between devices with their start and end apart: 11, of which 9 were waited for; matrix products, arithmetic and copies ran while one was open for 0% of the time, Pallas kernels for 29%

profile of v4, /device:TPU:0, one launch (start us, length us, event | category | flops | bytes accessed | tf_op | source)
XLA Modules:
  0.0 111.0 jit_solution(17632472682156428573)
XLA Ops:
  0.7 0.0 copy-start.2
  0.7 3.7 %shard_map.479 = (f32[384,384]{1,0:T(8,128)}, f32[384,384]{1,0:T(8,128)S(1)}, f32[2,384,384]{2,1,0:T(8,128)S(1)}, f32[112,384]{1,0:T(8,128)S(1)}, bf16[384,384]{...) custom-call(bf16[384,384]{1,0:T(8,128)(2,1)} %refs_0_.3, f32[384]{0:T(512)} %refs_18_.3, ...), custom_call_target="tpu_custom_call" | custom-call | flops 7000000000 | bytes 1048576 | tf_op jit(solution)/shard_map/pallas_call | solution.py:1152
  4.3 0.5 collective-permute-start
  4.9 0.0 copy-done.2
  4.9 0.1 collective-permute-start.1
  5.0 1.3 %collective-permute-done.1.refs_5_ = bf16[192,384]{1,0:T(8,128)(2,1)S(1)} collective-permute-done((bf16[192,384]{1,0:T(8,128)(2,1)S(1)}, bf16[192,384]{1,0:T(8,128)(2,1)S(1)}, u32[]{:S(2)}, u32[]{:S(2)}) %collective-permute-start.1) | collective-permute-done | bytes 147488 | tf_op jit(solution)/shard_map/ppermute | solution.py:1187
  6.2 0.0 collective-permute-done.refs_1_
  6.3 13.3 %shard_map.480 = (bf16[2,6160,384]{2,1,0:T(8,128)(2,1)}, f32[112,384]{1,0:T(8,128)}, f32[32,384]{1,0:T(8,128)}, f32[8,384]{1,0:T(8,128)}, f32[2304,128]{1,0:T(8,...) custom-call(f32[112,384]{1,0:T(8,128)S(1)} %get-tuple-element.124.re, ...), custom_call_target="tpu_custom_call" | custom-call | flops 15000000512 | bytes 1048576 | tf_op jit(solution)/shard_map/pallas_call | solution.py:1152
  19.6 8.1 %all-to-all-start = ((bf16[16,144,128]{2,1,0:T(8,128)(2,1)}), bf16[16,144,128]{2,1,0:T(8,128)(2,1)S(1)}, u32[]{:S(2)}, u32[]{:S(2)}) async-start(bf16[16,144,128]{2,1,0:T(8,128)(2,1)} %bitcast.4), calls=%async_computation | async-start | bytes 1179648 | tf_op jit(solution)/shard_map/all_to_all | solution.py:1054
  27.7 16.4 %shard_map.482 = (f32[112,384]{1,0:T(8,128)S(1)}, f32[2,384,384]{2,1,0:T(8,128)S(1)}, f32[2,24,384]{2,1,0:T(8,128)S(1)}, f32[19,2,384]{2,1,0:T(2,128)S(1)}) custom-call(bf16[2,6160,384]{2,1,0:T(8,128)(2,1)} %get-tuple-element.130.refs_0_, f32[19,2,384]{2,1,0:T(2,128)} %bitcast.45, f32[112,384]{1,0:T(8,128)} %get-tuple-element.131.refs_2_, ...), custom_call_target="tpu_custom_call" | custom-call | flops 15000000512 | bytes 1048576 | tf_op jit(solution)/shard_map/pallas_call | solution.py:1152
  44.2 0.2 all-to-all-done.refs_0_
  44.3 0.9 shard_map.481
  45.2 6.8 %all-to-all-start.1 = ((bf16[16,144,128]{2,1,0:T(8,128)(2,1)}), bf16[16,144,128]{2,1,0:T(8,128)(2,1)S(1)}, u32[]{:S(2)}, u32[]{:S(2)}) async-start(bf16[16,144,128]{2,1,0:T(8,128)(2,1)} %bitcast.6), calls=%async_computation.1 | async-start | bytes 1179648 | tf_op jit(solution)/shard_map/all_to_all | solution.py:1247
  52.0 0.1 collective-permute-start.2
  52.1 1.4 %collective-permute-done.2.refs_1_ = f32[112,384]{1,0:T(8,128)S(1)} collective-permute-done((f32[112,384]{1,0:T(8,128)S(1)}, f32[112,384]{1,0:T(8,128)S(1)}, u32[]{:S(2)}, u32[]{:S(2)}) %collective-permute-start.2) | collective-permute-done | bytes 172064 | tf_op jit(solution)/shard_map/ppermute | solution.py:1187
  53.5 8.0 %shard_map.483 = (bf16[1792,128]{1,0:T(8,128)(2,1)}, f32[200,384]{1,0:T(8,128)}, f32[200,384]{1,0:T(8,128)S(1)}, f32[192,384]{1,0:T(8,128)}, f32[192,384]{1,0:T(8,128)S(1)}) custom-call(f32[112,384]{1,0:T(8,128)S(1)} %get-tuple-element.140.refs_0_, f32[112,384]{1,0:T(8,128)S(1)} %collective-permute-done.2.refs_1_, s32[384]{0:T(512)} %refs_2_.4, ...), custom_call_target="tpu_custom_call" | custom-call | flops 2000000000 | bytes 1048576 | tf_op jit(solution)/shard_map/pallas_call | solution.py:1152
  61.5 6.6 %all-to-all-done.1 = bf16[16,144,128]{2,1,0:T(8,128)(2,1)S(1)} async-done(((bf16[16,144,128]{2,1,0:T(8,128)(2,1)}), bf16[16,144,128]{2,1,0:T(8,128)(2,1)S(1)}, u32[]{:S(2)}, u32[]{:S(2)}) %all-to-all-start.1) | async-done | bytes 589856 | tf_op jit(solution)/shard_map/all_to_all | solution.py:1247
  68.2 4.1 %all-to-all-start.2 = ((bf16[16,112,128]{2,1,0:T(8,128)(2,1)}), bf16[16,112,128]{2,1,0:T(8,128)(2,1)S(1)}, u32[]{:S(2)}, u32[]{:S(2)}) async-start(bf16[16,112,128]{2,1,0:T(8,128)(2,1)} %bitcast.8), calls=%async_computation.2 | async-start | bytes 917504 | tf_op jit(solution)/shard_map/all_to_all | solution.py:1054
  72.3 0.1 collective-permute-start.4
  72.4 0.5 collective-permute-start.3
  72.9 1.5 %collective-permute-done.3.refs_3_ = f32[192,384]{1,0:T(8,128)S(1)} collective-permute-done((f32[192,384]{1,0:T(8,128)S(1)}, f32[192,384]{1,0:T(8,128)S(1)}, u32[]{:S(2)}, u32[]{:S(2)}) %collective-permute-start.3) | collective-permute-done | bytes 294944 | tf_op jit(solution)/shard_map/ppermute | solution.py:1187
  74.4 0.0 collective-permute-done.4.refs_5_
  74.4 2.3 %shard_map.485 = (bf16[192,384]{1,0:T(8,128)(2,1)}, f32[192,384]{1,0:T(8,128)}) custom-call(bf16[384,384]{1,0:T(8,128)(2,1)} %refs_0_.3, bf16[192,384]{1,0:T(8,128)(2,1)} %bitcast.41, f32[192,384]{1,0:T(8,128)} %get-tuple-element.152.refs_2_, f32[192,384]{1,0:T(8,128)S(1)} %collective-permute-done.3.refs_3_, f32[200,384]{1,0:T(8,128)} %get-tuple-element.154.refs_4_, ...), custom_call_target="tpu_custom_call" | custom-call | flops 3000000000 | bytes 1048576 | tf_op jit(solution)/shard_map/pallas_call | solution.py:1152
  76.7 0.0 copy-start
  76.7 0.0 copy-start.1
  76.7 8.6 %all-to-all-done.2.refs_0_ = bf16[16,112,128]{2,1,0:T(8,128)(2,1)S(1)} async-done(((bf16[16,112,128]{2,1,0:T(8,128)(2,1)}), bf16[16,112,128]{2,1,0:T(8,128)(2,1)S(1)}, u32[]{:S(2)}, u32[]{:S(2)}) %all-to-all-start.2) | async-done | bytes 458784 | tf_op jit(solution)/shard_map/all_to_all | solution.py:1054
  85.4 0.8 shard_map.484
  86.2 3.7 %all-to-all-start.3 = ((bf16[16,112,128]{2,1,0:T(8,128)(2,1)}), bf16[16,112,128]{2,1,0:T(8,128)(2,1)S(1)}, u32[]{:S(2)}, u32[]{:S(2)}) async-start(bf16[16,112,128]{2,1,0:T(8,128)(2,1)} %bitcast.12), calls=%async_computation.3 | async-start | bytes 917504 | tf_op jit(solution)/shard_map/all_to_all | solution.py:1295
  90.0 0.0 copy-done
  90.0 0.0 copy-done.1
  90.0 0.1 collective-permute-start.6
  90.1 1.1 %collective-permute-done.6 = f32[2,192]{1,0:T(2,128)S(1)} collective-permute-done((f32[2,192]{1,0:T(2,128)S(1)}, f32[2,192]{1,0:T(2,128)S(1)}, u32[]{:S(2)}, u32[]{:S(2)}) %collective-permute-start.6) | collective-permute-done | bytes 1568 | tf_op jit(solution)/shard_map/ppermute | solution.py:1187
  91.2 0.1 maximum_select_fusion
  91.3 4.9 %shard_map.486 = (f32[384,384]{1,0:T(8,128)}, f32[384,384]{1,0:T(8,128)}, f32[384,2,384]{2,1,0:T(2,128)}, f32[384,2,384]{2,1,0:T(2,128)}, f32[384,384]{1,0:T(8,1...) custom-call(bf16[2304,128]{1,0:T(8,128)(2,1)S(1)} %bitcast.29, f32[384,384]{1,0:T(8,128)} %refs_19_.1, ...), custom_call_target="tpu_custom_call" | custom-call | flops 5000000000 | bytes 1048576 | tf_op jit(solution)/shard_map/pallas_call | solution.py:1152
  96.2 6.6 %all-to-all-done.3 = bf16[16,112,128]{2,1,0:T(8,128)(2,1)S(1)} async-done(((bf16[16,112,128]{2,1,0:T(8,128)(2,1)}), bf16[16,112,128]{2,1,0:T(8,128)(2,1)S(1)}, u32[]{:S(2)}, u32[]{:S(2)}) %all-to-all-start.3) | async-done | bytes 458784 | tf_op jit(solution)/shard_map/all_to_all | solution.py:1295
  102.7 3.8 %shard_map.487 = (f32[384,384]{1,0:T(8,128)S(1)}, f32[384,384]{1,0:T(8,128)S(1)}, f32[2,56,384]{2,1,0:T(8,128)}, f32[2,56,384]{2,1,0:T(8,128)}, f32[2,24,384]{2,...) custom-call(bf16[1792,128]{1,0:T(8,128)(2,1)S(1)} %bitcast.30, ...), custom_call_target="tpu_custom_call" | custom-call | flops 5000000000 | bytes 1048576 | tf_op jit(solution)/shard_map/pallas_call | solution.py:1152
  106.6 0.1 collective-permute-start.5
  106.6 0.2 shard_map.488.refs_3_
  106.8 1.0 collective-permute-done.5.refs_1_
  107.8 3.0 %shard_map.489 = (f32[384,2,384]{2,1,0:T(2,128)}, bf16[384,2,384]{2,1,0:T(2,128)(2,1)}, f32[384,384]{1,0:T(8,128)}, bf16[384,384]{1,0:T(8,128)(2,1)}, f32[2,56,3...) custom-call(f32[16,128]{1,0:T(8,128)S(1)} %get-tuple-element.166.ref, ...), custom_call_target="tpu_custom_call", output_to_operand_aliasing={{18}: (24, {}), {19}: (25, {})} | custom-call | flops 5000000000 | bytes 1048576 | tf_op jit(solution)/shard_map/pallas_call | solution.py:1152
  (2 shorter events, 0.0 us)
Async XLA Ops:
  0.7 4.2 %copy-start.2 = (bf16[384,192]{0,1:T(8,128)(2,1)S(1)}, bf16[384,192]{0,1:T(8,128)(2,1)}, u32[]{:S(2)}) copy-start(bf16[384,192]{0,1:T(8,128)(2,1)} %param.25) | copy-start | bytes 442372
  4.3 1.9 %collective-permute-start = (f32[112,384]{1,0:T(8,128)S(1)}, f32[112,384]{1,0:T(8,128)S(1)}, u32[]{:S(2)}, u32[]{:S(2)}) collective-permute-start(f32[112,384]{1,0:T(8,128)S(1)} %get-tuple-element.124.refs_0_), channel_id=1, source_target_pairs={{0,1},{1,0},{2,3},{3,2},{4,5},{5,4},{6,7},{7,6},{8,9},{9,8},{10,11... | collective-permute-start | bytes 516104 | tf_op jit(solution)/shard_map/ppermute | solution.py:1187
  4.9 1.4 %collective-permute-start.1 = (bf16[192,384]{1,0:T(8,128)(2,1)S(1)}, bf16[192,384]{1,0:T(8,128)(2,1)S(1)}, u32[]{:S(2)}, u32[]{:S(2)}) collective-permute-start(bf16[192,384]{1,0:T(8,128)(2,1)S(1)} %bitcast.42), channel_id=1, source_target_pairs={{0,1},{1,0},{2,3},{3,2},{4,5},{5,4},{6,7},{7,6},{8,9},{9,8},{10,11... | collective-permute-start | bytes 442376 | tf_op jit(solution)/shard_map/ppermute | solution.py:1187
  19.6 24.7 %all-to-all-start = ((bf16[16,144,128]{2,1,0:T(8,128)(2,1)}), bf16[16,144,128]{2,1,0:T(8,128)(2,1)S(1)}, u32[]{:S(2)}, u32[]{:S(2)}) async-start(bf16[16,144,128]{2,1,0:T(8,128)(2,1)} %bitcast.4), calls=%async_computation | async-start | bytes 1179648 | tf_op jit(solution)/shard_map/all_to_all | solution.py:1054
  45.2 22.9 %all-to-all-start.1 = ((bf16[16,144,128]{2,1,0:T(8,128)(2,1)}), bf16[16,144,128]{2,1,0:T(8,128)(2,1)S(1)}, u32[]{:S(2)}, u32[]{:S(2)}) async-start(bf16[16,144,128]{2,1,0:T(8,128)(2,1)} %bitcast.6), calls=%async_computation.1 | async-start | bytes 1179648 | tf_op jit(solution)/shard_map/all_to_all | solution.py:1247
  52.0 1.5 %collective-permute-start.2 = (f32[112,384]{1,0:T(8,128)S(1)}, f32[112,384]{1,0:T(8,128)S(1)}, u32[]{:S(2)}, u32[]{:S(2)}) collective-permute-start(f32[112,384]{1,0:T(8,128)S(1)} %get-tuple-element.140.refs_0_), channel_id=1, source_target_pairs={{0,1},{1,0},{2,3},{3,2},{4,5},{5,4},{6,7},{7,6},{8,9},{9,8},{10,11... | collective-permute-start | bytes 516104 | tf_op jit(solution)/shard_map/ppermute | solution.py:1187
  68.2 17.2 %all-to-all-start.2 = ((bf16[16,112,128]{2,1,0:T(8,128)(2,1)}), bf16[16,112,128]{2,1,0:T(8,128)(2,1)S(1)}, u32[]{:S(2)}, u32[]{:S(2)}) async-start(bf16[16,112,128]{2,1,0:T(8,128)(2,1)} %bitcast.8), calls=%async_computation.2 | async-start | bytes 917504 | tf_op jit(solution)/shard_map/all_to_all | solution.py:1054
  72.3 2.1 %collective-permute-start.4 = (f32[200,384]{1,0:T(8,128)S(1)}, f32[200,384]{1,0:T(8,128)S(1)}, u32[]{:S(2)}, u32[]{:S(2)}) collective-permute-start(f32[200,384]{1,0:T(8,128)S(1)} %get-tuple-element.155), channel_id=1, source_target_pairs={{0,1},{1,0},{2,3},{3,2},{4,5},{5,4},{6,7},{7,6},{8,9},{9,8},{10,11... | collective-permute-start | bytes 921608 | tf_op jit(solution)/shard_map/ppermute | solution.py:1187
  72.4 2.0 %collective-permute-start.3 = (f32[192,384]{1,0:T(8,128)S(1)}, f32[192,384]{1,0:T(8,128)S(1)}, u32[]{:S(2)}, u32[]{:S(2)}) collective-permute-start(f32[192,384]{1,0:T(8,128)S(1)} %get-tuple-element.153), channel_id=1, source_target_pairs={{0,1},{1,0},{2,3},{3,2},{4,5},{5,4},{6,7},{7,6},{8,9},{9,8},{10,11... | collective-permute-start | bytes 884744 | tf_op jit(solution)/shard_map/ppermute | solution.py:1187
  76.7 13.2 %copy-start = (f32[192]{0:T(256)S(1)}, f32[192]{0:T(256)}, u32[]{:S(2)}) copy-start(f32[192]{0:T(256)} %param.41) | copy-start | bytes 2308
  76.7 13.2 %copy-start.1 = (f32[192]{0:T(256)S(1)}, f32[192]{0:T(256)}, u32[]{:S(2)}) copy-start(f32[192]{0:T(256)} %param.34) | copy-start | bytes 2308
  86.2 16.5 %all-to-all-start.3 = ((bf16[16,112,128]{2,1,0:T(8,128)(2,1)}), bf16[16,112,128]{2,1,0:T(8,128)(2,1)S(1)}, u32[]{:S(2)}, u32[]{:S(2)}) async-start(bf16[16,112,128]{2,1,0:T(8,128)(2,1)} %bitcast.12), calls=%async_computation.3 | async-start | bytes 917504 | tf_op jit(solution)/shard_map/all_to_all | solution.py:1295
  90.0 1.2 %collective-permute-start.6 = (f32[2,192]{1,0:T(2,128)S(1)}, f32[2,192]{1,0:T(2,128)S(1)}, u32[]{:S(2)}, u32[]{:S(2)}) collective-permute-start(f32[2,192]{1,0:T(2,128)S(1)} %pad_maximum_fusion), channel_id=1, source_target_pairs={{0,1},{1,0},{2,3},{3,2},{4,5},{5,4},{6,7},{7,6},{8,9},{9,8},{10,11... | collective-permute-start | bytes 4616 | tf_op jit(solution)/shard_map/ppermute | solution.py:1187
  106.6 1.2 %collective-permute-start.5 = (f32[16,128]{1,0:T(8,128)S(1)}, f32[16,128]{1,0:T(8,128)S(1)}, u32[]{:S(2)}, u32[]{:S(2)}) collective-permute-start(f32[16,128]{1,0:T(8,128)S(1)} %get-tuple-element.166.refs_0_), channel_id=1, source_target_pairs={{0,1},{1,0},{2,3},{3,2},{4,5},{5,4},{6,7},{7,6},{8,9},{9,8},{10,11... | collective-permute-start | bytes 24584 | tf_op jit(solution)/shard_map/ppermute | solution.py:1187

commit v5 on v4

--- a/solution.py
+++ b/solution.py
@@ -83,8 +83,8 @@
 
 
 def front_kernel(
-    hid, gain, w_mix, w_gate, seg, taps, params, w_xp,
-    mix_out, gate_out, conv_out, part_out, norm_out, low_out, same_out,
+    hid, gain, w_mix, w_gate, seg, taps, w_xp,
+    mix_out, gate_out, conv_out, part_out, norm_out, low_out, same_out, params, near_dt, near_cot,
     padded, sgpad,
     *, need, save,
 ):
@@ -102,6 +102,7 @@
         return held
 
     each_rows(tokens, normalise, 0, NORM_ROWS)
+    save(norm_out)
     need(w_mix, w_gate)
     low_out[0] = w_mix[...].astype(bf16)
     low_out[1] = w_gate[...].astype(bf16)
@@ -148,7 +149,7 @@
         )
 
 
-SPAN = 64
+SPAN = 128
 
 
 class Sizes:
@@ -427,6 +428,7 @@
         for heading in range(2):
             skips[heading : heading + 1, cols(tile)] = jnp.sum(sums[heading], axis=0, keepdims=True)
     save(gate_low, branch_low, grad_maps, skips)
+    need()
     branch = branch_low[...]
     grad_w = dot(branch, low_cot, ((0,), (1,))).astype(bf16)
     for tile in range(width // LANES):
@@ -1110,16 +1112,15 @@
             source, kind = ins[len(args) + number], passed[number][1]
             source = source if kind == "h" else source.at[:, int(kind), :]
             loads[id(held)] = pltpu.make_async_copy(source, held, sems.at[len(staging) + number])
-            follow.append(id(held))
-        begun = []
+            loads[id(held)].start()
+        begun, resting = [], []
         for number, place in enumerate(kept):
-            begun.append(
+            resting.append(
                 pltpu.make_async_copy(
                     ins[place], results[n_own + len(passed) + number],
                     sems.at[len(staging) + len(passed) + number],
                 )
             )
-            begun[-1].start()
 
         def need(*wanted):
             keys = [id(ref) for ref in wanted] or list(loads)
@@ -1128,6 +1129,9 @@
                     loads.pop(key).wait()
             while follow:
                 loads[follow.pop(0)].start()
+            while resting:
+                begun.append(resting.pop(0))
+                begun[-1].start()
             for key in keys:
                 if key in loads:
                     loads.pop(key).wait()
@@ -1213,29 +1217,26 @@
     def padded_rows(amount):
         return -(-amount // (dp * 16)) * 16 * dp
 
-    mixing, gate, conv_pre, part, normed, low_in, same = call(
+    mixing, gate, conv_pre, part, normed, low_in, same, near_cp, near_dt, near_cot = call(
         front_kernel,
         at("h", shape(square, f32))
-        + at(
-            "x", shape(square, f32), shape((2,) + square, f32), shape((2 * rows, tokens), f32),
-            shape((tokens, width), bf16),
-        )
-        + at("h", shape((2, width, chans), bf16))
+        + at("x", shape(square, f32), shape((2,) + square, f32), shape((2 * rows, tokens), f32))
+        + at("h", shape((tokens, width), bf16), shape((2, width, chans), bf16))
         + at("x", shape((2, tokens, LANES), f32)),
         at("h", hidden_in, norm_gain) + at("0", in_weight) + at("1", in_weight)
-        + at("h", segment_ids, conv_weight, w_cp, w_xp),
+        + at("h", segment_ids, conv_weight, w_xp),
         [pltpu.VMEM((tokens + 16, chans), f32), pltpu.VMEM((tokens + 16, LANES), f32)],
-        limit=14, micros=7,
+        limit=14, micros=6, passed=at("h", w_cp, dtproj_weight, cot_own),
     )
     part_far = swap(part)
     early_rows = padded_rows(tiles * width + (width // LANES) * chans)
     (
         states, proj, grad_maps, skips, far_step, grad_y, pre_step, inflow_low, gate_low, branch_low, early,
-        conv_kept, normed_kept,
+        conv_kept,
     ) = forward_call(
-        at("x", part, part_far) + at("h", w_cp, dtproj_weight, cot_own) + at("x", cot_far) + at("h", out_weight)
-        + at("x", conv_pre, gate, same, normed) + smem,
-        z, early_rows, half_width, (7, 10),
+        at("x", part, part_far, near_cp, near_dt, near_cot, cot_far) + at("h", out_weight)
+        + at("x", conv_pre, gate, same) + at("h", normed) + smem,
+        z, early_rows, half_width, (7,),
     )
     early_pieces = send_pieces(early, dp)
     grad_part, grad_act, grad_dt, grad_chan = backward_call(
@@ -1256,7 +1257,7 @@
         + at("x", shape((half_width, tokens), f32)),
         at("x", grad_part, grad_far)
         + at("h", segment_ids, w_xp, conv_weight, mixing, conv_kept) + at("x", grad_act, grad_chan)
-        + at("h", normed_kept, gate_low, low_in, hidden_in, norm_gain) + at("x", grad_dt)
+        + at("h", normed, gate_low, low_in, hidden_in, norm_gain) + at("x", grad_dt)
         + at("h", branch_low, out_weight)
         + smem,
         [

time: 112 us -> 110 us (0.982)
  Pallas kernels: 57.4 us -> 56 us
    pallas_call x11, Pallas kernels: 57.4 us -> 56 us  [call(): pl.pallas_call(body, out_shape=[out if kind == 'x' else pltpu.HBM(out.sha...]
where the time goes in v5:
time: 110 us
  Pallas kernels  56 us (51%)
  waiting for transfers between devices  28.4 us (26%)
  starting transfers between devices  24.1 us (22%)
    pallas_call x11, Pallas kernels, call(): pl.pallas_call(body, out_shape=[out if kind == 'x' else pltpu.HBM(out.sha...  56 us
    all_to_all x2, starting transfers between devices, send_pieces(): lax.all_to_all(values, 'dp', 0, 0, tiled=True).reshape(dp, chunk, LANES)  12.3 us
    all_to_all x2, waiting for transfers between devices, send_pieces(): lax.all_to_all(values, 'dp', 0, 0, tiled=True).reshape(dp, chunk, LANES)  8.87 us
    all_to_all x1, starting transfers between devices, program(): early_sums = lax.all_to_all(early_copies, 'dp', 0, 0, tiled=True)  6.69 us
    all_to_all x1, waiting for transfers between devices, program(): early_sums = lax.all_to_all(early_copies, 'dp', 0, 0, tiled=True)  6.63 us
    all_to_all x1, waiting for transfers between devices, program(): late_sums = lax.all_to_all(late_copies, 'dp', 0, 0, tiled=True)  6.57 us
    ppermute x7, waiting for transfers between devices, swap(): return lax.ppermute(values, 'chan', [(0, 1), (1, 0)])  6.33 us
    all_to_all x1, starting transfers between devices, program(): late_sums = lax.all_to_all(late_copies, 'dp', 0, 0, tiled=True)  3.73 us
  transfers between devices with their start and end apart: 11, of which 9 were waited for; matrix products, arithmetic and copies ran while one was open for 0% of the time, Pallas kernels for 29%

profile of v5, /device:TPU:0, one launch (start us, length us, event | category | flops | bytes accessed | tf_op | source)
XLA Modules:
  0.0 109.6 jit_solution(4690374531991487187)
XLA Ops:
  0.7 0.0 copy-start.2
  0.7 3.7 %shard_map.479 = (f32[384,384]{1,0:T(8,128)}, f32[384,384]{1,0:T(8,128)S(1)}, f32[2,384,384]{2,1,0:T(8,128)S(1)}, f32[112,384]{1,0:T(8,128)S(1)}, bf16[384,384]{...) custom-call(bf16[384,384]{1,0:T(8,128)(2,1)} %refs_0_.3, ...), custom_call_target="tpu_custom_call" | custom-call | flops 6000000000 | bytes 1048576 | tf_op jit(solution)/shard_map/pallas_call | solution.py:1156
  4.4 0.5 collective-permute-start
  4.9 0.0 copy-done.2
  4.9 0.1 collective-permute-start.1
  5.0 1.3 %collective-permute-done.1.refs_5_ = bf16[192,384]{1,0:T(8,128)(2,1)S(1)} collective-permute-done((bf16[192,384]{1,0:T(8,128)(2,1)S(1)}, bf16[192,384]{1,0:T(8,128)(2,1)S(1)}, u32[]{:S(2)}, u32[]{:S(2)}) %collective-permute-start.1) | collective-permute-done | bytes 147488 | tf_op jit(solution)/shard_map/ppermute | solution.py:1191
  6.3 0.0 collective-permute-done.refs_1_
  6.3 12.5 %shard_map.480 = (bf16[2,6160,384]{2,1,0:T(8,128)(2,1)}, f32[112,384]{1,0:T(8,128)}, f32[32,384]{1,0:T(8,128)}, f32[8,384]{1,0:T(8,128)}, f32[2304,128]{1,0:T(8,...) custom-call(f32[112,384]{1,0:T(8,128)S(1)} %get-tuple-element.126.re, ...), custom_call_target="tpu_custom_call" | custom-call | flops 15000000512 | bytes 1048576 | tf_op jit(solution)/shard_map/pallas_call | solution.py:1156
  18.8 8.1 %all-to-all-start = ((bf16[16,144,128]{2,1,0:T(8,128)(2,1)}), bf16[16,144,128]{2,1,0:T(8,128)(2,1)S(1)}, u32[]{:S(2)}, u32[]{:S(2)}) async-start(bf16[16,144,128]{2,1,0:T(8,128)(2,1)} %bitcast.4), calls=%async_computation | async-start | bytes 1179648 | tf_op jit(solution)/shard_map/all_to_all | solution.py:1056
  26.9 16.4 %shard_map.482 = (f32[112,384]{1,0:T(8,128)S(1)}, f32[2,384,384]{2,1,0:T(8,128)S(1)}, f32[2,24,384]{2,1,0:T(8,128)S(1)}, f32[19,2,384]{2,1,0:T(2,128)S(1)}) custom-call(bf16[2,6160,384]{2,1,0:T(8,128)(2,1)} %get-tuple-element.135.refs_0_, f32[19,2,384]{2,1,0:T(2,128)} %bitcast.44, f32[112,384]{1,0:T(8,128)} %get-tuple-element.136.refs_2_, ...), custom_call_target="tpu_custom_call" | custom-call | flops 15000000512 | bytes 1048576 | tf_op jit(solution)/shard_map/pallas_call | solution.py:1156
  43.3 0.2 all-to-all-done.refs_0_
  43.5 0.9 shard_map.481
  44.4 6.7 %all-to-all-start.1 = ((bf16[16,144,128]{2,1,0:T(8,128)(2,1)}), bf16[16,144,128]{2,1,0:T(8,128)(2,1)S(1)}, u32[]{:S(2)}, u32[]{:S(2)}) async-start(bf16[16,144,128]{2,1,0:T(8,128)(2,1)} %bitcast.6), calls=%async_computation.1 | async-start | bytes 1179648 | tf_op jit(solution)/shard_map/all_to_all | solution.py:1248
  51.1 0.1 collective-permute-start.2
  51.2 1.4 %collective-permute-done.2.refs_1_ = f32[112,384]{1,0:T(8,128)S(1)} collective-permute-done((f32[112,384]{1,0:T(8,128)S(1)}, f32[112,384]{1,0:T(8,128)S(1)}, u32[]{:S(2)}, u32[]{:S(2)}) %collective-permute-start.2) | collective-permute-done | bytes 172064 | tf_op jit(solution)/shard_map/ppermute | solution.py:1191
  52.6 8.0 %shard_map.483 = (bf16[1792,128]{1,0:T(8,128)(2,1)}, f32[200,384]{1,0:T(8,128)}, f32[200,384]{1,0:T(8,128)S(1)}, f32[192,384]{1,0:T(8,128)}, f32[192,384]{1,0:T(8,128)S(1)}) custom-call(f32[112,384]{1,0:T(8,128)S(1)} %get-tuple-element.145.refs_0_, f32[112,384]{1,0:T(8,128)S(1)} %collective-permute-done.2.refs_1_, s32[384]{0:T(512)} %refs_2_.4, ...), custom_call_target="tpu_custom_call" | custom-call | flops 2000000000 | bytes 1048576 | tf_op jit(solution)/shard_map/pallas_call | solution.py:1156
  60.7 6.6 %all-to-all-done.1 = bf16[16,144,128]{2,1,0:T(8,128)(2,1)S(1)} async-done(((bf16[16,144,128]{2,1,0:T(8,128)(2,1)}), bf16[16,144,128]{2,1,0:T(8,128)(2,1)S(1)}, u32[]{:S(2)}, u32[]{:S(2)}) %all-to-all-start.1) | async-done | bytes 589856 | tf_op jit(solution)/shard_map/all_to_all | solution.py:1248
  67.3 4.1 %all-to-all-start.2 = ((bf16[16,112,128]{2,1,0:T(8,128)(2,1)}), bf16[16,112,128]{2,1,0:T(8,128)(2,1)S(1)}, u32[]{:S(2)}, u32[]{:S(2)}) async-start(bf16[16,112,128]{2,1,0:T(8,128)(2,1)} %bitcast.8), calls=%async_computation.2 | async-start | bytes 917504 | tf_op jit(solution)/shard_map/all_to_all | solution.py:1056
  71.4 0.1 collective-permute-start.4
  71.5 0.5 collective-permute-start.3
  72.0 1.5 %collective-permute-done.3.refs_3_ = f32[192,384]{1,0:T(8,128)S(1)} collective-permute-done((f32[192,384]{1,0:T(8,128)S(1)}, f32[192,384]{1,0:T(8,128)S(1)}, u32[]{:S(2)}, u32[]{:S(2)}) %collective-permute-start.3) | collective-permute-done | bytes 294944 | tf_op jit(solution)/shard_map/ppermute | solution.py:1191
  73.5 0.0 collective-permute-done.4.refs_5_
  73.5 2.3 %shard_map.485 = (bf16[192,384]{1,0:T(8,128)(2,1)}, f32[192,384]{1,0:T(8,128)}) custom-call(bf16[384,384]{1,0:T(8,128)(2,1)} %refs_0_.3, bf16[192,384]{1,0:T(8,128)(2,1)} %bitcast.41, f32[192,384]{1,0:T(8,128)} %get-tuple-element.156.refs_2_, f32[192,384]{1,0:T(8,128)S(1)} %collective-permute-done.3.refs_3_, f32[200,384]{1,0:T(8,128)} %get-tuple-element.158.refs_4_, ...), custom_call_target="tpu_custom_call" | custom-call | flops 3000000000 | bytes 1048576 | tf_op jit(solution)/shard_map/pallas_call | solution.py:1156
  75.8 0.0 copy-start
  75.9 0.0 copy-start.1
  75.9 8.6 %all-to-all-done.2.refs_0_ = bf16[16,112,128]{2,1,0:T(8,128)(2,1)S(1)} async-done(((bf16[16,112,128]{2,1,0:T(8,128)(2,1)}), bf16[16,112,128]{2,1,0:T(8,128)(2,1)S(1)}, u32[]{:S(2)}, u32[]{:S(2)}) %all-to-all-start.2) | async-done | bytes 458784 | tf_op jit(solution)/shard_map/all_to_all | solution.py:1056
  84.5 0.8 shard_map.484
  85.3 3.7 %all-to-all-start.3 = ((bf16[16,112,128]{2,1,0:T(8,128)(2,1)}), bf16[16,112,128]{2,1,0:T(8,128)(2,1)S(1)}, u32[]{:S(2)}, u32[]{:S(2)}) async-start(bf16[16,112,128]{2,1,0:T(8,128)(2,1)} %bitcast.12), calls=%async_computation.3 | async-start | bytes 917504 | tf_op jit(solution)/shard_map/all_to_all | solution.py:1296
  89.1 0.0 copy-done
  89.1 0.0 copy-done.1
  89.1 0.1 collective-permute-start.6
  89.2 1.1 %collective-permute-done.6 = f32[2,192]{1,0:T(2,128)S(1)} collective-permute-done((f32[2,192]{1,0:T(2,128)S(1)}, f32[2,192]{1,0:T(2,128)S(1)}, u32[]{:S(2)}, u32[]{:S(2)}) %collective-permute-start.6) | collective-permute-done | bytes 1568 | tf_op jit(solution)/shard_map/ppermute | solution.py:1191
  90.3 0.1 maximum_select_fusion
  90.4 4.9 %shard_map.486 = (f32[384,384]{1,0:T(8,128)}, f32[384,384]{1,0:T(8,128)}, f32[384,2,384]{2,1,0:T(2,128)}, f32[384,2,384]{2,1,0:T(2,128)}, f32[384,384]{1,0:T(8,1...) custom-call(bf16[2304,128]{1,0:T(8,128)(2,1)S(1)} %bitcast.29, f32[384,384]{1,0:T(8,128)} %refs_19_.1, ...), custom_call_target="tpu_custom_call" | custom-call | flops 5000000000 | bytes 1048576 | tf_op jit(solution)/shard_map/pallas_call | solution.py:1156
  95.3 6.6 %all-to-all-done.3 = bf16[16,112,128]{2,1,0:T(8,128)(2,1)S(1)} async-done(((bf16[16,112,128]{2,1,0:T(8,128)(2,1)}), bf16[16,112,128]{2,1,0:T(8,128)(2,1)S(1)}, u32[]{:S(2)}, u32[]{:S(2)}) %all-to-all-start.3) | async-done | bytes 458784 | tf_op jit(solution)/shard_map/all_to_all | solution.py:1296
  101.9 3.3 %shard_map.487 = (f32[384,384]{1,0:T(8,128)S(1)}, f32[384,384]{1,0:T(8,128)S(1)}, f32[2,56,384]{2,1,0:T(8,128)}, f32[2,56,384]{2,1,0:T(8,128)}, f32[2,24,384]{2,...) custom-call(bf16[1792,128]{1,0:T(8,128)(2,1)S(1)} %bitcast.30, ...), custom_call_target="tpu_custom_call" | custom-call | flops 5000000000 | bytes 1048576 | tf_op jit(solution)/shard_map/pallas_call | solution.py:1156
  105.2 0.1 collective-permute-start.5
  105.2 0.2 shard_map.488.refs_3_
  105.4 1.0 collective-permute-done.5.refs_1_
  106.4 3.0 %shard_map.489 = (f32[384,2,384]{2,1,0:T(2,128)}, bf16[384,2,384]{2,1,0:T(2,128)(2,1)}, f32[384,384]{1,0:T(8,128)}, bf16[384,384]{1,0:T(8,128)(2,1)}, f32[2,56,3...) custom-call(f32[16,128]{1,0:T(8,128)S(1)} %get-tuple-element.170.ref, ...), custom_call_target="tpu_custom_call", output_to_operand_aliasing={{18}: (24, {}), {19}: (25, {})} | custom-call | flops 5000000000 | bytes 1048576 | tf_op jit(solution)/shard_map/pallas_call | solution.py:1156
  (2 shorter events, 0.0 us)
Async XLA Ops:
  0.7 4.2 %copy-start.2 = (bf16[384,192]{0,1:T(8,128)(2,1)S(1)}, bf16[384,192]{0,1:T(8,128)(2,1)}, u32[]{:S(2)}) copy-start(bf16[384,192]{0,1:T(8,128)(2,1)} %param.25) | copy-start | bytes 442372
  4.4 1.9 %collective-permute-start = (f32[112,384]{1,0:T(8,128)S(1)}, f32[112,384]{1,0:T(8,128)S(1)}, u32[]{:S(2)}, u32[]{:S(2)}) collective-permute-start(f32[112,384]{1,0:T(8,128)S(1)} %get-tuple-element.126.refs_0_), channel_id=1, source_target_pairs={{0,1},{1,0},{2,3},{3,2},{4,5},{5,4},{6,7},{7,6},{8,9},{9,8},{10,11... | collective-permute-start | bytes 516104 | tf_op jit(solution)/shard_map/ppermute | solution.py:1191
  4.9 1.4 %collective-permute-start.1 = (bf16[192,384]{1,0:T(8,128)(2,1)S(1)}, bf16[192,384]{1,0:T(8,128)(2,1)S(1)}, u32[]{:S(2)}, u32[]{:S(2)}) collective-permute-start(bf16[192,384]{1,0:T(8,128)(2,1)S(1)} %bitcast.42), channel_id=1, source_target_pairs={{0,1},{1,0},{2,3},{3,2},{4,5},{5,4},{6,7},{7,6},{8,9},{9,8},{10,11... | collective-permute-start | bytes 442376 | tf_op jit(solution)/shard_map/ppermute | solution.py:1191
  18.8 24.7 %all-to-all-start = ((bf16[16,144,128]{2,1,0:T(8,128)(2,1)}), bf16[16,144,128]{2,1,0:T(8,128)(2,1)S(1)}, u32[]{:S(2)}, u32[]{:S(2)}) async-start(bf16[16,144,128]{2,1,0:T(8,128)(2,1)} %bitcast.4), calls=%async_computation | async-start | bytes 1179648 | tf_op jit(solution)/shard_map/all_to_all | solution.py:1056
  44.4 22.8 %all-to-all-start.1 = ((bf16[16,144,128]{2,1,0:T(8,128)(2,1)}), bf16[16,144,128]{2,1,0:T(8,128)(2,1)S(1)}, u32[]{:S(2)}, u32[]{:S(2)}) async-start(bf16[16,144,128]{2,1,0:T(8,128)(2,1)} %bitcast.6), calls=%async_computation.1 | async-start | bytes 1179648 | tf_op jit(solution)/shard_map/all_to_all | solution.py:1248
  51.1 1.5 %collective-permute-start.2 = (f32[112,384]{1,0:T(8,128)S(1)}, f32[112,384]{1,0:T(8,128)S(1)}, u32[]{:S(2)}, u32[]{:S(2)}) collective-permute-start(f32[112,384]{1,0:T(8,128)S(1)} %get-tuple-element.145.refs_0_), channel_id=1, source_target_pairs={{0,1},{1,0},{2,3},{3,2},{4,5},{5,4},{6,7},{7,6},{8,9},{9,8},{10,11... | collective-permute-start | bytes 516104 | tf_op jit(solution)/shard_map/ppermute | solution.py:1191
  67.3 17.2 %all-to-all-start.2 = ((bf16[16,112,128]{2,1,0:T(8,128)(2,1)}), bf16[16,112,128]{2,1,0:T(8,128)(2,1)S(1)}, u32[]{:S(2)}, u32[]{:S(2)}) async-start(bf16[16,112,128]{2,1,0:T(8,128)(2,1)} %bitcast.8), calls=%async_computation.2 | async-start | bytes 917504 | tf_op jit(solution)/shard_map/all_to_all | solution.py:1056
  71.4 2.1 %collective-permute-start.4 = (f32[200,384]{1,0:T(8,128)S(1)}, f32[200,384]{1,0:T(8,128)S(1)}, u32[]{:S(2)}, u32[]{:S(2)}) collective-permute-start(f32[200,384]{1,0:T(8,128)S(1)} %get-tuple-element.159), channel_id=1, source_target_pairs={{0,1},{1,0},{2,3},{3,2},{4,5},{5,4},{6,7},{7,6},{8,9},{9,8},{10,11... | collective-permute-start | bytes 921608 | tf_op jit(solution)/shard_map/ppermute | solution.py:1191
  71.5 2.0 %collective-permute-start.3 = (f32[192,384]{1,0:T(8,128)S(1)}, f32[192,384]{1,0:T(8,128)S(1)}, u32[]{:S(2)}, u32[]{:S(2)}) collective-permute-start(f32[192,384]{1,0:T(8,128)S(1)} %get-tuple-element.157), channel_id=1, source_target_pairs={{0,1},{1,0},{2,3},{3,2},{4,5},{5,4},{6,7},{7,6},{8,9},{9,8},{10,11... | collective-permute-start | bytes 884744 | tf_op jit(solution)/shard_map/ppermute | solution.py:1191
  75.8 13.2 %copy-start = (f32[192]{0:T(256)S(1)}, f32[192]{0:T(256)}, u32[]{:S(2)}) copy-start(f32[192]{0:T(256)} %param.41) | copy-start | bytes 2308
  75.9 13.2 %copy-start.1 = (f32[192]{0:T(256)S(1)}, f32[192]{0:T(256)}, u32[]{:S(2)}) copy-start(f32[192]{0:T(256)} %param.34) | copy-start | bytes 2308
  85.3 16.5 %all-to-all-start.3 = ((bf16[16,112,128]{2,1,0:T(8,128)(2,1)}), bf16[16,112,128]{2,1,0:T(8,128)(2,1)S(1)}, u32[]{:S(2)}, u32[]{:S(2)}) async-start(bf16[16,112,128]{2,1,0:T(8,128)(2,1)} %bitcast.12), calls=%async_computation.3 | async-start | bytes 917504 | tf_op jit(solution)/shard_map/all_to_all | solution.py:1296
  89.1 1.2 %collective-permute-start.6 = (f32[2,192]{1,0:T(2,128)S(1)}, f32[2,192]{1,0:T(2,128)S(1)}, u32[]{:S(2)}, u32[]{:S(2)}) collective-permute-start(f32[2,192]{1,0:T(2,128)S(1)} %pad_maximum_fusion), channel_id=1, source_target_pairs={{0,1},{1,0},{2,3},{3,2},{4,5},{5,4},{6,7},{7,6},{8,9},{9,8},{10,11... | collective-permute-start | bytes 4616 | tf_op jit(solution)/shard_map/ppermute | solution.py:1191
  105.2 1.2 %collective-permute-start.5 = (f32[16,128]{1,0:T(8,128)S(1)}, f32[16,128]{1,0:T(8,128)S(1)}, u32[]{:S(2)}, u32[]{:S(2)}) collective-permute-start(f32[16,128]{1,0:T(8,128)S(1)} %get-tuple-element.170.refs_0_), channel_id=1, source_target_pairs={{0,1},{1,0},{2,3},{3,2},{4,5},{5,4},{6,7},{7,6},{8,9},{9,8},{10,11... | collective-permute-start | bytes 24584 | tf_op jit(solution)/shard_map/ppermute | solution.py:1191

commit v6 on v5

--- a/solution.py
+++ b/solution.py
@@ -84,7 +84,7 @@
 
 def front_kernel(
     hid, gain, w_mix, w_gate, seg, taps, w_xp,
-    mix_out, gate_out, conv_out, part_out, norm_out, low_out, same_out, params, near_dt, near_cot,
+    mix_out, gate_out, conv_out, part_out, norm_out, low_out, same_out, params, near_dt, near_cot, near_out,
     padded, sgpad,
     *, need, save,
 ):
@@ -279,10 +279,23 @@
             rates[heading, n : n + 1, :] = jnp.minimum(value, FLOOR)
 
 
+def activate_kernel(conv_pre, act, *, need, save):
+    for heading in range(2):
+        for tile in range(conv_pre.shape[2] // LANES):
+
+            def activate(start, held, heading=heading, tile=tile):
+                here = pl.ds(start, SPAN)
+                pre = conv_pre[heading, here, cols(tile)]
+                act[heading, here, cols(tile)] = pre * sigmoid(pre)
+                return held
+
+            each_rows(conv_pre.shape[1], activate, 0, SPAN)
+
+
 def forward_kernel(
-    own_part, far_part, params, w_dt, cot_own, cot_far, w_out, conv_pre, gate, same, normed, core,
+    own_part, far_part, params, w_dt, cot_own, cot_far, w_out, conv_pre, act, gate, same, normed, core,
     states_out, proj, grad_maps, skips, far_step, grad_y, pre_step, inflow_low, gate_low, branch_low, early,
-    grad_branch, inflow, grad_y_low, act, result, maps, diagonal, gathered, states, low_one, low_two,
+    grad_branch, inflow, grad_y_low, result, maps, diagonal, gathered, states, low_one, low_two,
     rates, sems,
     *, need, save,
 ):
@@ -301,16 +314,6 @@
         first = heading * rows + rank
         group_maps(maps, proj[first : first + count, :], heading, count)
         diagonal_maps(diagonal, proj[first + count : first + 2 * count, :], heading, count)
-    for tile in range(tiles):
-
-        def activate(start, held, tile=tile):
-            here = pl.ds(start, SPAN)
-            for heading in range(2):
-                pre = conv_pre[heading, here, cols(tile)]
-                act[heading, here, cols(tile)] = pre * sigmoid(pre)
-            return held
-
-        each_rows(tokens, activate, 0, SPAN)
     need(params, w_dt)
     fill_rates(rates, params, count)
     for heading in range(2):
@@ -590,7 +593,7 @@
         args,
         [
             pltpu.VMEM(square, f32), pltpu.VMEM(flat, f32), pltpu.VMEM(square, bf16), pltpu.VMEM(both, f32),
-            pltpu.VMEM(both, f32), pltpu.VMEM((2, groups, z.count, LANES), f32),
+            pltpu.VMEM((2, groups, z.count, LANES), f32),
             pltpu.VMEM((2, groups, 2, z.count, squared), bf16), pltpu.VMEM((2, groups, z.count, z.count), f32),
             pltpu.VMEM(states, bf16), slot, slot, pltpu.VMEM((2, z.count, z.chans), f32),
             pltpu.SemaphoreType.DMA((2, z.blocks)),
@@ -945,12 +948,29 @@
     spread[...] = jnp.broadcast_to(spread_of(u_mix, stats[4:5, :], u_mix.shape[0]), spread.shape)
 
 
+def apply_out_kernel(norms_own, norms_far, w_out, u_out, n_out, c_out, *, need, save):
+    chans = w_out.shape[0]
+    need(norms_own)
+    sums = jnp.sum(norms_own[...] + norms_far[...], axis=1, keepdims=True)
+    scale = learn_rate * jnp.sqrt(sums[1:2]) / (jnp.sqrt(sums[7:8]) + adam_eps)
+    need()
+
+    def one_out(start, held):
+        here = pl.ds(start, LAMB_ROWS)
+        fresh = w_out[here, :] - scale * u_out[here, :]
+        n_out[here, :] = fresh
+        c_out[here, :] = fresh.astype(bf16)
+        return held
+
+    each_rows(chans, one_out, 0, LAMB_ROWS)
+
+
 def apply_kernel(
     norms_own, norms_far, stats, mix_spread,
-    w_mix, w_gate, w_out, w_xp, w_dt, w_cv, w_cp,
-    u_mix, u_gate, u_out, u_xp, u_dt, u_cv, u_cp,
+    w_mix, w_gate, w_xp, w_dt, w_cv, w_cp,
+    u_mix, u_gate, u_xp, u_dt, u_cv, u_cp,
     gain, gain_first, gain_second, x_mix, y_mix, core, x_given, y_given,
-    n_in, c_in, n_out, c_out, n_xp, c_xp, n_dt, c_dt, n_cv, c_cv, n_cp, c_cp,
+    n_in, c_in, n_xp, c_xp, n_dt, c_dt, n_cv, c_cv, n_cp, c_cp,
     g_first, g_second, g_new, g_copy, norms_out, stats_out, x_in, y_in,
     sems,
     *, need, save,
@@ -987,15 +1007,6 @@
     each_rows(width, one_in, 0, LAMB_ROWS)
     save(n_in, c_in)
 
-    def one_out(start, held):
-        here = pl.ds(start, LAMB_ROWS)
-        fresh = w_out[here, :] - scales[2] * u_out[here, :]
-        n_out[here, :] = fresh
-        c_out[here, :] = fresh.astype(bf16)
-        return held
-
-    each_rows(chans, one_out, 0, LAMB_ROWS)
-    save(n_out, c_out)
     need()
     gain_grad = jnp.concatenate(
         [totals[12 + tile : 13 + tile, :] for tile in range(width // LANES)], axis=1
@@ -1217,7 +1228,7 @@
     def padded_rows(amount):
         return -(-amount // (dp * 16)) * 16 * dp
 
-    mixing, gate, conv_pre, part, normed, low_in, same, near_cp, near_dt, near_cot = call(
+    mixing, gate, conv_pre, part, normed, low_in, same, near_cp, near_dt, near_cot, near_out = call(
         front_kernel,
         at("h", shape(square, f32))
         + at("x", shape(square, f32), shape((2,) + square, f32), shape((2 * rows, tokens), f32))
@@ -1226,16 +1237,19 @@
         at("h", hidden_in, norm_gain) + at("0", in_weight) + at("1", in_weight)
         + at("h", segment_ids, conv_weight, w_xp),
         [pltpu.VMEM((tokens + 16, chans), f32), pltpu.VMEM((tokens + 16, LANES), f32)],
-        limit=14, micros=6, passed=at("h", w_cp, dtproj_weight, cot_own),
+        limit=14, micros=6, passed=at("h", w_cp, dtproj_weight, cot_own, out_weight),
     )
     part_far = swap(part)
+    act = call(
+        activate_kernel, at("x", shape((2,) + square, f32)), at("x", conv_pre), limit=4, micros=1
+    )[0]
     early_rows = padded_rows(tiles * width + (width // LANES) * chans)
     (
         states, proj, grad_maps, skips, far_step, grad_y, pre_step, inflow_low, gate_low, branch_low, early,
         conv_kept,
     ) = forward_call(
-        at("x", part, part_far, near_cp, near_dt, near_cot, cot_far) + at("h", out_weight)
-        + at("x", conv_pre, gate, same) + at("h", normed) + smem,
+        at("x", part, part_far, near_cp, near_dt, near_cot, cot_far, near_out)
+        + at("x", conv_pre, act, gate, same) + at("h", normed) + smem,
         z, early_rows, half_width, (7,),
     )
     early_pieces = send_pieces(early, dp)
@@ -1294,6 +1308,12 @@
     )
     late_copies, output, input_grad = lax.optimization_barrier((join_pieces(late_pieces), output, input_grad))
     late_sums = lax.all_to_all(late_copies, "dp", 0, 0, tiled=True)
+    n_out, c_out = call(
+        apply_out_kernel, at("h", whole_out, shape(whole_out.shape, bf16)),
+        at("h", early_norms) + at("x", swap(early_norms)) + at("h", out_weight, u_out),
+        limit=8, micros=2,
+    )
+    late_sums, n_out, c_out = lax.optimization_barrier((late_sums, n_out, c_out))
     shapes = [shape(tensor.shape, f32) for tensor in weights]
     late_outs = []
     for entry in shapes:
@@ -1306,16 +1326,16 @@
         at("x", late_sums) + at("h", early_norms, early_stats, *moments_in)
         + at("0", first_in_weight, second_in_weight),
         limit=12, micros=5,
-        passed=at("h", *weights) + at("0", in_weight) + at("1", in_weight) + at("h", out_weight, u_gate, u_out),
+        passed=at("h", *weights) + at("0", in_weight) + at("1", in_weight) + at("h", u_gate),
     )
     moments, updates, norms, stats, kept = got[:10], got[10:15], got[15], got[16], got[17:]
-    kept_small, (kept_mix, kept_gate, kept_out, changed_gate, changed_out) = kept[0:4], kept[4:]
+    kept_small, (kept_mix, kept_gate, changed_gate) = kept[0:4], kept[4:]
     norms_far = swap(norms)
     mix_spread = call(
         spread_kernel, at("x", shape((8, chans), f32)), at("x", updates[0], stats), limit=8, micros=1
     )[0]
     pairs = []
-    for entry in [whole_in, whole_out, *shapes]:
+    for entry in [whole_in, *shapes]:
         pairs += [entry, shape(entry.shape, bf16)]
     row = shape((half_width,), f32)
     whole_low = shape(whole_in.shape, bf16)
@@ -1327,23 +1347,25 @@
             shape((2, chans), f32),
         )
         + at("m", whole_in, whole_in),
-        at("x", norms, norms_far, stats, mix_spread, kept_mix, kept_gate, kept_out, *kept_small, updates[0], changed_gate, changed_out, *updates[1:])
+        at("x", norms, norms_far, stats, mix_spread, kept_mix, kept_gate, *kept_small, updates[0], changed_gate, *updates[1:])
         + at("h", norm_gain) + at("x", moments_gain[0:1], moments_gain[1:2], moments[0], moments[1])
         + smem + at("m", x_in, y_in),
         [pltpu.SemaphoreType.DMA((2,))],
-        limit=14, micros=5, aliases={24: 18, 25: 19},
-    )
-    flat = list(done[12:16])
-    firsts_out = [done[18], x_out, *moments[2::2]]
-    seconds_out = [done[19], y_out, *moments[3::2]]
+        limit=14, micros=5, aliases={22: 16, 23: 17},
+    )
+    flat = list(done[10:14])
+    firsts_out = [done[16], x_out, *moments[2::2]]
+    seconds_out = [done[17], y_out, *moments[3::2]]
+    fresh = [done[0], n_out, *done[2:10:2]]
+    copied = [done[1], c_out, *done[3:10:2]]
     for place in range(6):
-        entry = [firsts_out[place], seconds_out[place], done[2 * place], done[2 * place + 1]]
+        entry = [firsts_out[place], seconds_out[place], fresh[place], copied[place]]
         if place == 2:
             entry = [flip(tensor) for tensor in entry]
         if place == 5:
             entry = [turn(tensor) for tensor in entry]
         flat += entry
-    return (output.T, input_grad.T, *flat, done[16].T, done[17])
+    return (output.T, input_grad.T, *flat, done[14].T, done[15])
 
 
 def solution(mesh):

time: 110 us -> 109 us (level)
  waiting for transfers between devices: 28.4 us -> 25.3 us
  Pallas kernels: 56 us -> 57.7 us
    all_to_all x1, waiting for transfers between devices: 6.57 us -> 3.68 us  [program(): late_sums = lax.all_to_all(late_copies, 'dp', 0, 0, tiled=True)]
    pallas_call x11 -> x13, Pallas kernels: 56 us -> 57.7 us  [call(): pl.pallas_call(body, out_shape=[out if kind == 'x' else pltpu.HBM(out.sha...]
    ppermute x7 -> x8, waiting for transfers between devices: 6.33 us -> 6.24 us  [swap(): return lax.ppermute(values, 'chan', [(0, 1), (1, 0)])]
  transfers between devices with their start and end apart: 11 -> 12, of which waited for: 9 -> 9; matrix products, arithmetic and copies ran while one was open for 0% -> 0% of each run, Pallas kernels for 29% -> 32%
where the time goes in v6:
time: 109 us; the launch traced here: 108 us
  Pallas kernels  57.7 us (53%)
  waiting for transfers between devices  25.3 us (23%)
  starting transfers between devices  24.2 us (22%)
    pallas_call x13, Pallas kernels, call(): pl.pallas_call(body, out_shape=[out if kind == 'x' else pltpu.HBM(out.sha...  57.7 us
    all_to_all x2, starting transfers between devices, send_pieces(): lax.all_to_all(values, 'dp', 0, 0, tiled=True).reshape(dp, chunk, LANES)  12.3 us
    all_to_all x2, waiting for transfers between devices, send_pieces(): lax.all_to_all(values, 'dp', 0, 0, tiled=True).reshape(dp, chunk, LANES)  8.8 us
    all_to_all x1, starting transfers between devices, program(): early_sums = lax.all_to_all(early_copies, 'dp', 0, 0, tiled=True)  6.69 us
    all_to_all x1, waiting for transfers between devices, program(): early_sums = lax.all_to_all(early_copies, 'dp', 0, 0, tiled=True)  6.63 us
    ppermute x8, waiting for transfers between devices, swap(): return lax.ppermute(values, 'chan', [(0, 1), (1, 0)])  6.24 us
    all_to_all x1, starting transfers between devices, program(): late_sums = lax.all_to_all(late_copies, 'dp', 0, 0, tiled=True)  3.73 us
    all_to_all x1, waiting for transfers between devices, program(): late_sums = lax.all_to_all(late_copies, 'dp', 0, 0, tiled=True)  3.68 us
  transfers between devices with their start and end apart: 12, of which 9 were waited for; matrix products, arithmetic and copies ran while one was open for 0% of the time, Pallas kernels for 32%

profile of v6, /device:TPU:0, one launch (start us, length us, event | category | flops | bytes accessed | tf_op | source)
XLA Modules:
  0.0 108.4 jit_solution(9941081465077399029)
XLA Ops:
  0.7 3.7 %shard_map.479 = (f32[384,384]{1,0:T(8,128)}, f32[384,384]{1,0:T(8,128)S(1)}, f32[2,384,384]{2,1,0:T(8,128)S(1)}, f32[112,384]{1,0:T(8,128)S(1)}, bf16[384,384]{...) custom-call(bf16[384,384]{1,0:T(8,128)(2,1)} %refs_0_.3, ...), custom_call_target="tpu_custom_call" | custom-call | flops 6000000000 | bytes 1048576 | tf_op jit(solution)/shard_map/pallas_call | solution.py:1167
  4.4 0.5 collective-permute-start
  4.9 0.1 collective-permute-start.1
  5.0 0.4 shard_map.480.refs_8_
  5.3 1.1 %collective-permute-done.1.refs_5_ = bf16[192,384]{1,0:T(8,128)(2,1)S(1)} collective-permute-done((bf16[192,384]{1,0:T(8,128)(2,1)}, bf16[192,384]{1,0:T(8,128)(2,1)S(1)}, u32[]{:S(2)}, u32[]{:S(2)}) %collective-permute-start.1) | collective-permute-done | bytes 147488 | tf_op jit(solution)/shard_map/ppermute | solution.py:1202
  6.5 0.0 collective-permute-done.refs_1_
  6.5 11.4 %shard_map.481 = (bf16[2,6160,384]{2,1,0:T(8,128)(2,1)}, f32[112,384]{1,0:T(8,128)}, f32[32,384]{1,0:T(8,128)}, f32[8,384]{1,0:T(8,128)}, f32[2304,128]{1,0:T(8,...) custom-call(f32[112,384]{1,0:T(8,128)S(1)} %get-tuple-element.128.re, ...), custom_call_target="tpu_custom_call" | custom-call | flops 15000000512 | bytes 1048576 | tf_op jit(solution)/shard_map/pallas_call | solution.py:1167
  17.9 8.1 %all-to-all-start = ((bf16[16,144,128]{2,1,0:T(8,128)(2,1)}), bf16[16,144,128]{2,1,0:T(8,128)(2,1)S(1)}, u32[]{:S(2)}, u32[]{:S(2)}) async-start(bf16[16,144,128]{2,1,0:T(8,128)(2,1)} %bitcast.4), calls=%async_computation | async-start | bytes 1179648 | tf_op jit(solution)/shard_map/all_to_all | solution.py:1067
  26.0 16.4 %shard_map.483 = (f32[112,384]{1,0:T(8,128)S(1)}, f32[2,384,384]{2,1,0:T(8,128)S(1)}, f32[2,24,384]{2,1,0:T(8,128)S(1)}, f32[19,2,384]{2,1,0:T(2,128)S(1)}) custom-call(bf16[2,6160,384]{2,1,0:T(8,128)(2,1)} %get-tuple-element.138.refs_0_, f32[19,2,384]{2,1,0:T(2,128)} %bitcast.41, f32[112,384]{1,0:T(8,128)} %get-tuple-element.139.refs_2_, ...), custom_call_target="tpu_custom_call" | custom-call | flops 15000000512 | bytes 1048576 | tf_op jit(solution)/shard_map/pallas_call | solution.py:1167
  42.4 0.2 all-to-all-done.refs_0_
  42.6 0.9 shard_map.482
  43.5 6.7 %all-to-all-start.1 = ((bf16[16,144,128]{2,1,0:T(8,128)(2,1)}), bf16[16,144,128]{2,1,0:T(8,128)(2,1)S(1)}, u32[]{:S(2)}, u32[]{:S(2)}) async-start(bf16[16,144,128]{2,1,0:T(8,128)(2,1)} %bitcast.6), calls=%async_computation.1 | async-start | bytes 1179648 | tf_op jit(solution)/shard_map/all_to_all | solution.py:1262
  50.2 0.1 collective-permute-start.2
  50.3 1.4 %collective-permute-done.2.refs_1_ = f32[112,384]{1,0:T(8,128)S(1)} collective-permute-done((f32[112,384]{1,0:T(8,128)S(1)}, f32[112,384]{1,0:T(8,128)S(1)}, u32[]{:S(2)}, u32[]{:S(2)}) %collective-permute-start.2) | collective-permute-done | bytes 172064 | tf_op jit(solution)/shard_map/ppermute | solution.py:1202
  51.7 0.0 copy-start
  51.7 0.0 copy-start.1
  51.7 8.0 %shard_map.484 = (bf16[1792,128]{1,0:T(8,128)(2,1)}, f32[200,384]{1,0:T(8,128)}, f32[200,384]{1,0:T(8,128)S(1)}, f32[192,384]{1,0:T(8,128)}, f32[192,384]{1,0:T(8,128)S(1)}) custom-call(f32[112,384]{1,0:T(8,128)S(1)} %get-tuple-element.148.refs_0_, f32[112,384]{1,0:T(8,128)S(1)} %collective-permute-done.2.refs_1_, s32[384]{0:T(512)} %refs_2_.5, ...), custom_call_target="tpu_custom_call" | custom-call | flops 2000000000 | bytes 1048576 | tf_op jit(solution)/shard_map/pallas_call | solution.py:1167
  59.7 6.6 %all-to-all-done.1 = bf16[16,144,128]{2,1,0:T(8,128)(2,1)S(1)} async-done(((bf16[16,144,128]{2,1,0:T(8,128)(2,1)}), bf16[16,144,128]{2,1,0:T(8,128)(2,1)S(1)}, u32[]{:S(2)}, u32[]{:S(2)}) %all-to-all-start.1) | async-done | bytes 589856 | tf_op jit(solution)/shard_map/all_to_all | solution.py:1262
  66.4 4.1 %all-to-all-start.2 = ((bf16[16,112,128]{2,1,0:T(8,128)(2,1)}), bf16[16,112,128]{2,1,0:T(8,128)(2,1)S(1)}, u32[]{:S(2)}, u32[]{:S(2)}) async-start(bf16[16,112,128]{2,1,0:T(8,128)(2,1)} %bitcast.8), calls=%async_computation.2 | async-start | bytes 917504 | tf_op jit(solution)/shard_map/all_to_all | solution.py:1067
  70.5 0.1 collective-permute-start.4
  70.6 0.5 collective-permute-start.3
  71.1 0.0 copy-done
  71.1 0.0 copy-done.1
  71.1 0.1 collective-permute-start.7
  71.3 1.3 %collective-permute-done.7 = f32[2,192]{1,0:T(2,128)S(1)} collective-permute-done((f32[2,192]{1,0:T(2,128)S(1)}, f32[2,192]{1,0:T(2,128)S(1)}, u32[]{:S(2)}, u32[]{:S(2)}) %collective-permute-start.7) | collective-permute-done | bytes 1568 | tf_op jit(solution)/shard_map/ppermute | solution.py:1202
  72.6 0.1 maximum_select_fusion
  72.7 0.0 collective-permute-done.3.refs_3_
  72.7 0.0 collective-permute-done.4.refs_5_
  72.7 2.3 %shard_map.486 = (bf16[192,384]{1,0:T(8,128)(2,1)}, f32[192,384]{1,0:T(8,128)}) custom-call(bf16[384,384]{1,0:T(8,128)(2,1)} %refs_0_.3, bf16[192,384]{1,0:T(8,128)(2,1)} %bitcast.2.refs_9_.refs_1_, f32[192,384]{1,0:T(8,128)} %get-tuple-element.159.refs_2_, f32[192,384]{1,0:T(8,128)S(1)} %collective-permute-done.3.refs_3_, ...), custom_call_target="tpu_custom_call" | custom-call | flops 3000000000 | bytes 1048576 | tf_op jit(solution)/shard_map/pallas_call | solution.py:1167
  75.0 8.6 %all-to-all-done.2.refs_0_ = bf16[16,112,128]{2,1,0:T(8,128)(2,1)S(1)} async-done(((bf16[16,112,128]{2,1,0:T(8,128)(2,1)}), bf16[16,112,128]{2,1,0:T(8,128)(2,1)S(1)}, u32[]{:S(2)}, u32[]{:S(2)}) %all-to-all-start.2) | async-done | bytes 458784 | tf_op jit(solution)/shard_map/all_to_all | solution.py:1067
  83.6 0.9 shard_map.485
  84.5 3.7 %all-to-all-start.3 = ((bf16[16,112,128]{2,1,0:T(8,128)(2,1)}), bf16[16,112,128]{2,1,0:T(8,128)(2,1)S(1)}, u32[]{:S(2)}, u32[]{:S(2)}) async-start(bf16[16,112,128]{2,1,0:T(8,128)(2,1)} %bitcast.12), calls=%async_computation.3 | async-start | bytes 917504 | tf_op jit(solution)/shard_map/all_to_all | solution.py:1310
  88.2 4.9 %shard_map.487 = (f32[384,384]{1,0:T(8,128)}, f32[384,384]{1,0:T(8,128)}, f32[384,2,384]{2,1,0:T(2,128)}, f32[384,2,384]{2,1,0:T(2,128)}, f32[384,384]{1,0:T(8,1...) custom-call(bf16[2304,128]{1,0:T(8,128)(2,1)S(1)} %bitcast.29, f32[384,384]{1,0:T(8,128)} %refs_2_.7, ...), custom_call_target="tpu_custom_call" | custom-call | flops 5000000000 | bytes 1048576 | tf_op jit(solution)/shard_map/pallas_call | solution.py:1167
  93.1 0.1 collective-permute-start.5
  93.2 1.4 %collective-permute-done.5.refs_1_ = f32[16,128]{1,0:T(8,128)S(1)} collective-permute-done((f32[16,128]{1,0:T(8,128)}, f32[16,128]{1,0:T(8,128)S(1)}, u32[]{:S(2)}, u32[]{:S(2)}) %collective-permute-start.5) | collective-permute-done | bytes 8224 | tf_op jit(solution)/shard_map/ppermute | solution.py:1202
  94.5 2.8 %shard_map.488 = (f32[384,384]{1,0:T(8,128)}, bf16[384,384]{1,0:T(8,128)(2,1)}) custom-call(f32[16,128]{1,0:T(8,128)} %get-tuple-element.169.refs_0_.refs_1_, f32[16,128]{1,0:T(8,128)S(1)} %collective-permute-done.5.refs_1_, f32[384,384]{1,0:T(8,128)} %refs_2_.7, f32[384,384]{1,0:T(8,128)} %get-tuple-element.170.refs_3_), custom_call_target="tpu_custom_call" | custom-call | flops 2000000000 | bytes 1048576 | tf_op jit(solution)/shard_map/pallas_call | solution.py:1167
  97.3 3.7 %all-to-all-done.3 = bf16[16,112,128]{2,1,0:T(8,128)(2,1)S(1)} async-done(((bf16[16,112,128]{2,1,0:T(8,128)(2,1)}), bf16[16,112,128]{2,1,0:T(8,128)(2,1)S(1)}, u32[]{:S(2)}, u32[]{:S(2)}) %all-to-all-start.3) | async-done | bytes 458784 | tf_op jit(solution)/shard_map/all_to_all | solution.py:1310
  101.0 3.3 %shard_map.489 = (f32[384,384]{1,0:T(8,128)S(1)}, f32[384,384]{1,0:T(8,128)S(1)}, f32[2,56,384]{2,1,0:T(8,128)}, f32[2,56,384]{2,1,0:T(8,128)}, f32[2,24,384]{2,...) custom-call(bf16[1792,128]{1,0:T(8,128)(2,1)S(1)} %bitcast.30, ...), custom_call_target="tpu_custom_call" | custom-call | flops 5000000000 | bytes 1048576 | tf_op jit(solution)/shard_map/pallas_call | solution.py:1167
  104.2 0.1 collective-permute-start.6
  104.3 0.2 shard_map.490.refs_3_
  104.5 1.0 collective-permute-done.6.refs_1_
  105.5 2.7 %shard_map.491 = (f32[384,2,384]{2,1,0:T(2,128)}, bf16[384,2,384]{2,1,0:T(2,128)(2,1)}, f32[2,56,384]{2,1,0:T(8,128)}, bf16[2,56,384]{2,1,0:T(8,128)(2,1)}, f32[...) custom-call(f32[16,128]{1,0:T(8,128)S(1)} %get-tuple-element.176.ref, ...), custom_call_target="tpu_custom_call", output_to_operand_aliasing={{16}: (22, {}), {17}: (23, {})} | custom-call | flops 5000000000 | bytes 1048576 | tf_op jit(solution)/shard_map/pallas_call | solution.py:1167
  (2 shorter events, 0.0 us)
Async XLA Ops:
  4.4 2.1 %collective-permute-start = (f32[112,384]{1,0:T(8,128)S(1)}, f32[112,384]{1,0:T(8,128)S(1)}, u32[]{:S(2)}, u32[]{:S(2)}) collective-permute-start(f32[112,384]{1,0:T(8,128)S(1)} %get-tuple-element.128.refs_0_), channel_id=1, source_target_pairs={{0,1},{1,0},{2,3},{3,2},{4,5},{5,4},{6,7},{7,6},{8,9},{9,8},{10,11... | collective-permute-start | bytes 516104 | tf_op jit(solution)/shard_map/ppermute | solution.py:1202
  4.9 1.6 %collective-permute-start.1 = (bf16[192,384]{1,0:T(8,128)(2,1)}, bf16[192,384]{1,0:T(8,128)(2,1)S(1)}, u32[]{:S(2)}, u32[]{:S(2)}) collective-permute-start(bf16[192,384]{1,0:T(8,128)(2,1)} %bitcast.2.refs_9_.refs_1_), channel_id=1, source_target_pairs={{0,1},{1,0},{2,3},{3,2},{4,5},{5,4},{6,7},{7,6},{8,9},{9,8},{10,11... | collective-permute-start | bytes 442376 | tf_op jit(solution)/shard_map/ppermute | solution.py:1202
  17.9 24.7 %all-to-all-start = ((bf16[16,144,128]{2,1,0:T(8,128)(2,1)}), bf16[16,144,128]{2,1,0:T(8,128)(2,1)S(1)}, u32[]{:S(2)}, u32[]{:S(2)}) async-start(bf16[16,144,128]{2,1,0:T(8,128)(2,1)} %bitcast.4), calls=%async_computation | async-start | bytes 1179648 | tf_op jit(solution)/shard_map/all_to_all | solution.py:1067
  43.5 22.8 %all-to-all-start.1 = ((bf16[16,144,128]{2,1,0:T(8,128)(2,1)}), bf16[16,144,128]{2,1,0:T(8,128)(2,1)S(1)}, u32[]{:S(2)}, u32[]{:S(2)}) async-start(bf16[16,144,128]{2,1,0:T(8,128)(2,1)} %bitcast.6), calls=%async_computation.1 | async-start | bytes 1179648 | tf_op jit(solution)/shard_map/all_to_all | solution.py:1262
  50.2 1.5 %collective-permute-start.2 = (f32[112,384]{1,0:T(8,128)S(1)}, f32[112,384]{1,0:T(8,128)S(1)}, u32[]{:S(2)}, u32[]{:S(2)}) collective-permute-start(f32[112,384]{1,0:T(8,128)S(1)} %get-tuple-element.148.refs_0_), channel_id=1, source_target_pairs={{0,1},{1,0},{2,3},{3,2},{4,5},{5,4},{6,7},{7,6},{8,9},{9,8},{10,11... | collective-permute-start | bytes 516104 | tf_op jit(solution)/shard_map/ppermute | solution.py:1202
  51.7 19.4 %copy-start = (f32[192]{0:T(256)S(1)}, f32[192]{0:T(256)}, u32[]{:S(2)}) copy-start(f32[192]{0:T(256)} %param.41) | copy-start | bytes 2308
  51.7 19.4 %copy-start.1 = (f32[192]{0:T(256)S(1)}, f32[192]{0:T(256)}, u32[]{:S(2)}) copy-start(f32[192]{0:T(256)} %param.34) | copy-start | bytes 2308
  66.4 17.2 %all-to-all-start.2 = ((bf16[16,112,128]{2,1,0:T(8,128)(2,1)}), bf16[16,112,128]{2,1,0:T(8,128)(2,1)S(1)}, u32[]{:S(2)}, u32[]{:S(2)}) async-start(bf16[16,112,128]{2,1,0:T(8,128)(2,1)} %bitcast.8), calls=%async_computation.2 | async-start | bytes 917504 | tf_op jit(solution)/shard_map/all_to_all | solution.py:1067
  70.5 2.2 %collective-permute-start.4 = (f32[200,384]{1,0:T(8,128)S(1)}, f32[200,384]{1,0:T(8,128)S(1)}, u32[]{:S(2)}, u32[]{:S(2)}) collective-permute-start(f32[200,384]{1,0:T(8,128)S(1)} %get-tuple-element.162), channel_id=1, source_target_pairs={{0,1},{1,0},{2,3},{3,2},{4,5},{5,4},{6,7},{7,6},{8,9},{9,8},{10,11... | collective-permute-start | bytes 921608 | tf_op jit(solution)/shard_map/ppermute | solution.py:1202
  70.6 2.1 %collective-permute-start.3 = (f32[192,384]{1,0:T(8,128)S(1)}, f32[192,384]{1,0:T(8,128)S(1)}, u32[]{:S(2)}, u32[]{:S(2)}) collective-permute-start(f32[192,384]{1,0:T(8,128)S(1)} %get-tuple-element.160), channel_id=1, source_target_pairs={{0,1},{1,0},{2,3},{3,2},{4,5},{5,4},{6,7},{7,6},{8,9},{9,8},{10,11... | collective-permute-start | bytes 884744 | tf_op jit(solution)/shard_map/ppermute | solution.py:1202
  71.1 1.5 %collective-permute-start.7 = (f32[2,192]{1,0:T(2,128)S(1)}, f32[2,192]{1,0:T(2,128)S(1)}, u32[]{:S(2)}, u32[]{:S(2)}) collective-permute-start(f32[2,192]{1,0:T(2,128)S(1)} %pad_maximum_fusion), channel_id=1, source_target_pairs={{0,1},{1,0},{2,3},{3,2},{4,5},{5,4},{6,7},{7,6},{8,9},{9,8},{10,11... | collective-permute-start | bytes 4616 | tf_op jit(solution)/shard_map/ppermute | solution.py:1202
  84.5 16.5 %all-to-all-start.3 = ((bf16[16,112,128]{2,1,0:T(8,128)(2,1)}), bf16[16,112,128]{2,1,0:T(8,128)(2,1)S(1)}, u32[]{:S(2)}, u32[]{:S(2)}) async-start(bf16[16,112,128]{2,1,0:T(8,128)(2,1)} %bitcast.12), calls=%async_computation.3 | async-start | bytes 917504 | tf_op jit(solution)/shard_map/all_to_all | solution.py:1310
  93.1 1.4 %collective-permute-start.5 = (f32[16,128]{1,0:T(8,128)}, f32[16,128]{1,0:T(8,128)S(1)}, u32[]{:S(2)}, u32[]{:S(2)}) collective-permute-start(f32[16,128]{1,0:T(8,128)} %get-tuple-element.169.refs_0_.refs_1_), channel_id=1, source_target_pairs={{0,1},{1,0},{2,3},{3,2},{4,5},{5,4},{6,7},{7,6},{8,9},{9,8},{10,11... | collective-permute-start | bytes 24584 | tf_op jit(solution)/shard_map/ppermute | solution.py:1202
  104.2 1.2 %collective-permute-start.6 = (f32[16,128]{1,0:T(8,128)S(1)}, f32[16,128]{1,0:T(8,128)S(1)}, u32[]{:S(2)}, u32[]{:S(2)}) collective-permute-start(f32[16,128]{1,0:T(8,128)S(1)} %get-tuple-element.176.refs_0_), channel_id=1, source_target_pairs={{0,1},{1,0},{2,3},{3,2},{4,5},{5,4},{6,7},{7,6},{8,9},{9,8},{10,11... | collective-permute-start | bytes 24584 | tf_op jit(solution)/shard_map/ppermute | solution.py:1202

commit v7 on v6

--- a/solution.py
+++ b/solution.py
@@ -231,16 +231,17 @@
 
 
 class Sweep:
-    def __init__(self, z, turned):
-        self.z, self.turned = z, turned
+    def __init__(self, z, turned, stages):
+        self.z, self.turned, self.stages = z, turned, stages
+        self.stage_rows = z.tokens * z.count // stages
         self.groups = z.tokens // z.count
-        self.stage_groups = self.groups // z.blocks
+        self.stage_groups = self.groups // stages
 
     def group(self, order, heading):
         return self.groups - 1 - order if heading == self.turned else order
 
     def block(self, stage, heading):
-        return self.z.blocks - 1 - stage if heading == self.turned else stage
+        return self.stages - 1 - stage if heading == self.turned else stage
 
     def inner(self, ahead, heading):
         return self.z.count - 1 - ahead if heading == self.turned else ahead
@@ -257,7 +258,7 @@
             return scan(order + 1, held, 1)
 
         per = self.stage_groups // 2
-        for stage in range(z.blocks):
+        for stage in range(self.stages):
             between(stage, True)
             carried = lax.fori_loop(stage * per, (stage + 1) * per, step, carried)
             between(stage, False)
@@ -305,7 +306,7 @@
     half_width = cot_own.shape[0]
     width = 2 * half_width
     me = core[0]
-    sweep = Sweep(z, 1)
+    sweep = Sweep(z, 1, sems.shape[1])
     lows = (low_one, low_two)
 
     proj[...] = own_part[...] + far_part[...]
@@ -391,7 +392,7 @@
         if before:
             return
         for heading in range(2):
-            begin, extent = sweep.block(stage, heading) * z.block_rows, z.block_rows
+            begin, extent = sweep.block(stage, heading) * sweep.stage_rows, sweep.stage_rows
             if stage == 0:
                 extent += count
             elif heading == 0:
@@ -456,13 +457,13 @@
     _, tokens, chans = conv_pre.shape
     z = Sizes(tokens, chans, params.shape[0] - 3, w_dt.shape[1])
     count, rank, rows, tiles = z.count, z.rank, z.rows, z.tiles
-    sweep = Sweep(z, 0)
+    sweep = Sweep(z, 0, sems.shape[1])
     lows, products = (low_one, low_two), (products_one, products_two)
     loads = {}
-    for stage in range(z.blocks):
+    for stage in range(sweep.stages):
         for heading in range(2):
-            begin = sweep.block(stage, heading) * z.block_rows + (count if heading == 1 else 0)
-            piece = pl.ds(begin, z.block_rows)
+            begin = sweep.block(stage, heading) * sweep.stage_rows + (count if heading == 1 else 0)
+            piece = pl.ds(begin, sweep.stage_rows)
             load = pltpu.make_async_copy(
                 states_in.at[heading, piece, :], states.at[heading, piece, :], sems.at[heading, stage]
             )
@@ -596,7 +597,7 @@
             pltpu.VMEM((2, groups, z.count, LANES), f32),
             pltpu.VMEM((2, groups, 2, z.count, squared), bf16), pltpu.VMEM((2, groups, z.count, z.count), f32),
             pltpu.VMEM(states, bf16), slot, slot, pltpu.VMEM((2, z.count, z.chans), f32),
-            pltpu.SemaphoreType.DMA((2, z.blocks)),
+            pltpu.SemaphoreType.DMA((2, 2 * z.blocks)),
         ],
         limit=limit, micros=15, kept=kept,
     )
@@ -620,7 +621,7 @@
             pltpu.VMEM(both, f32), pltpu.VMEM(both, f32), pltpu.VMEM((2, groups, z.count, LANES), f32),
             pltpu.VMEM((2, groups, 2, z.count, squared), bf16), pltpu.VMEM((2, groups, z.count, z.count), f32),
             pltpu.VMEM((2, (z.tokens + 1) * z.count, z.chans), bf16), slot, slot, slot, slot,
-            pltpu.VMEM((2, z.count, z.chans), f32), pltpu.SemaphoreType.DMA((2, z.blocks)),
+            pltpu.VMEM((2, z.count, z.chans), f32), pltpu.SemaphoreType.DMA((2, 2 * z.blocks)),
         ],
         limit=limit, micros=15,
     )

time: 109 us -> 109 us (level)
  no operation moved by 1% of the time
where the time goes in v7:
time: 109 us; the launch traced here: 108 us
  Pallas kernels  57.6 us (53%)
  waiting for transfers between devices  25.2 us (23%)
  starting transfers between devices  24.4 us (22%)
    pallas_call x13, Pallas kernels, call(): pl.pallas_call(body, out_shape=[out if kind == 'x' else pltpu.HBM(out.sha...  57.6 us
    all_to_all x2, starting transfers between devices, send_pieces(): lax.all_to_all(values, 'dp', 0, 0, tiled=True).reshape(dp, chunk, LANES)  12.3 us
    all_to_all x2, waiting for transfers between devices, send_pieces(): lax.all_to_all(values, 'dp', 0, 0, tiled=True).reshape(dp, chunk, LANES)  8.71 us
    all_to_all x1, starting transfers between devices, program(): early_sums = lax.all_to_all(early_copies, 'dp', 0, 0, tiled=True)  6.76 us
    all_to_all x1, waiting for transfers between devices, program(): early_sums = lax.all_to_all(early_copies, 'dp', 0, 0, tiled=True)  6.65 us
    ppermute x8, waiting for transfers between devices, swap(): return lax.ppermute(values, 'chan', [(0, 1), (1, 0)])  6.24 us
    all_to_all x1, starting transfers between devices, program(): late_sums = lax.all_to_all(late_copies, 'dp', 0, 0, tiled=True)  3.83 us
    all_to_all x1, waiting for transfers between devices, program(): late_sums = lax.all_to_all(late_copies, 'dp', 0, 0, tiled=True)  3.58 us
  transfers between devices with their start and end apart: 12, of which 9 were waited for; matrix products, arithmetic and copies ran while one was open for 0% of the time, Pallas kernels for 32%

profile of v7, /device:TPU:0, one launch (start us, length us, event | category | flops | bytes accessed | tf_op | source)
XLA Modules:
  0.0 108.3 jit_solution(1467315758022127512)
XLA Ops:
  0.7 3.7 %shard_map.479 = (f32[384,384]{1,0:T(8,128)}, f32[384,384]{1,0:T(8,128)S(1)}, f32[2,384,384]{2,1,0:T(8,128)S(1)}, f32[112,384]{1,0:T(8,128)S(1)}, bf16[384,384]{...) custom-call(bf16[384,384]{1,0:T(8,128)(2,1)} %refs_0_.3, ...), custom_call_target="tpu_custom_call" | custom-call | flops 6000000000 | bytes 1048576 | tf_op jit(solution)/shard_map/pallas_call | solution.py:1168
  4.4 0.5 collective-permute-start
  4.9 0.1 collective-permute-start.1
  5.0 0.4 shard_map.480.refs_8_
  5.3 1.1 %collective-permute-done.1.refs_5_ = bf16[192,384]{1,0:T(8,128)(2,1)S(1)} collective-permute-done((bf16[192,384]{1,0:T(8,128)(2,1)}, bf16[192,384]{1,0:T(8,128)(2,1)S(1)}, u32[]{:S(2)}, u32[]{:S(2)}) %collective-permute-start.1) | collective-permute-done | bytes 147488 | tf_op jit(solution)/shard_map/ppermute | solution.py:1203
  6.5 0.0 collective-permute-done.refs_1_
  6.5 11.2 %shard_map.481 = (bf16[2,6160,384]{2,1,0:T(8,128)(2,1)}, f32[112,384]{1,0:T(8,128)}, f32[32,384]{1,0:T(8,128)}, f32[8,384]{1,0:T(8,128)}, f32[2304,128]{1,0:T(8,...) custom-call(f32[112,384]{1,0:T(8,128)S(1)} %get-tuple-element.128.re, ...), custom_call_target="tpu_custom_call" | custom-call | flops 15000000512 | bytes 1048576 | tf_op jit(solution)/shard_map/pallas_call | solution.py:1168
  17.7 8.1 %all-to-all-start = ((bf16[16,144,128]{2,1,0:T(8,128)(2,1)}), bf16[16,144,128]{2,1,0:T(8,128)(2,1)S(1)}, u32[]{:S(2)}, u32[]{:S(2)}) async-start(bf16[16,144,128]{2,1,0:T(8,128)(2,1)} %bitcast.4), calls=%async_computation | async-start | bytes 1179648 | tf_op jit(solution)/shard_map/all_to_all | solution.py:1068
  25.8 16.4 %shard_map.483 = (f32[112,384]{1,0:T(8,128)S(1)}, f32[2,384,384]{2,1,0:T(8,128)S(1)}, f32[2,24,384]{2,1,0:T(8,128)S(1)}, f32[19,2,384]{2,1,0:T(2,128)S(1)}) custom-call(bf16[2,6160,384]{2,1,0:T(8,128)(2,1)} %get-tuple-element.138.refs_0_, f32[19,2,384]{2,1,0:T(2,128)} %bitcast.41, f32[112,384]{1,0:T(8,128)} %get-tuple-element.139.refs_2_, ...), custom_call_target="tpu_custom_call" | custom-call | flops 15000000512 | bytes 1048576 | tf_op jit(solution)/shard_map/pallas_call | solution.py:1168
  42.3 0.2 all-to-all-done.refs_0_
  42.4 0.9 shard_map.482
  43.4 6.8 %all-to-all-start.1 = ((bf16[16,144,128]{2,1,0:T(8,128)(2,1)}), bf16[16,144,128]{2,1,0:T(8,128)(2,1)S(1)}, u32[]{:S(2)}, u32[]{:S(2)}) async-start(bf16[16,144,128]{2,1,0:T(8,128)(2,1)} %bitcast.6), calls=%async_computation.1 | async-start | bytes 1179648 | tf_op jit(solution)/shard_map/all_to_all | solution.py:1263
  50.1 0.1 collective-permute-start.2
  50.2 1.4 %collective-permute-done.2.refs_1_ = f32[112,384]{1,0:T(8,128)S(1)} collective-permute-done((f32[112,384]{1,0:T(8,128)S(1)}, f32[112,384]{1,0:T(8,128)S(1)}, u32[]{:S(2)}, u32[]{:S(2)}) %collective-permute-start.2) | collective-permute-done | bytes 172064 | tf_op jit(solution)/shard_map/ppermute | solution.py:1203
  51.6 0.0 copy-start
  51.6 0.0 copy-start.1
  51.6 8.0 %shard_map.484 = (bf16[1792,128]{1,0:T(8,128)(2,1)}, f32[200,384]{1,0:T(8,128)}, f32[200,384]{1,0:T(8,128)S(1)}, f32[192,384]{1,0:T(8,128)}, f32[192,384]{1,0:T(8,128)S(1)}) custom-call(f32[112,384]{1,0:T(8,128)S(1)} %get-tuple-element.148.refs_0_, f32[112,384]{1,0:T(8,128)S(1)} %collective-permute-done.2.refs_1_, s32[384]{0:T(512)} %refs_2_.5, ...), custom_call_target="tpu_custom_call" | custom-call | flops 2000000000 | bytes 1048576 | tf_op jit(solution)/shard_map/pallas_call | solution.py:1168
  59.6 6.6 %all-to-all-done.1 = bf16[16,144,128]{2,1,0:T(8,128)(2,1)S(1)} async-done(((bf16[16,144,128]{2,1,0:T(8,128)(2,1)}), bf16[16,144,128]{2,1,0:T(8,128)(2,1)S(1)}, u32[]{:S(2)}, u32[]{:S(2)}) %all-to-all-start.1) | async-done | bytes 589856 | tf_op jit(solution)/shard_map/all_to_all | solution.py:1263
  66.3 4.1 %all-to-all-start.2 = ((bf16[16,112,128]{2,1,0:T(8,128)(2,1)}), bf16[16,112,128]{2,1,0:T(8,128)(2,1)S(1)}, u32[]{:S(2)}, u32[]{:S(2)}) async-start(bf16[16,112,128]{2,1,0:T(8,128)(2,1)} %bitcast.8), calls=%async_computation.2 | async-start | bytes 917504 | tf_op jit(solution)/shard_map/all_to_all | solution.py:1068
  70.4 0.1 collective-permute-start.4
  70.5 0.5 collective-permute-start.3
  71.0 0.0 copy-done
  71.0 0.0 copy-done.1
  71.0 0.1 collective-permute-start.7
  71.2 1.3 %collective-permute-done.7 = f32[2,192]{1,0:T(2,128)S(1)} collective-permute-done((f32[2,192]{1,0:T(2,128)S(1)}, f32[2,192]{1,0:T(2,128)S(1)}, u32[]{:S(2)}, u32[]{:S(2)}) %collective-permute-start.7) | collective-permute-done | bytes 1568 | tf_op jit(solution)/shard_map/ppermute | solution.py:1203
  72.5 0.1 maximum_select_fusion
  72.6 0.0 collective-permute-done.3.refs_3_
  72.6 0.0 collective-permute-done.4.refs_5_
  72.6 2.3 %shard_map.486 = (bf16[192,384]{1,0:T(8,128)(2,1)}, f32[192,384]{1,0:T(8,128)}) custom-call(bf16[384,384]{1,0:T(8,128)(2,1)} %refs_0_.3, bf16[192,384]{1,0:T(8,128)(2,1)} %bitcast.2.refs_9_.refs_1_, f32[192,384]{1,0:T(8,128)} %get-tuple-element.159.refs_2_, f32[192,384]{1,0:T(8,128)S(1)} %collective-permute-done.3.refs_3_, ...), custom_call_target="tpu_custom_call" | custom-call | flops 3000000000 | bytes 1048576 | tf_op jit(solution)/shard_map/pallas_call | solution.py:1168
  74.9 8.6 %all-to-all-done.2.refs_0_ = bf16[16,112,128]{2,1,0:T(8,128)(2,1)S(1)} async-done(((bf16[16,112,128]{2,1,0:T(8,128)(2,1)}), bf16[16,112,128]{2,1,0:T(8,128)(2,1)S(1)}, u32[]{:S(2)}, u32[]{:S(2)}) %all-to-all-start.2) | async-done | bytes 458784 | tf_op jit(solution)/shard_map/all_to_all | solution.py:1068
  83.5 0.9 shard_map.485
  84.4 3.8 %all-to-all-start.3 = ((bf16[16,112,128]{2,1,0:T(8,128)(2,1)}), bf16[16,112,128]{2,1,0:T(8,128)(2,1)S(1)}, u32[]{:S(2)}, u32[]{:S(2)}) async-start(bf16[16,112,128]{2,1,0:T(8,128)(2,1)} %bitcast.12), calls=%async_computation.3 | async-start | bytes 917504 | tf_op jit(solution)/shard_map/all_to_all | solution.py:1311
  88.2 4.9 %shard_map.487 = (f32[384,384]{1,0:T(8,128)}, f32[384,384]{1,0:T(8,128)}, f32[384,2,384]{2,1,0:T(2,128)}, f32[384,2,384]{2,1,0:T(2,128)}, f32[384,384]{1,0:T(8,1...) custom-call(bf16[2304,128]{1,0:T(8,128)(2,1)S(1)} %bitcast.29, f32[384,384]{1,0:T(8,128)} %refs_2_.7, ...), custom_call_target="tpu_custom_call" | custom-call | flops 5000000000 | bytes 1048576 | tf_op jit(solution)/shard_map/pallas_call | solution.py:1168
  93.1 0.1 collective-permute-start.5
  93.2 1.4 %collective-permute-done.5.refs_1_ = f32[16,128]{1,0:T(8,128)S(1)} collective-permute-done((f32[16,128]{1,0:T(8,128)}, f32[16,128]{1,0:T(8,128)S(1)}, u32[]{:S(2)}, u32[]{:S(2)}) %collective-permute-start.5) | collective-permute-done | bytes 8224 | tf_op jit(solution)/shard_map/ppermute | solution.py:1203
  94.5 2.8 %shard_map.488 = (f32[384,384]{1,0:T(8,128)}, bf16[384,384]{1,0:T(8,128)(2,1)}) custom-call(f32[16,128]{1,0:T(8,128)} %get-tuple-element.169.refs_0_.refs_1_, f32[16,128]{1,0:T(8,128)S(1)} %collective-permute-done.5.refs_1_, f32[384,384]{1,0:T(8,128)} %refs_2_.7, f32[384,384]{1,0:T(8,128)} %get-tuple-element.170.refs_3_), custom_call_target="tpu_custom_call" | custom-call | flops 2000000000 | bytes 1048576 | tf_op jit(solution)/shard_map/pallas_call | solution.py:1168
  97.3 3.6 %all-to-all-done.3 = bf16[16,112,128]{2,1,0:T(8,128)(2,1)S(1)} async-done(((bf16[16,112,128]{2,1,0:T(8,128)(2,1)}), bf16[16,112,128]{2,1,0:T(8,128)(2,1)S(1)}, u32[]{:S(2)}, u32[]{:S(2)}) %all-to-all-start.3) | async-done | bytes 458784 | tf_op jit(solution)/shard_map/all_to_all | solution.py:1311
  100.9 3.3 %shard_map.489 = (f32[384,384]{1,0:T(8,128)S(1)}, f32[384,384]{1,0:T(8,128)S(1)}, f32[2,56,384]{2,1,0:T(8,128)}, f32[2,56,384]{2,1,0:T(8,128)}, f32[2,24,384]{2,...) custom-call(bf16[1792,128]{1,0:T(8,128)(2,1)S(1)} %bitcast.30, ...), custom_call_target="tpu_custom_call" | custom-call | flops 5000000000 | bytes 1048576 | tf_op jit(solution)/shard_map/pallas_call | solution.py:1168
  104.1 0.1 collective-permute-start.6
  104.2 0.2 shard_map.490.refs_3_
  104.4 1.0 collective-permute-done.6.refs_1_
  105.4 2.7 %shard_map.491 = (f32[384,2,384]{2,1,0:T(2,128)}, bf16[384,2,384]{2,1,0:T(2,128)(2,1)}, f32[2,56,384]{2,1,0:T(8,128)}, bf16[2,56,384]{2,1,0:T(8,128)(2,1)}, f32[...) custom-call(f32[16,128]{1,0:T(8,128)S(1)} %get-tuple-element.176.ref, ...), custom_call_target="tpu_custom_call", output_to_operand_aliasing={{16}: (22, {}), {17}: (23, {})} | custom-call | flops 5000000000 | bytes 1048576 | tf_op jit(solution)/shard_map/pallas_call | solution.py:1168
  (2 shorter events, 0.0 us)
Async XLA Ops:
  4.4 2.1 %collective-permute-start = (f32[112,384]{1,0:T(8,128)S(1)}, f32[112,384]{1,0:T(8,128)S(1)}, u32[]{:S(2)}, u32[]{:S(2)}) collective-permute-start(f32[112,384]{1,0:T(8,128)S(1)} %get-tuple-element.128.refs_0_), channel_id=1, source_target_pairs={{0,1},{1,0},{2,3},{3,2},{4,5},{5,4},{6,7},{7,6},{8,9},{9,8},{10,11... | collective-permute-start | bytes 516104 | tf_op jit(solution)/shard_map/ppermute | solution.py:1203
  4.9 1.6 %collective-permute-start.1 = (bf16[192,384]{1,0:T(8,128)(2,1)}, bf16[192,384]{1,0:T(8,128)(2,1)S(1)}, u32[]{:S(2)}, u32[]{:S(2)}) collective-permute-start(bf16[192,384]{1,0:T(8,128)(2,1)} %bitcast.2.refs_9_.refs_1_), channel_id=1, source_target_pairs={{0,1},{1,0},{2,3},{3,2},{4,5},{5,4},{6,7},{7,6},{8,9},{9,8},{10,11... | collective-permute-start | bytes 442376 | tf_op jit(solution)/shard_map/ppermute | solution.py:1203
  17.7 24.7 %all-to-all-start = ((bf16[16,144,128]{2,1,0:T(8,128)(2,1)}), bf16[16,144,128]{2,1,0:T(8,128)(2,1)S(1)}, u32[]{:S(2)}, u32[]{:S(2)}) async-start(bf16[16,144,128]{2,1,0:T(8,128)(2,1)} %bitcast.4), calls=%async_computation | async-start | bytes 1179648 | tf_op jit(solution)/shard_map/all_to_all | solution.py:1068
  43.4 22.9 %all-to-all-start.1 = ((bf16[16,144,128]{2,1,0:T(8,128)(2,1)}), bf16[16,144,128]{2,1,0:T(8,128)(2,1)S(1)}, u32[]{:S(2)}, u32[]{:S(2)}) async-start(bf16[16,144,128]{2,1,0:T(8,128)(2,1)} %bitcast.6), calls=%async_computation.1 | async-start | bytes 1179648 | tf_op jit(solution)/shard_map/all_to_all | solution.py:1263
  50.1 1.5 %collective-permute-start.2 = (f32[112,384]{1,0:T(8,128)S(1)}, f32[112,384]{1,0:T(8,128)S(1)}, u32[]{:S(2)}, u32[]{:S(2)}) collective-permute-start(f32[112,384]{1,0:T(8,128)S(1)} %get-tuple-element.148.refs_0_), channel_id=1, source_target_pairs={{0,1},{1,0},{2,3},{3,2},{4,5},{5,4},{6,7},{7,6},{8,9},{9,8},{10,11... | collective-permute-start | bytes 516104 | tf_op jit(solution)/shard_map/ppermute | solution.py:1203
  51.6 19.4 %copy-start = (f32[192]{0:T(256)S(1)}, f32[192]{0:T(256)}, u32[]{:S(2)}) copy-start(f32[192]{0:T(256)} %param.41) | copy-start | bytes 2308
  51.6 19.4 %copy-start.1 = (f32[192]{0:T(256)S(1)}, f32[192]{0:T(256)}, u32[]{:S(2)}) copy-start(f32[192]{0:T(256)} %param.34) | copy-start | bytes 2308
  66.3 17.2 %all-to-all-start.2 = ((bf16[16,112,128]{2,1,0:T(8,128)(2,1)}), bf16[16,112,128]{2,1,0:T(8,128)(2,1)S(1)}, u32[]{:S(2)}, u32[]{:S(2)}) async-start(bf16[16,112,128]{2,1,0:T(8,128)(2,1)} %bitcast.8), calls=%async_computation.2 | async-start | bytes 917504 | tf_op jit(solution)/shard_map/all_to_all | solution.py:1068
  70.4 2.2 %collective-permute-start.4 = (f32[200,384]{1,0:T(8,128)S(1)}, f32[200,384]{1,0:T(8,128)S(1)}, u32[]{:S(2)}, u32[]{:S(2)}) collective-permute-start(f32[200,384]{1,0:T(8,128)S(1)} %get-tuple-element.162), channel_id=1, source_target_pairs={{0,1},{1,0},{2,3},{3,2},{4,5},{5,4},{6,7},{7,6},{8,9},{9,8},{10,11... | collective-permute-start | bytes 921608 | tf_op jit(solution)/shard_map/ppermute | solution.py:1203
  70.5 2.1 %collective-permute-start.3 = (f32[192,384]{1,0:T(8,128)S(1)}, f32[192,384]{1,0:T(8,128)S(1)}, u32[]{:S(2)}, u32[]{:S(2)}) collective-permute-start(f32[192,384]{1,0:T(8,128)S(1)} %get-tuple-element.160), channel_id=1, source_target_pairs={{0,1},{1,0},{2,3},{3,2},{4,5},{5,4},{6,7},{7,6},{8,9},{9,8},{10,11... | collective-permute-start | bytes 884744 | tf_op jit(solution)/shard_map/ppermute | solution.py:1203
  71.0 1.5 %collective-permute-start.7 = (f32[2,192]{1,0:T(2,128)S(1)}, f32[2,192]{1,0:T(2,128)S(1)}, u32[]{:S(2)}, u32[]{:S(2)}) collective-permute-start(f32[2,192]{1,0:T(2,128)S(1)} %pad_maximum_fusion), channel_id=1, source_target_pairs={{0,1},{1,0},{2,3},{3,2},{4,5},{5,4},{6,7},{7,6},{8,9},{9,8},{10,11... | collective-permute-start | bytes 4616 | tf_op jit(solution)/shard_map/ppermute | solution.py:1203
  84.4 16.5 %all-to-all-start.3 = ((bf16[16,112,128]{2,1,0:T(8,128)(2,1)}), bf16[16,112,128]{2,1,0:T(8,128)(2,1)S(1)}, u32[]{:S(2)}, u32[]{:S(2)}) async-start(bf16[16,112,128]{2,1,0:T(8,128)(2,1)} %bitcast.12), calls=%async_computation.3 | async-start | bytes 917504 | tf_op jit(solution)/shard_map/all_to_all | solution.py:1311
  93.1 1.4 %collective-permute-start.5 = (f32[16,128]{1,0:T(8,128)}, f32[16,128]{1,0:T(8,128)S(1)}, u32[]{:S(2)}, u32[]{:S(2)}) collective-permute-start(f32[16,128]{1,0:T(8,128)} %get-tuple-element.169.refs_0_.refs_1_), channel_id=1, source_target_pairs={{0,1},{1,0},{2,3},{3,2},{4,5},{5,4},{6,7},{7,6},{8,9},{9,8},{10,11... | collective-permute-start | bytes 24584 | tf_op jit(solution)/shard_map/ppermute | solution.py:1203
  104.1 1.2 %collective-permute-start.6 = (f32[16,128]{1,0:T(8,128)S(1)}, f32[16,128]{1,0:T(8,128)S(1)}, u32[]{:S(2)}, u32[]{:S(2)}) collective-permute-start(f32[16,128]{1,0:T(8,128)S(1)} %get-tuple-element.176.refs_0_), channel_id=1, source_target_pairs={{0,1},{1,0},{2,3},{3,2},{4,5},{5,4},{6,7},{7,6},{8,9},{9,8},{10,11... | collective-permute-start | bytes 24584 | tf_op jit(solution)/shard_map/ppermute | solution.py:1203
